TPU v7x, 32 devices: a whole 2x2x4 slice. The times are simulated.
32 devices in a mesh: prompt: 2 (over x), sample: 8 (over z, y), width: 2 (over core).
Axes of the slice: x: 2, y: 2, z: 4, core: 2. Of those that a mesh axis runs over, the one named last changes fastest.
Arguments:
- embeddings: bfloat16 [32, 128, 1024], P(('prompt', 'sample'), None, 'width'), parts along dimension 0, may hold values from -24 to 24
- lengths: int32 [32], P(('prompt', 'sample')), parts along dimension 0, may hold values from 8 to 128, as said below
Outputs:
- fscore: float32 [32, 16], P(('prompt', 'sample', 'width')), parts along dimension 0
- utility: float32 [32], P(('prompt', 'sample', 'width')), parts along dimension 0
There are 2 independent parts, one for each index of `prompt`. A program takes and returns all parts, laid end to end along the dimension named above; each array names one. Nothing has to cross between parts.
Inputs may be any that keep to these rules, and one draw needn't show every extreme that they name: `lengths`: some hypothesis has exactly 128 tokens and some exactly 8.
All inputs are finite; a program needn't handle non-finite values.
Results may differ from a plain program's by a relative error of at most 0.0003.
Values may be sent and summed in bfloat16 or wider, within the bound.
No kernel may reach another device: no remote copies, remote signals or barrier semaphores. Data moves between devices by JAX's collectives and lax.ppermute only.
A program may use at most 64 MiB of HBM per device.

v0:
```python
import math

import jax
import jax.numpy as jnp
from jax import lax
from jax.sharding import PartitionSpec as P


def from_behind(block, axis, distance):
    devices = range(lax.axis_size(axis))
    route = [((i - distance) % len(devices), i) for i in devices]
    return lax.ppermute(block, axis, route)


def bert_f(similar, query_len, refer_len):
    position = jnp.arange(similar.shape[-1]).astype(jnp.float32)
    query_mask = position[None, :] < query_len[:, None]
    refer_mask = position[None, :] < refer_len[:, None]
    by_rows = jnp.where(refer_mask[None, :, None, :], similar, -4.0)
    best_query = jnp.max(by_rows, axis=3)
    precis = (
        jnp.sum(jnp.where(query_mask[:, None, :], best_query, 0.0), axis=2) / query_len[:, None]
    )
    by_cols = jnp.where(query_mask[:, None, :, None], similar, -4.0)
    best_refer = jnp.max(by_cols, axis=2)
    recall = (
        jnp.sum(jnp.where(refer_mask[None, :, :], best_refer, 0.0), axis=2) / refer_len[None, :]
    )
    return 2.0 * precis * recall / jnp.maximum(precis + recall, 1.0)


def body(embeddings, lengths):
    block_rows = embeddings.shape[0]
    feature_part = embeddings.shape[2]
    width_count = lax.axis_size("width")
    cycle_count = lax.axis_size("sample")
    full_width = feature_part * width_count
    width_index = lax.axis_index("width")
    cycle_index = lax.axis_index("sample")
    values = embeddings.astype(jnp.float32)
    sumsq = lax.psum(jnp.sum(values * values, axis=-1), "width")
    scale = lax.rsqrt(sumsq / full_width + 1e-06) / math.sqrt(full_width)
    normed = (values * scale[:, :, None]).astype(jnp.bfloat16)
    own_len = lengths.astype(jnp.bfloat16)
    my_rows = block_rows // width_count
    my_len = lax.dynamic_slice_in_dim(lengths, width_index * my_rows, my_rows, 0).astype(
        jnp.float32
    )
    total_rows = block_rows * cycle_count

    def process(scores, piece, piece_len, source):
        similar = lax.psum_scatter(
            jnp.einsum("iae,jbe->ijab", normed, piece, preferred_element_type=jnp.float32),
            "width",
            scatter_dimension=0,
            tiled=True,
        )
        block = bert_f(similar, my_len, piece_len.astype(jnp.float32))
        column = source * block_rows
        return lax.dynamic_update_slice(scores, block, (jnp.int32(0), column))

    scores = jnp.zeros((my_rows, total_rows), jnp.float32)
    scores = process(scores, normed, own_len, cycle_index)

    def turn_one(step_index, carry):
        scores, piece, piece_len = carry
        piece, piece_len = from_behind((piece, piece_len), "sample", 1)
        scores = process(scores, piece, piece_len, (cycle_index - step_index) % cycle_count)
        return (scores, piece, piece_len)

    carried = lax.fori_loop(1, cycle_count, turn_one, (scores, normed, own_len))
    scores = carried[0]
    row_global = (cycle_index * width_count + width_index) * my_rows + jnp.arange(my_rows)
    column_index = jnp.arange(total_rows)
    diagonal = jnp.sum(jnp.where(column_index[None, :] == row_global[:, None], scores, 0.0), axis=1)
    utility = (jnp.sum(scores, axis=1) - diagonal) / (total_rows - 1)
    return (scores, utility)


def solution(mesh):
    in_specs = (P(("prompt", "sample"), None, "width"), P(("prompt", "sample")))
    out_specs = (P(("prompt", "sample", "width"), None), P(("prompt", "sample", "width")))
    return jax.shard_map(body, mesh=mesh, in_specs=in_specs, out_specs=out_specs, check_vma=False)
```

profile of v0, /device:TPU:0, one launch (start us, length us, event | category | flops | bytes accessed | tf_op | source)
XLA Modules:
  0.0 265.1 jit_solution(8730833762044616634)
XLA Ops:
  8.3 2.6 psum.7
  15.3 17.7 %all-reduce.7.cloned.1.call-done = f32[2,2,128,128]{2,3,0,1:T(8,128)} async-done(((f32[2,2,128,128]{2,3,0,1:T(8,128)}), f32[2,2,128,128]{2,3,0,1:T(8,128)}) %all-reduce.7.cloned.1.call-update) | async-done | bytes 262160
  35.1 219.5 %while.19 = (s32[]{:T(128)}, f32[1,16]{1,0:T(1,128)S(1)}, bf16[2,128,512]{2,1,0:T(8,128)(2,1)S(1)}, bf16[2]{0:T(256)(128)(2,1)S(1)}, f32[1]{0:T(128)}, /*index=5...) while((s32[]{:T(128)}, f32[1,16]{1,0:T(1,128)S(1)}, ...), condition=%wide.region_13.14_spmd, body=%wide.region_7.13_spmd.sunk | while | flops 67306896 | bytes 4070352 | solution.py:71
  35.2 1.9 collective-permute-start
  38.5 8.1 %collective-permute-done = bf16[2,128,512]{2,1,0:T(8,128)(2,1)S(1)} collective-permute-done((bf16[2,128,512]{2,1,0:T(8,128)(2,1)S(1)}, bf16[2,128,512]{2,1,0:T(8,128)(2,1)S(1)}, u32[]{:S(2)}, u32[]{:S(2)}) %collective-permute-start) | collective-permute-done | bytes 262176 | tf_op jit(solution)/shard_map/while/body/eval_jaxpr/ppermute | solution.py:12
  48.3 16.1 %all-reduce.9.cloned.1.call-done = f32[2,2,128,128]{2,3,0,1:T(8,128)} async-done(((f32[2,2,128,128]{2,3,0,1:T(8,128)}), f32[2,2,128,128]{2,3,0,1:T(8,128)}) %all-reduce.9.cloned.1.call-update) | async-done | bytes 262160 | tf_op jit(solution)/shard_map/while
  69.8 8.1 %collective-permute-done = bf16[2,128,512]{2,1,0:T(8,128)(2,1)S(1)} collective-permute-done((bf16[2,128,512]{2,1,0:T(8,128)(2,1)S(1)}, bf16[2,128,512]{2,1,0:T(8,128)(2,1)S(1)}, u32[]{:S(2)}, u32[]{:S(2)}) %collective-permute-start) | collective-permute-done | bytes 262176 | tf_op jit(solution)/shard_map/while/body/eval_jaxpr/ppermute | solution.py:12
  79.6 16.1 %all-reduce.9.cloned.1.call-done = f32[2,2,128,128]{2,3,0,1:T(8,128)} async-done(((f32[2,2,128,128]{2,3,0,1:T(8,128)}), f32[2,2,128,128]{2,3,0,1:T(8,128)}) %all-reduce.9.cloned.1.call-update) | async-done | bytes 262160 | tf_op jit(solution)/shard_map/while
  95.7 1.7 select_reduce_fusion.10
  97.9 1.8 collective-permute-start
  101.1 8.1 %collective-permute-done = bf16[2,128,512]{2,1,0:T(8,128)(2,1)S(1)} collective-permute-done((bf16[2,128,512]{2,1,0:T(8,128)(2,1)S(1)}, bf16[2,128,512]{2,1,0:T(8,128)(2,1)S(1)}, u32[]{:S(2)}, u32[]{:S(2)}) %collective-permute-start) | collective-permute-done | bytes 262176 | tf_op jit(solution)/shard_map/while/body/eval_jaxpr/ppermute | solution.py:12
  111.0 16.1 %all-reduce.9.cloned.1.call-done = f32[2,2,128,128]{2,3,0,1:T(8,128)} async-done(((f32[2,2,128,128]{2,3,0,1:T(8,128)}), f32[2,2,128,128]{2,3,0,1:T(8,128)}) %all-reduce.9.cloned.1.call-update) | async-done | bytes 262160 | tf_op jit(solution)/shard_map/while
  129.3 1.8 collective-permute-start
  132.5 8.1 %collective-permute-done = bf16[2,128,512]{2,1,0:T(8,128)(2,1)S(1)} collective-permute-done((bf16[2,128,512]{2,1,0:T(8,128)(2,1)S(1)}, bf16[2,128,512]{2,1,0:T(8,128)(2,1)S(1)}, u32[]{:S(2)}, u32[]{:S(2)}) %collective-permute-start) | collective-permute-done | bytes 262176 | tf_op jit(solution)/shard_map/while/body/eval_jaxpr/ppermute | solution.py:12
  142.3 16.1 %all-reduce.9.cloned.1.call-done = f32[2,2,128,128]{2,3,0,1:T(8,128)} async-done(((f32[2,2,128,128]{2,3,0,1:T(8,128)}), f32[2,2,128,128]{2,3,0,1:T(8,128)}) %all-reduce.9.cloned.1.call-update) | async-done | bytes 262160 | tf_op jit(solution)/shard_map/while
  160.6 1.8 collective-permute-start
  163.9 8.1 %collective-permute-done = bf16[2,128,512]{2,1,0:T(8,128)(2,1)S(1)} collective-permute-done((bf16[2,128,512]{2,1,0:T(8,128)(2,1)S(1)}, bf16[2,128,512]{2,1,0:T(8,128)(2,1)S(1)}, u32[]{:S(2)}, u32[]{:S(2)}) %collective-permute-start) | collective-permute-done | bytes 262176 | tf_op jit(solution)/shard_map/while/body/eval_jaxpr/ppermute | solution.py:12
  173.7 16.1 %all-reduce.9.cloned.1.call-done = f32[2,2,128,128]{2,3,0,1:T(8,128)} async-done(((f32[2,2,128,128]{2,3,0,1:T(8,128)}), f32[2,2,128,128]{2,3,0,1:T(8,128)}) %all-reduce.9.cloned.1.call-update) | async-done | bytes 262160 | tf_op jit(solution)/shard_map/while
  191.9 1.8 collective-permute-start
  195.2 8.1 %collective-permute-done = bf16[2,128,512]{2,1,0:T(8,128)(2,1)S(1)} collective-permute-done((bf16[2,128,512]{2,1,0:T(8,128)(2,1)S(1)}, bf16[2,128,512]{2,1,0:T(8,128)(2,1)S(1)}, u32[]{:S(2)}, u32[]{:S(2)}) %collective-permute-start) | collective-permute-done | bytes 262176 | tf_op jit(solution)/shard_map/while/body/eval_jaxpr/ppermute | solution.py:12
  205.0 16.1 %all-reduce.9.cloned.1.call-done = f32[2,2,128,128]{2,3,0,1:T(8,128)} async-done(((f32[2,2,128,128]{2,3,0,1:T(8,128)}), f32[2,2,128,128]{2,3,0,1:T(8,128)}) %all-reduce.9.cloned.1.call-update) | async-done | bytes 262160 | tf_op jit(solution)/shard_map/while
  223.3 1.8 collective-permute-start
  226.5 8.1 %collective-permute-done = bf16[2,128,512]{2,1,0:T(8,128)(2,1)S(1)} collective-permute-done((bf16[2,128,512]{2,1,0:T(8,128)(2,1)S(1)}, bf16[2,128,512]{2,1,0:T(8,128)(2,1)S(1)}, u32[]{:S(2)}, u32[]{:S(2)}) %collective-permute-start) | collective-permute-done | bytes 262176 | tf_op jit(solution)/shard_map/while/body/eval_jaxpr/ppermute | solution.py:12
  236.3 16.1 %all-reduce.9.cloned.1.call-done = f32[2,2,128,128]{2,3,0,1:T(8,128)} async-done(((f32[2,2,128,128]{2,3,0,1:T(8,128)}), f32[2,2,128,128]{2,3,0,1:T(8,128)}) %all-reduce.9.cloned.1.call-update) | async-done | bytes 262160 | tf_op jit(solution)/shard_map/while
  (139 shorter events, 45.4 us)
Async XLA Ops:
  7.2 3.8 %copy-start = (bf16[2,128,512]{2,1,0:T(8,128)(2,1)S(1)}, bf16[2,128,512]{2,1,0:T(8,128)(2,1)}, u32[]{:S(2)}) copy-start(bf16[2,128,512]{2,1,0:T(8,128)(2,1)} %param.4) | copy-start | bytes 786436
  7.2 25.8 %all-reduce.7.cloned.1.call-start = ((), (), s32[]{:S(2)}) async-start(), calls=%async_computation | async-start | bytes 524288
  14.0 0.7 copy-start.3
  35.1 29.3 %all-reduce.9.cloned.1.call-start = ((), (), s32[]{:S(2)}) async-start(), calls=%async_computation.1 | async-start | bytes 524288 | tf_op jit(solution)/shard_map/while
  35.2 11.4 %collective-permute-start = (bf16[2,128,512]{2,1,0:T(8,128)(2,1)S(1)}, bf16[2,128,512]{2,1,0:T(8,128)(2,1)S(1)}, u32[]{:S(2)}, u32[]{:S(2)}) collective-permute-start(bf16[2,128,512]{2,1,0:T(8,128)(2,1)S(1)} %get-tuple-element.274), channel_id=1, source_target_pairs={{14,0},{0,2},{2,4},{4,6},{6,8},{8,10},{10,12},{12,14},{15,1},{1,3}... | collective-permute-start | bytes 786440 | tf_op jit(solution)/shard_map/while/body/eval_jaxpr/ppermute | solution.py:12
  37.0 11.2 %collective-permute-start.1 = (bf16[2]{0:T(256)(128)(2,1)S(1)}, bf16[2]{0:T(256)(128)(2,1)S(1)}, u32[]{:S(2)}, u32[]{:S(2)}) collective-permute-start(bf16[2]{0:T(256)(128)(2,1)S(1)} %get-tuple-element.275), channel_id=1, source_target_pairs={{14,0},{0,2},{2,4},{4,6},{6,8},{8,10},{10,12},{12,14},{15,1},{1,3}... | collective-permute-start | bytes 20 | tf_op jit(solution)/shard_map/while/body/eval_jaxpr/ppermute | solution.py:12
  66.5 29.2 %all-reduce.9.cloned.1.call-start = ((), (), s32[]{:S(2)}) async-start(), calls=%async_computation.1 | async-start | bytes 524288 | tf_op jit(solution)/shard_map/while
  66.6 11.3 %collective-permute-start = (bf16[2,128,512]{2,1,0:T(8,128)(2,1)S(1)}, bf16[2,128,512]{2,1,0:T(8,128)(2,1)S(1)}, u32[]{:S(2)}, u32[]{:S(2)}) collective-permute-start(bf16[2,128,512]{2,1,0:T(8,128)(2,1)S(1)} %get-tuple-element.274), channel_id=1, source_target_pairs={{14,0},{0,2},{2,4},{4,6},{6,8},{8,10},{10,12},{12,14},{15,1},{1,3}... | collective-permute-start | bytes 786440 | tf_op jit(solution)/shard_map/while/body/eval_jaxpr/ppermute | solution.py:12
  68.3 11.2 %collective-permute-start.1 = (bf16[2]{0:T(256)(128)(2,1)S(1)}, bf16[2]{0:T(256)(128)(2,1)S(1)}, u32[]{:S(2)}, u32[]{:S(2)}) collective-permute-start(bf16[2]{0:T(256)(128)(2,1)S(1)} %get-tuple-element.275), channel_id=1, source_target_pairs={{14,0},{0,2},{2,4},{4,6},{6,8},{8,10},{10,12},{12,14},{15,1},{1,3}... | collective-permute-start | bytes 20 | tf_op jit(solution)/shard_map/while/body/eval_jaxpr/ppermute | solution.py:12
  97.9 29.2 %all-reduce.9.cloned.1.call-start = ((), (), s32[]{:S(2)}) async-start(), calls=%async_computation.1 | async-start | bytes 524288 | tf_op jit(solution)/shard_map/while
  97.9 11.3 %collective-permute-start = (bf16[2,128,512]{2,1,0:T(8,128)(2,1)S(1)}, bf16[2,128,512]{2,1,0:T(8,128)(2,1)S(1)}, u32[]{:S(2)}, u32[]{:S(2)}) collective-permute-start(bf16[2,128,512]{2,1,0:T(8,128)(2,1)S(1)} %get-tuple-element.274), channel_id=1, source_target_pairs={{14,0},{0,2},{2,4},{4,6},{6,8},{8,10},{10,12},{12,14},{15,1},{1,3}... | collective-permute-start | bytes 786440 | tf_op jit(solution)/shard_map/while/body/eval_jaxpr/ppermute | solution.py:12
  99.7 11.2 %collective-permute-start.1 = (bf16[2]{0:T(256)(128)(2,1)S(1)}, bf16[2]{0:T(256)(128)(2,1)S(1)}, u32[]{:S(2)}, u32[]{:S(2)}) collective-permute-start(bf16[2]{0:T(256)(128)(2,1)S(1)} %get-tuple-element.275), channel_id=1, source_target_pairs={{14,0},{0,2},{2,4},{4,6},{6,8},{8,10},{10,12},{12,14},{15,1},{1,3}... | collective-permute-start | bytes 20 | tf_op jit(solution)/shard_map/while/body/eval_jaxpr/ppermute | solution.py:12
  129.2 29.2 %all-reduce.9.cloned.1.call-start = ((), (), s32[]{:S(2)}) async-start(), calls=%async_computation.1 | async-start | bytes 524288 | tf_op jit(solution)/shard_map/while
  129.3 11.3 %collective-permute-start = (bf16[2,128,512]{2,1,0:T(8,128)(2,1)S(1)}, bf16[2,128,512]{2,1,0:T(8,128)(2,1)S(1)}, u32[]{:S(2)}, u32[]{:S(2)}) collective-permute-start(bf16[2,128,512]{2,1,0:T(8,128)(2,1)S(1)} %get-tuple-element.274), channel_id=1, source_target_pairs={{14,0},{0,2},{2,4},{4,6},{6,8},{8,10},{10,12},{12,14},{15,1},{1,3}... | collective-permute-start | bytes 786440 | tf_op jit(solution)/shard_map/while/body/eval_jaxpr/ppermute | solution.py:12
  131.0 11.2 %collective-permute-start.1 = (bf16[2]{0:T(256)(128)(2,1)S(1)}, bf16[2]{0:T(256)(128)(2,1)S(1)}, u32[]{:S(2)}, u32[]{:S(2)}) collective-permute-start(bf16[2]{0:T(256)(128)(2,1)S(1)} %get-tuple-element.275), channel_id=1, source_target_pairs={{14,0},{0,2},{2,4},{4,6},{6,8},{8,10},{10,12},{12,14},{15,1},{1,3}... | collective-permute-start | bytes 20 | tf_op jit(solution)/shard_map/while/body/eval_jaxpr/ppermute | solution.py:12
  160.6 29.2 %all-reduce.9.cloned.1.call-start = ((), (), s32[]{:S(2)}) async-start(), calls=%async_computation.1 | async-start | bytes 524288 | tf_op jit(solution)/shard_map/while
  160.6 11.3 %collective-permute-start = (bf16[2,128,512]{2,1,0:T(8,128)(2,1)S(1)}, bf16[2,128,512]{2,1,0:T(8,128)(2,1)S(1)}, u32[]{:S(2)}, u32[]{:S(2)}) collective-permute-start(bf16[2,128,512]{2,1,0:T(8,128)(2,1)S(1)} %get-tuple-element.274), channel_id=1, source_target_pairs={{14,0},{0,2},{2,4},{4,6},{6,8},{8,10},{10,12},{12,14},{15,1},{1,3}... | collective-permute-start | bytes 786440 | tf_op jit(solution)/shard_map/while/body/eval_jaxpr/ppermute | solution.py:12
  162.4 11.2 %collective-permute-start.1 = (bf16[2]{0:T(256)(128)(2,1)S(1)}, bf16[2]{0:T(256)(128)(2,1)S(1)}, u32[]{:S(2)}, u32[]{:S(2)}) collective-permute-start(bf16[2]{0:T(256)(128)(2,1)S(1)} %get-tuple-element.275), channel_id=1, source_target_pairs={{14,0},{0,2},{2,4},{4,6},{6,8},{8,10},{10,12},{12,14},{15,1},{1,3}... | collective-permute-start | bytes 20 | tf_op jit(solution)/shard_map/while/body/eval_jaxpr/ppermute | solution.py:12
  191.9 29.2 %all-reduce.9.cloned.1.call-start = ((), (), s32[]{:S(2)}) async-start(), calls=%async_computation.1 | async-start | bytes 524288 | tf_op jit(solution)/shard_map/while
  191.9 11.3 %collective-permute-start = (bf16[2,128,512]{2,1,0:T(8,128)(2,1)S(1)}, bf16[2,128,512]{2,1,0:T(8,128)(2,1)S(1)}, u32[]{:S(2)}, u32[]{:S(2)}) collective-permute-start(bf16[2,128,512]{2,1,0:T(8,128)(2,1)S(1)} %get-tuple-element.274), channel_id=1, source_target_pairs={{14,0},{0,2},{2,4},{4,6},{6,8},{8,10},{10,12},{12,14},{15,1},{1,3}... | collective-permute-start | bytes 786440 | tf_op jit(solution)/shard_map/while/body/eval_jaxpr/ppermute | solution.py:12
  193.7 11.2 %collective-permute-start.1 = (bf16[2]{0:T(256)(128)(2,1)S(1)}, bf16[2]{0:T(256)(128)(2,1)S(1)}, u32[]{:S(2)}, u32[]{:S(2)}) collective-permute-start(bf16[2]{0:T(256)(128)(2,1)S(1)} %get-tuple-element.275), channel_id=1, source_target_pairs={{14,0},{0,2},{2,4},{4,6},{6,8},{8,10},{10,12},{12,14},{15,1},{1,3}... | collective-permute-start | bytes 20 | tf_op jit(solution)/shard_map/while/body/eval_jaxpr/ppermute | solution.py:12
  223.2 29.2 %all-reduce.9.cloned.1.call-start = ((), (), s32[]{:S(2)}) async-start(), calls=%async_computation.1 | async-start | bytes 524288 | tf_op jit(solution)/shard_map/while
  223.3 11.3 %collective-permute-start = (bf16[2,128,512]{2,1,0:T(8,128)(2,1)S(1)}, bf16[2,128,512]{2,1,0:T(8,128)(2,1)S(1)}, u32[]{:S(2)}, u32[]{:S(2)}) collective-permute-start(bf16[2,128,512]{2,1,0:T(8,128)(2,1)S(1)} %get-tuple-element.274), channel_id=1, source_target_pairs={{14,0},{0,2},{2,4},{4,6},{6,8},{8,10},{10,12},{12,14},{15,1},{1,3}... | collective-permute-start | bytes 786440 | tf_op jit(solution)/shard_map/while/body/eval_jaxpr/ppermute | solution.py:12
  225.1 11.2 %collective-permute-start.1 = (bf16[2]{0:T(256)(128)(2,1)S(1)}, bf16[2]{0:T(256)(128)(2,1)S(1)}, u32[]{:S(2)}, u32[]{:S(2)}) collective-permute-start(bf16[2]{0:T(256)(128)(2,1)S(1)} %get-tuple-element.275), channel_id=1, source_target_pairs={{14,0},{0,2},{2,4},{4,6},{6,8},{8,10},{10,12},{12,14},{15,1},{1,3}... | collective-permute-start | bytes 20 | tf_op jit(solution)/shard_map/while/body/eval_jaxpr/ppermute | solution.py:12
  (2 other events, 1.2 us)
Sparse Core Ops, SparseCore 0:
  12.2 20.8 all-reduce.6
  47.7 16.6 all-reduce.8
  79.0 16.6 all-reduce.8
  110.4 16.6 all-reduce.8
  141.7 16.6 all-reduce.8
  173.0 16.6 all-reduce.8
  204.4 16.6 all-reduce.8
  235.7 16.6 all-reduce.8
where the time goes:
time: 266 us; the launch traced here: 265 us
  waiting for transfers between devices  187 us (70%)
  starting transfers between devices  23.1 us (9%)
  other arithmetic  17.9 us (7%)
  between operations  17.2 us (6%)
  local copies, waits for them, and re-layouts  9.11 us (3%)
  matrix products  7.7 us (3%)
    while x14, waiting for transfers between devices  113 us
    ppermute x14, waiting for transfers between devices, from_behind(): return lax.ppermute(block, axis, route)  56.5 us
    ppermute x14, starting transfers between devices, from_behind(): return lax.ppermute(block, axis, route)  22.8 us
    unnamed x2, waiting for transfers between devices  17.7 us
    reduce_max x8, other arithmetic, bert_f(): best_query = jnp.max(by_rows, axis=3)  13.7 us
    dot_general x8, matrix products, process(): jnp.einsum('iae,jbe->ijab', normed, piece, preferred_element_type=jnp.flo...  7.7 us
  transfers between devices with their start and end apart: 22, of which 15 were waited for; matrix products, arithmetic and copies ran while one was open for 5% of the time, Pallas kernels for 0%

commit v1 on v0

--- a/solution.py
+++ b/solution.py
@@ -1,9 +1,184 @@
+import functools
 import math
 
 import jax
 import jax.numpy as jnp
 from jax import lax
+from jax.experimental import pallas as pl
+from jax.experimental.pallas import tpu as pltpu
 from jax.sharding import PartitionSpec as P
+
+VMEM = pltpu.VMEM
+SMEM = pltpu.SMEM
+
+
+def normalise(first, second, width):
+    a = first.astype(jnp.float32)
+    b = second.astype(jnp.float32)
+    sumsq = jnp.sum(a * a + b * b, axis=-1, keepdims=True)
+    scale = lax.rsqrt(sumsq / width + 1e-06) / math.sqrt(width)
+    return (a * scale).astype(jnp.bfloat16), (b * scale).astype(jnp.bfloat16)
+
+
+def pair_f(similar, row_len, col_len):
+    slots = similar.shape[0]
+    rows = lax.broadcasted_iota(jnp.int32, (slots, 1), 0).astype(jnp.float32)
+    cols = lax.broadcasted_iota(jnp.int32, (1, slots), 1).astype(jnp.float32)
+    row_real = rows < row_len
+    col_real = cols < col_len
+    by_row = jnp.max(similar + jnp.where(col_real, 0.0, -8.0), axis=1, keepdims=True)
+    by_col = jnp.max(similar + jnp.where(row_real, 0.0, -8.0), axis=0, keepdims=True)
+    prec = jnp.sum(jnp.where(row_real, by_row, 0.0), axis=0, keepdims=True) / row_len
+    recall = jnp.sum(jnp.where(col_real, by_col, 0.0), axis=1, keepdims=True) / col_len
+    return 2.0 * prec * recall / jnp.maximum(prec + recall, 1.0)
+
+
+def dot_nt(a, b):
+    return lax.dot_general(a, b, (((1,), (1,)), ((), ())), preferred_element_type=jnp.float32)
+
+
+def peers(chip, half):
+    turn = jnp.where(chip < half, 2, 3)
+    return chip ^ 1, chip ^ turn, chip ^ (half + 2)
+
+
+def early_kernel(
+    half, len_o, len_y, len_z, len_r, o0, o1, y0, y1, z0, z1, tokens, lens, local, to_z
+):
+    slots, feat = o0.shape[1], o0.shape[2]
+    width = 2 * feat
+    w = lax.axis_index("width")
+    chip = lax.axis_index("sample")
+    y_chip, z_chip, _ = peers(chip, half)
+    for k, (a, b) in enumerate(((o0, o1), (y0, y1), (z0, z1))):
+        for v in range(2):
+            na, nb = normalise(a[v], b[v], width)
+            tokens[2 * k + v, :, :feat] = na
+            tokens[2 * k + v, :, feat:] = nb
+    lanes = lax.broadcasted_iota(jnp.int32, lens.shape, 1)
+    table = jnp.zeros(lens.shape, jnp.float32)
+    for k, ref in enumerate((len_o, len_y, len_z, len_r)):
+        for v in range(2):
+            table = jnp.where(lanes == 2 * k + v, ref[v].astype(jnp.float32), table)
+    lens[...] = table
+    o_len = len_o[w].astype(jnp.float32)
+    z_len = len_z[w].astype(jnp.float32)
+    own = tokens[w]
+    every = tokens[...].reshape(6 * slots, width)
+    sim = dot_nt(own, every)
+    out_lane = lax.broadcasted_iota(jnp.int32, local.shape, 1)
+    row = jnp.zeros(local.shape, jnp.float32)
+    for k, (ref, place) in enumerate(((len_o, chip), (len_y, y_chip), (len_z, z_chip))):
+        for v in range(2):
+            at = (2 * k + v) * slots
+            f = pair_f(sim[:, at : at + slots], o_len, ref[v].astype(jnp.float32))
+            row = jnp.where(out_lane == 2 * place + v, f, row)
+    local[...] = row
+    sim = dot_nt(tokens[4 + w], tokens[2:4].reshape(2 * slots, width))
+    row = jnp.zeros(to_z.shape, jnp.float32)
+    for v in range(2):
+        f = pair_f(sim[:, v * slots : (v + 1) * slots], z_len, len_y[v].astype(jnp.float32))
+        row = jnp.where(out_lane == 2 * y_chip + v, f, row)
+    to_z[...] = row
+
+
+def late_kernel(half, tokens, lens, local_in, to_z_in, r0, r1, local, to_z, to_r, normed):
+    slots, feat = r0.shape[1], r0.shape[2]
+    width = 2 * feat
+    w = lax.axis_index("width")
+    chip = lax.axis_index("sample")
+    y_chip, z_chip, r_chip = peers(chip, half)
+    for v in range(2):
+        na, nb = normalise(r0[v], r1[v], width)
+        normed[v, :, :feat] = na
+        normed[v, :, feat:] = nb
+    table = lens[...]
+    length = [table[:, k : k + 1] for k in range(8)]
+
+    def of_core(k):
+        return jnp.where(w == 0, length[k], length[k + 1])
+
+    out_lane = lax.broadcasted_iota(jnp.int32, local.shape, 1)
+    both = normed[...].reshape(2 * slots, width)
+    for source, row_len, base, out in (
+        (w, of_core(0), local_in, local),
+        (4 + w, of_core(4), to_z_in, to_z),
+    ):
+        sim = dot_nt(tokens[source], both)
+        row = base[...]
+        for v in range(2):
+            f = pair_f(sim[:, v * slots : (v + 1) * slots], row_len, length[6 + v])
+            row = jnp.where(out_lane == 2 * r_chip + v, f, row)
+        out[...] = row
+    sim = dot_nt(normed[w], tokens[2:6].reshape(4 * slots, width))
+    row = jnp.zeros(to_r.shape, jnp.float32)
+    for k, place in enumerate((y_chip, z_chip)):
+        for v in range(2):
+            at = (2 * k + v) * slots
+            f = pair_f(sim[:, at : at + slots], of_core(6), length[2 + 2 * k + v])
+            row = jnp.where(out_lane == 2 * place + v, f, row)
+    to_r[...] = row
+
+
+def cross_body(embeddings, lengths):
+    count = lax.axis_size("sample")
+    half = count // 2
+    _, slots, feat = embeddings.shape
+    hyps = 2 * count
+    swap = [(0, 1), (1, 0)]
+    y_route = [(i, i ^ 1) for i in range(count)]
+    z_route = [(i, i ^ (2 if i < half else 3)) for i in range(count)]
+    r_route = [(i, i ^ (half + 2)) for i in range(count)]
+
+    def send(x, route):
+        return lax.ppermute(x, "sample", route)
+
+    def other(x):
+        return lax.ppermute(x, "width", swap)
+
+    r = send(embeddings, r_route)
+    z = send(embeddings, z_route)
+    y = send(embeddings, y_route)
+    len_r = send(lengths, r_route)
+    len_z = send(lengths, z_route)
+    len_y = send(lengths, y_route)
+    row = jax.ShapeDtypeStruct((1, hyps), jnp.float32)
+    limit = pltpu.CompilerParams(vmem_limit_bytes=16 * 1024 * 1024)
+    tokens, lens, local, to_z = pl.pallas_call(
+        functools.partial(early_kernel, half),
+        out_shape=(
+            jax.ShapeDtypeStruct((6, slots, 2 * feat), jnp.bfloat16),
+            jax.ShapeDtypeStruct((1, slots), jnp.float32),
+            row,
+            row,
+        ),
+        in_specs=[pl.BlockSpec(memory_space=SMEM)] * 4 + [pl.BlockSpec(memory_space=VMEM)] * 6,
+        out_specs=[pl.BlockSpec(memory_space=VMEM)] * 4,
+        compiler_params=limit,
+        cost_estimate=pl.CostEstimate(
+            flops=2 * 8 * slots * slots * 2 * feat, bytes_accessed=4 << 20, transcendentals=0
+        ),
+    )(lengths, len_y, len_z, len_r, *halves(embeddings, other), *halves(y, other), *halves(z, other))
+    local, to_z, to_r = pl.pallas_call(
+        functools.partial(late_kernel, half),
+        out_shape=(row, row, row),
+        in_specs=[pl.BlockSpec(memory_space=VMEM)] * 6,
+        out_specs=[pl.BlockSpec(memory_space=VMEM)] * 3,
+        scratch_shapes=[pltpu.VMEM((2, slots, 2 * feat), jnp.bfloat16)],
+        compiler_params=limit,
+        cost_estimate=pl.CostEstimate(
+            flops=2 * 8 * slots * slots * 2 * feat, bytes_accessed=2 << 20, transcendentals=0
+        ),
+    )(tokens, lens, local, to_z, *halves(r, other))
+    scores = local + send(to_z, z_route) + send(to_r, r_route)
+    own = 2 * lax.axis_index("sample") + lax.axis_index("width")
+    rest = jnp.where(jnp.arange(hyps)[None, :] == own, 0.0, scores)
+    return scores, jnp.sum(rest, axis=1) / (hyps - 1)
+
+
+def halves(x, other):
+    back = other(x)
+    return x, back
 
 
 def from_behind(block, axis, distance):
@@ -29,7 +204,7 @@
     return 2.0 * precis * recall / jnp.maximum(precis + recall, 1.0)
 
 
-def body(embeddings, lengths):
+def ring_body(embeddings, lengths):
     block_rows = embeddings.shape[0]
     feature_part = embeddings.shape[2]
     width_count = lax.axis_size("width")
@@ -80,4 +255,5 @@
 def solution(mesh):
     in_specs = (P(("prompt", "sample"), None, "width"), P(("prompt", "sample")))
     out_specs = (P(("prompt", "sample", "width"), None), P(("prompt", "sample", "width")))
+    body = cross_body if mesh.shape["sample"] == 8 and mesh.shape["width"] == 2 else ring_body
     return jax.shard_map(body, mesh=mesh, in_specs=in_specs, out_specs=out_specs, check_vma=False)

time: 266 us -> 45.6 us (0.17)
  waiting for transfers between devices: 187 us -> 20.7 us
  other arithmetic: 17.9 us -> 1.11 us
  between operations: 17.2 us -> 2.45 us
  matrix products: 7.7 us -> 0 us
  local copies, waits for them, and re-layouts: 9.11 us -> 1.6 us
  starting transfers between devices: 23.1 us -> 16.3 us
  Pallas kernels: 0 us -> 3.3 us
    while x14 -> x0, waiting for transfers between devices: 113 us -> none
    ppermute x14 -> x12, waiting for transfers between devices: 56.5 us -> 20.7 us  [the longest x8 20.7 us: send(): return lax.ppermute(x, 'sample', route)]
    unnamed x2 -> x0, waiting for transfers between devices: 17.7 us -> none
    reduce_max x8 -> x0, other arithmetic: 13.7 us -> none  [bert_f(): best_query = jnp.max(by_rows, axis=3)]
    dot_general x8 -> x0, matrix products: 7.7 us -> none  [process(): jnp.einsum('iae,jbe->ijab', normed, piece, preferred_element_type=jnp.flo...]
    ppermute x14 -> x12, starting transfers between devices: 22.8 us -> 16.3 us  [the longest x8 16.3 us: send(): return lax.ppermute(x, 'sample', route)]
    while x21 -> x0, local copies, waits for them, and re-layouts: 4.24 us -> none
    pallas_call x0 -> x2, Pallas kernels: none -> 3.3 us  [the longest x1 2.08 us: cross_body(): pl.pallas_call(functools.partial(early_kernel, half), out_shape=(jax.Shap...]
  transfers between devices with their start and end apart: 22 -> 12, of which waited for: 15 -> 7; matrix products, arithmetic and copies ran while one was open for 5% -> 0% of each run, Pallas kernels for 0% -> 5%
where the time goes in v1:
time: 45.6 us; the launch traced here: 45.5 us
  waiting for transfers between devices  20.7 us (45%)
  starting transfers between devices  16.3 us (36%)
  Pallas kernels  3.3 us (7%)
  between operations  2.45 us (5%)
  local copies, waits for them, and re-layouts  1.6 us (4%)
  other arithmetic  1.11 us (2%)
    ppermute x8, waiting for transfers between devices, send(): return lax.ppermute(x, 'sample', route)  20.7 us
    ppermute x8, starting transfers between devices, send(): return lax.ppermute(x, 'sample', route)  16.3 us
    pallas_call x1, Pallas kernels, cross_body(): pl.pallas_call(functools.partial(early_kernel, half), out_shape=(jax.Shap...  2.08 us
    unnamed x4, local copies, waits for them, and re-layouts  1.6 us
    pallas_call x1, Pallas kernels, cross_body(): pl.pallas_call(functools.partial(late_kernel, half), out_shape=(row, row,...  1.22 us
    reduce_sum x1, other arithmetic, cross_body(): return (scores, jnp.sum(rest, axis=1) / (hyps - 1))  1.11 us
  transfers between devices with their start and end apart: 12, of which 7 were waited for; matrix products, arithmetic and copies ran while one was open for 0% of the time, Pallas kernels for 5%

profile of v1, /device:TPU:0, one launch (start us, length us, event | category | flops | bytes accessed | tf_op | source)
XLA Modules:
  0.0 45.5 jit_solution(2552850806588966676)
XLA Ops:
  0.6 3.0 %collective-permute-start.4 = (bf16[2,128,512]{2,1,0:T(8,128)(2,1)}, bf16[2,128,512]{2,1,0:T(8,128)(2,1)S(1)}, u32[]{:S(2)}, u32[]{:S(2)}) collective-permute-start(bf16[2,128,512]{2,1,0:T(8,128)(2,1)} %o0.1), channel_id=1, source_target_pairs={{0,2},{2,0},{4,6},{6,4},{8,10},{10,8},{12,14},{14,12},{1,3},{3,1},... | collective-permute-start | bytes 786440 | tf_op jit(solution)/shard_map/ppermute | solution.py:134
  3.7 1.6 %collective-permute-start.6 = (bf16[2,128,512]{2,1,0:T(8,128)(2,1)}, bf16[2,128,512]{2,1,0:T(8,128)(2,1)S(1)}, u32[]{:S(2)}, u32[]{:S(2)}) collective-permute-start(bf16[2,128,512]{2,1,0:T(8,128)(2,1)} %o0.1), channel_id=1, source_target_pairs={{0,4},{2,6},{4,0},{6,2},{8,14},{10,12},{12,10},{14,8},{1,5},{3,7},... | collective-permute-start | bytes 786440 | tf_op jit(solution)/shard_map/ppermute | solution.py:134
  5.2 2.4 %collective-permute-start.8 = (bf16[2,128,512]{2,1,0:T(8,128)(2,1)}, bf16[2,128,512]{2,1,0:T(8,128)(2,1)S(1)}, u32[]{:S(2)}, u32[]{:S(2)}) collective-permute-start(bf16[2,128,512]{2,1,0:T(8,128)(2,1)} %o0.1), channel_id=1, source_target_pairs={{0,12},{2,14},{4,8},{6,10},{8,4},{10,6},{12,0},{14,2},{1,13},{3,15... | collective-permute-start | bytes 786440 | tf_op jit(solution)/shard_map/ppermute | solution.py:134
  7.7 0.0 collective-permute-start.3
  7.7 2.5 %collective-permute-done.4.y0 = bf16[2,128,512]{2,1,0:T(8,128)(2,1)S(1)} collective-permute-done((bf16[2,128,512]{2,1,0:T(8,128)(2,1)}, bf16[2,128,512]{2,1,0:T(8,128)(2,1)S(1)}, u32[]{:S(2)}, u32[]{:S(2)}) %collective-permute-start.4) | collective-permute-done | bytes 262176 | tf_op jit(solution)/shard_map/ppermute | solution.py:134
  10.2 0.0 collective-permute-start.5
  10.2 2.1 %collective-permute-done.6.z0 = bf16[2,128,512]{2,1,0:T(8,128)(2,1)S(1)} collective-permute-done((bf16[2,128,512]{2,1,0:T(8,128)(2,1)}, bf16[2,128,512]{2,1,0:T(8,128)(2,1)S(1)}, u32[]{:S(2)}, u32[]{:S(2)}) %collective-permute-start.6) | collective-permute-done | bytes 262176 | tf_op jit(solution)/shard_map/ppermute | solution.py:134
  12.3 0.0 collective-permute-start.7
  12.3 7.1 %collective-permute-done.8.r0 = bf16[2,128,512]{2,1,0:T(8,128)(2,1)S(1)} collective-permute-done((bf16[2,128,512]{2,1,0:T(8,128)(2,1)}, bf16[2,128,512]{2,1,0:T(8,128)(2,1)S(1)}, u32[]{:S(2)}, u32[]{:S(2)}) %collective-permute-start.8) | collective-permute-done | bytes 262176 | tf_op jit(solution)/shard_map/ppermute | solution.py:134
  19.4 0.0 collective-permute-start.9
  19.4 1.5 %collective-permute-start = (s32[2]{0:T(128)}, s32[2]{0:T(128)S(1)}, u32[]{:S(2)}, u32[]{:S(2)}) collective-permute-start(s32[2]{0:T(128)} %len_o.1), channel_id=1, source_target_pairs={{0,2},{2,0},{4,6},{6,4},{8,10},{10,8},{12,14},{14,12},{1,3},{3,1},... | collective-permute-start | bytes 32 | tf_op jit(solution)/shard_map/ppermute | solution.py:134
  20.9 2.2 %collective-permute-done.len_y = s32[2]{0:T(128)S(1)} collective-permute-done((s32[2]{0:T(128)}, s32[2]{0:T(128)S(1)}, u32[]{:S(2)}, u32[]{:S(2)}) %collective-permute-start) | collective-permute-done | bytes 40 | tf_op jit(solution)/shard_map/ppermute | solution.py:134
  23.1 0.1 collective-permute-start.1
  23.1 3.6 %collective-permute-done.1.len_z = s32[2]{0:T(128)S(1)} collective-permute-done((s32[2]{0:T(128)}, s32[2]{0:T(128)S(1)}, u32[]{:S(2)}, u32[]{:S(2)}) %collective-permute-start.1) | collective-permute-done | bytes 40 | tf_op jit(solution)/shard_map/ppermute | solution.py:134
  26.7 3.8 %collective-permute-start.2 = (s32[2]{0:T(128)}, s32[2]{0:T(128)S(1)}, u32[]{:S(2)}, u32[]{:S(2)}) collective-permute-start(s32[2]{0:T(128)} %len_o.1), channel_id=1, source_target_pairs={{0,12},{2,14},{4,8},{6,10},{8,4},{10,6},{12,0},{14,2},{1,13},{3,15... | collective-permute-start | bytes 32 | tf_op jit(solution)/shard_map/ppermute | solution.py:134
  30.6 1.7 %collective-permute-done.2.len_r = s32[2]{0:T(128)S(1)} collective-permute-done((s32[2]{0:T(128)}, s32[2]{0:T(128)S(1)}, u32[]{:S(2)}, u32[]{:S(2)}) %collective-permute-start.2) | collective-permute-done | bytes 40 | tf_op jit(solution)/shard_map/ppermute | solution.py:134
  32.2 0.9 %copy-done = bf16[2,128,512]{2,1,0:T(8,128)(2,1)S(1)} copy-done((bf16[2,128,512]{2,1,0:T(8,128)(2,1)S(1)}, bf16[2,128,512]{2,1,0:T(8,128)(2,1)}, u32[]{:S(2)}) %copy-start) | copy-done | bytes 262168
  33.2 0.7 %copy-done.1 = s32[2]{0:T(128)S(1)} copy-done((s32[2]{0:T(128)S(1)}, s32[2]{0:T(128)}, u32[]{:S(2)}) %copy-start.1) | copy-done | bytes 32
  33.8 2.1 %shard_map.41 = (bf16[6,128,1024]{2,1,0:T(8,128)(2,1)S(1)}, f32[1,128]{1,0:T(1,128)S(1)}, f32[1,16]{1,0:T(1,128)S(1)}, f32[1,16]{1,0:T(1,128)S(1)}) custom-call(s32[2]{0:T(128)S(1)} %copy-done.1, s32[2]{0:T(128)S(1)} %collective-permute-done.len_y, s32[2]{0:T(128)S(1)} %collective-permute-done.1.len_z, s32[2]{0:T(128)S(1)} %collective-permute-done.2.len_r, ...), custom_call_target="tpu_custom_call" | custom-call | flops 268435456 | bytes 4194304 | tf_op jit(solution)/shard_map/pallas_call | solution.py:147
  35.9 1.2 %shard_map.42 = (f32[1,16]{1,0:T(1,128)S(1)}, f32[1,16]{1,0:T(1,128)S(1)}, f32[1,16]{1,0:T(1,128)S(1)}) custom-call(bf16[6,128,1024]{2,1,0:T(8,128)(2,1)S(1)} %get-tuple-element.9.tokens, f32[1,128]{1,0:T(1,128)S(1)} %get-tuple-element.10.lens, f32[1,16]{1,0:T(1,128)S(1)} %get-tuple-element.11.local_in, f32[1,16]{1,0:T(1,128)S(1)} %get-tuple-element.12.to_z_in, ...), custom_call_target="tpu_custom_call" | custom-call | flops 268435456 | bytes 2097152 | tf_op jit(solution)/shard_map/pallas_call | solution.py:162
  37.2 0.0 collective-permute-start.10
  37.2 3.9 %collective-permute-start.11 = (f32[1,16]{1,0:T(1,128)S(1)}, f32[1,16]{1,0:T(1,128)S(1)}, u32[]{:S(2)}, u32[]{:S(2)}) collective-permute-start(f32[1,16]{1,0:T(1,128)S(1)} %get-tuple-element.15), channel_id=1, source_target_pairs={{0,12},{2,14},{4,8},{6,10},{8,4},{10,6},{12,0},{14,2},{1,13},{3,15... | collective-permute-start | bytes 200 | tf_op jit(solution)/shard_map/ppermute | solution.py:134
  41.1 1.5 %collective-permute-done.11 = f32[1,16]{1,0:T(1,128)S(1)} collective-permute-done((f32[1,16]{1,0:T(1,128)S(1)}, f32[1,16]{1,0:T(1,128)S(1)}, u32[]{:S(2)}, u32[]{:S(2)}) %collective-permute-start.11) | collective-permute-done | bytes 96 | tf_op jit(solution)/shard_map/ppermute | solution.py:134
  42.6 1.1 %fusion = (f32[]{:T(128)}, f32[1,16]{1,0:T(1,128)}) fusion(s32[]{:T(128)S(6)} %add.11, f32[1,16]{1,0:T(1,128)S(1)} %collective-permute-done.11, f32[1,16]{1,0:T(1,128)S(1)} %get-tuple-element.13, f32[1,16]{1,0:T(1,128)S(1)} %collective-permute-done.10), kind=kLoop, calls=%fused_computation.1 | loop fusion | flops 79 | bytes 264 | tf_op jit(solution)/shard_map/reduce_sum | solution.py:176
  (7 shorter events, 0.0 us)
Async XLA Ops:
  0.6 9.5 %collective-permute-start.4 = (bf16[2,128,512]{2,1,0:T(8,128)(2,1)}, bf16[2,128,512]{2,1,0:T(8,128)(2,1)S(1)}, u32[]{:S(2)}, u32[]{:S(2)}) collective-permute-start(bf16[2,128,512]{2,1,0:T(8,128)(2,1)} %o0.1), channel_id=1, source_target_pairs={{0,2},{2,0},{4,6},{6,4},{8,10},{10,8},{12,14},{14,12},{1,3},{3,1},... | collective-permute-start | bytes 786440 | tf_op jit(solution)/shard_map/ppermute | solution.py:134
  3.7 8.6 %collective-permute-start.6 = (bf16[2,128,512]{2,1,0:T(8,128)(2,1)}, bf16[2,128,512]{2,1,0:T(8,128)(2,1)S(1)}, u32[]{:S(2)}, u32[]{:S(2)}) collective-permute-start(bf16[2,128,512]{2,1,0:T(8,128)(2,1)} %o0.1), channel_id=1, source_target_pairs={{0,4},{2,6},{4,0},{6,2},{8,14},{10,12},{12,10},{14,8},{1,5},{3,7},... | collective-permute-start | bytes 786440 | tf_op jit(solution)/shard_map/ppermute | solution.py:134
  5.2 14.1 %collective-permute-start.8 = (bf16[2,128,512]{2,1,0:T(8,128)(2,1)}, bf16[2,128,512]{2,1,0:T(8,128)(2,1)S(1)}, u32[]{:S(2)}, u32[]{:S(2)}) collective-permute-start(bf16[2,128,512]{2,1,0:T(8,128)(2,1)} %o0.1), channel_id=1, source_target_pairs={{0,12},{2,14},{4,8},{6,10},{8,4},{10,6},{12,0},{14,2},{1,13},{3,15... | collective-permute-start | bytes 786440 | tf_op jit(solution)/shard_map/ppermute | solution.py:134
  7.7 24.6 %collective-permute-start.3 = (bf16[2,128,512]{2,1,0:T(8,128)(2,1)}, bf16[2,128,512]{2,1,0:T(8,128)(2,1)S(1)}, u32[]{:S(2)}, u32[]{:S(2)}) collective-permute-start(bf16[2,128,512]{2,1,0:T(8,128)(2,1)} %o0.1), channel_id=1, source_target_pairs={{0,1},{1,0},{2,3},{3,2},{4,5},{5,4},{6,7},{7,6},{8,9},{9,8},{10,11... | collective-permute-start | bytes 786440 | tf_op jit(solution)/shard_map/ppermute | solution.py:137
  10.2 22.0 %collective-permute-start.5 = (bf16[2,128,512]{2,1,0:T(8,128)(2,1)S(1)}, bf16[2,128,512]{2,1,0:T(8,128)(2,1)S(1)}, u32[]{:S(2)}, u32[]{:S(2)}) collective-permute-start(bf16[2,128,512]{2,1,0:T(8,128)(2,1)S(1)} %collective-permute-done.4.y0), channel_id=1, source_target_pairs={{0,1},{1,0},{2,3},{3,2},{4,5},{5,4},{6,7},{7,6},{8,9},{9,8},{10,11... | collective-permute-start | bytes 786440 | tf_op jit(solution)/shard_map/ppermute | solution.py:137
  12.3 19.9 %collective-permute-start.7 = (bf16[2,128,512]{2,1,0:T(8,128)(2,1)S(1)}, bf16[2,128,512]{2,1,0:T(8,128)(2,1)S(1)}, u32[]{:S(2)}, u32[]{:S(2)}) collective-permute-start(bf16[2,128,512]{2,1,0:T(8,128)(2,1)S(1)} %collective-permute-done.6.z0), channel_id=1, source_target_pairs={{0,1},{1,0},{2,3},{3,2},{4,5},{5,4},{6,7},{7,6},{8,9},{9,8},{10,11... | collective-permute-start | bytes 786440 | tf_op jit(solution)/shard_map/ppermute | solution.py:137
  19.4 16.6 %collective-permute-start.9 = (bf16[2,128,512]{2,1,0:T(8,128)(2,1)S(1)}, bf16[2,128,512]{2,1,0:T(8,128)(2,1)S(1)}, u32[]{:S(2)}, u32[]{:S(2)}) collective-permute-start(bf16[2,128,512]{2,1,0:T(8,128)(2,1)S(1)} %collective-permute-done.8.r0), channel_id=1, source_target_pairs={{0,1},{1,0},{2,3},{3,2},{4,5},{5,4},{6,7},{7,6},{8,9},{9,8},{10,11... | collective-permute-start | bytes 786440 | tf_op jit(solution)/shard_map/ppermute | solution.py:137
  19.4 3.7 %collective-permute-start = (s32[2]{0:T(128)}, s32[2]{0:T(128)S(1)}, u32[]{:S(2)}, u32[]{:S(2)}) collective-permute-start(s32[2]{0:T(128)} %len_o.1), channel_id=1, source_target_pairs={{0,2},{2,0},{4,6},{6,4},{8,10},{10,8},{12,14},{14,12},{1,3},{3,1},... | collective-permute-start | bytes 32 | tf_op jit(solution)/shard_map/ppermute | solution.py:134
  23.1 3.7 %collective-permute-start.1 = (s32[2]{0:T(128)}, s32[2]{0:T(128)S(1)}, u32[]{:S(2)}, u32[]{:S(2)}) collective-permute-start(s32[2]{0:T(128)} %len_o.1), channel_id=1, source_target_pairs={{0,4},{2,6},{4,0},{6,2},{8,14},{10,12},{12,10},{14,8},{1,5},{3,7},... | collective-permute-start | bytes 32 | tf_op jit(solution)/shard_map/ppermute | solution.py:134
  26.7 5.5 %collective-permute-start.2 = (s32[2]{0:T(128)}, s32[2]{0:T(128)S(1)}, u32[]{:S(2)}, u32[]{:S(2)}) collective-permute-start(s32[2]{0:T(128)} %len_o.1), channel_id=1, source_target_pairs={{0,12},{2,14},{4,8},{6,10},{8,4},{10,6},{12,0},{14,2},{1,13},{3,15... | collective-permute-start | bytes 32 | tf_op jit(solution)/shard_map/ppermute | solution.py:134
  32.2 1.0 %copy-start = (bf16[2,128,512]{2,1,0:T(8,128)(2,1)S(1)}, bf16[2,128,512]{2,1,0:T(8,128)(2,1)}, u32[]{:S(2)}) copy-start(bf16[2,128,512]{2,1,0:T(8,128)(2,1)} %o0.1) | copy-start | bytes 786436
  33.2 0.7 %copy-start.1 = (s32[2]{0:T(128)S(1)}, s32[2]{0:T(128)}, u32[]{:S(2)}) copy-start(s32[2]{0:T(128)} %len_o.1) | copy-start | bytes 28
  37.2 3.9 %collective-permute-start.10 = (f32[1,16]{1,0:T(1,128)S(1)}, f32[1,16]{1,0:T(1,128)S(1)}, u32[]{:S(2)}, u32[]{:S(2)}) collective-permute-start(f32[1,16]{1,0:T(1,128)S(1)} %get-tuple-element.14), channel_id=1, source_target_pairs={{0,4},{2,6},{4,0},{6,2},{8,14},{10,12},{12,10},{14,8},{1,5},{3,7},... | collective-permute-start | bytes 200 | tf_op jit(solution)/shard_map/ppermute | solution.py:134
  37.2 5.4 %collective-permute-start.11 = (f32[1,16]{1,0:T(1,128)S(1)}, f32[1,16]{1,0:T(1,128)S(1)}, u32[]{:S(2)}, u32[]{:S(2)}) collective-permute-start(f32[1,16]{1,0:T(1,128)S(1)} %get-tuple-element.15), channel_id=1, source_target_pairs={{0,12},{2,14},{4,8},{6,10},{8,4},{10,6},{12,0},{14,2},{1,13},{3,15... | collective-permute-start | bytes 200 | tf_op jit(solution)/shard_map/ppermute | solution.py:134

commit v2 on v0

--- a/solution.py
+++ b/solution.py
@@ -1,9 +1,215 @@
+import functools
 import math
 
 import jax
 import jax.numpy as jnp
 from jax import lax
+from jax.experimental import pallas as pl
+from jax.experimental.pallas import tpu as pltpu
 from jax.sharding import PartitionSpec as P
+
+VMEM = pltpu.VMEM
+SMEM = pltpu.SMEM
+
+
+def normalise(first, second, width):
+    a = first.astype(jnp.float32)
+    b = second.astype(jnp.float32)
+    sumsq = jnp.sum(a * a + b * b, axis=-1, keepdims=True)
+    scale = lax.rsqrt(sumsq / width + 1e-06) / math.sqrt(width)
+    return (a * scale).astype(jnp.bfloat16), (b * scale).astype(jnp.bfloat16)
+
+
+def pair_f(similar, row_len, col_len):
+    slots = similar.shape[0]
+    rows = lax.broadcasted_iota(jnp.int32, (slots, 1), 0).astype(jnp.float32)
+    cols = lax.broadcasted_iota(jnp.int32, (1, slots), 1).astype(jnp.float32)
+    row_real = rows < row_len
+    col_real = cols < col_len
+    by_row = jnp.max(similar + jnp.where(col_real, 0.0, -8.0), axis=1, keepdims=True)
+    by_col = jnp.max(similar + jnp.where(row_real, 0.0, -8.0), axis=0, keepdims=True)
+    prec = jnp.sum(jnp.where(row_real, by_row, 0.0), axis=0, keepdims=True) / row_len
+    recall = jnp.sum(jnp.where(col_real, by_col, 0.0), axis=1, keepdims=True) / col_len
+    return 2.0 * prec * recall / jnp.maximum(prec + recall, 1.0)
+
+
+def dot_nt(a, b):
+    return lax.dot_general(a, b, (((1,), (1,)), ((), ())), preferred_element_type=jnp.float32)
+
+
+def peers(chip, half):
+    turn = jnp.where(chip < half, 2, 3)
+    return chip ^ 1, chip ^ turn, chip ^ (half + 2)
+
+
+def pack_kernel(lengths, block, packed, scalars, sems):
+    rows = packed.shape[0] - 16
+    body = pltpu.make_async_copy(block, packed.at[:rows], sems.at[0])
+    body.start()
+    tail = pltpu.make_async_copy(lengths, scalars, sems.at[1])
+    tail.start()
+    tail.wait()
+    row = lax.broadcasted_iota(jnp.int32, (16, 1), 0)
+    value = jnp.where(row == 0, scalars[0], scalars[1]).astype(jnp.float32)
+    packed[rows:] = jnp.broadcast_to(value, (16, packed.shape[1])).astype(packed.dtype)
+    body.wait()
+
+
+def near_kernel(len_r, o0, o1, y0, y1, z0, z1, tokens):
+    slots, feat = (o0.shape[0] - 16) // 2, o0.shape[1]
+    tails = []
+    for k, (a, b) in enumerate(((o0, o1), (y0, y1), (z0, z1))):
+        for v in range(2):
+            at = slice(v * slots, (v + 1) * slots)
+            na, nb = normalise(a[at], b[at], 2 * feat)
+            to = slice((2 * k + v) * slots, (2 * k + v + 1) * slots)
+            tokens[to, :feat] = na
+            tokens[to, feat:] = nb
+        tails.append(a[2 * slots :, :128].astype(jnp.float32))
+    row = lax.broadcasted_iota(jnp.int32, (16, 128), 0)
+    table = jnp.where(row == 6, len_r[0], len_r[1]).astype(jnp.float32)
+    for k, tail in enumerate(tails):
+        for v in range(2):
+            table = jnp.where(row == 2 * k + v, tail[v : v + 1], table)
+    tokens[6 * slots :, :128] = table.astype(tokens.dtype)
+
+
+def lengths_of(tokens):
+    table = tokens[tokens.shape[0] - 16 :, :128].astype(jnp.float32)
+    w = lax.axis_index("width")
+    every = [table[k : k + 1, :1] for k in range(8)]
+    return every, [jnp.where(w == 0, every[k], every[k + 1]) for k in range(0, 8, 2)]
+
+
+def early_kernel(half, tokens, local, to_z):
+    slots = (tokens.shape[0] - 16) // 6
+    w = lax.axis_index("width")
+    chip = lax.axis_index("sample")
+    y_chip, z_chip, _ = peers(chip, half)
+    length, mine = lengths_of(tokens)
+    out_lane = lax.broadcasted_iota(jnp.int32, local.shape, 1)
+    row = jnp.zeros(local.shape, jnp.float32)
+    sim = dot_nt(tokens[pl.ds(w * slots, slots)], tokens[: 6 * slots])
+    for k, place in enumerate((chip, y_chip, z_chip)):
+        for v in range(2):
+            at = (2 * k + v) * slots
+            f = pair_f(sim[:, at : at + slots], mine[0], length[2 * k + v])
+            row = jnp.where(out_lane == 2 * place + v, f, row)
+    local[...] = row
+    sim = dot_nt(tokens[pl.ds((4 + w) * slots, slots)], tokens[2 * slots : 4 * slots])
+    row = jnp.zeros(to_z.shape, jnp.float32)
+    for v in range(2):
+        f = pair_f(sim[:, v * slots : (v + 1) * slots], mine[2], length[2 + v])
+        row = jnp.where(out_lane == 2 * y_chip + v, f, row)
+    to_z[...] = row
+
+
+def late_kernel(half, tokens, local_in, to_z_in, r0, r1, local, to_z, to_r, normed):
+    slots, feat = r0.shape[1], r0.shape[2]
+    width = 2 * feat
+    w = lax.axis_index("width")
+    chip = lax.axis_index("sample")
+    y_chip, z_chip, r_chip = peers(chip, half)
+    for v in range(2):
+        na, nb = normalise(r0[v], r1[v], width)
+        normed[v * slots : (v + 1) * slots, :feat] = na
+        normed[v * slots : (v + 1) * slots, feat:] = nb
+    length, mine = lengths_of(tokens)
+    out_lane = lax.broadcasted_iota(jnp.int32, local.shape, 1)
+    for k, base, out in ((0, local_in, local), (2, to_z_in, to_z)):
+        sim = dot_nt(tokens[pl.ds((2 * k + w) * slots, slots)], normed[...])
+        row = base[...]
+        for v in range(2):
+            f = pair_f(sim[:, v * slots : (v + 1) * slots], mine[k], length[6 + v])
+            row = jnp.where(out_lane == 2 * r_chip + v, f, row)
+        out[...] = row
+    sim = dot_nt(normed[pl.ds(w * slots, slots)], tokens[2 * slots : 6 * slots])
+    row = jnp.zeros(to_r.shape, jnp.float32)
+    for k, place in enumerate((y_chip, z_chip)):
+        for v in range(2):
+            at = (2 * k + v) * slots
+            f = pair_f(sim[:, at : at + slots], mine[3], length[2 + 2 * k + v])
+            row = jnp.where(out_lane == 2 * place + v, f, row)
+    to_r[...] = row
+
+
+def final_kernel(local, from_z, from_r, scores, utility):
+    hyps = local.shape[1]
+    own = 2 * lax.axis_index("sample") + lax.axis_index("width")
+    row = local[...] + from_z[...] + from_r[...]
+    scores[...] = row
+    lane = lax.broadcasted_iota(jnp.int32, row.shape, 1)
+    rest = jnp.where(lane == own, 0.0, row)
+    utility[...] = jnp.sum(rest, axis=1, keepdims=True) / (hyps - 1)
+
+
+def cross_body(embeddings, lengths):
+    count = lax.axis_size("sample")
+    half = count // 2
+    _, slots, feat = embeddings.shape
+    hyps = 2 * count
+    swap = [(0, 1), (1, 0)]
+    y_route = [(i, i ^ 1) for i in range(count)]
+    z_route = [(i, i ^ (2 if i < half else 3)) for i in range(count)]
+    r_route = [(i, i ^ (half + 2)) for i in range(count)]
+
+    def send(x, route):
+        return lax.ppermute(x, "sample", route)
+
+    def other(x):
+        return lax.ppermute(x, "width", swap)
+
+    row = jax.ShapeDtypeStruct((1, hyps), jnp.float32)
+    limit = pltpu.CompilerParams(vmem_limit_bytes=16 * 1024 * 1024)
+
+    def call(kernel, arrays, outs, scratch=(), places=None):
+        places = places or [VMEM] * len(arrays)
+        return pl.pallas_call(
+            kernel,
+            out_shape=outs,
+            in_specs=[pl.BlockSpec(memory_space=place) for place in places],
+            out_specs=[pl.BlockSpec(memory_space=VMEM)] * len(outs),
+            scratch_shapes=scratch,
+            compiler_params=limit,
+        )(*arrays)
+
+    def near():
+        (packed,) = call(
+            pack_kernel,
+            (lengths, embeddings.reshape(2 * slots, feat)),
+            (jax.ShapeDtypeStruct((2 * slots + 16, feat), jnp.bfloat16),),
+            [pltpu.SMEM((2,), jnp.int32), pltpu.SemaphoreType.DMA((2,))],
+            [pl.ANY] * 2,
+        )
+        len_r = send(lengths, r_route)
+        y = send(packed, y_route)
+        z = send(packed, z_route)
+        y, z, len_r = lax.optimization_barrier((y, z, len_r))
+        (tokens,) = call(
+            near_kernel,
+            (len_r, packed, other(packed), y, other(y), z, other(z)),
+            (jax.ShapeDtypeStruct((6 * slots + 16, 2 * feat), jnp.bfloat16),),
+            places=[SMEM] + [VMEM] * 6,
+        )
+        return tokens
+
+    def nothing():
+        return jnp.zeros((6 * slots + 16, 2 * feat), jnp.bfloat16)
+
+    r = send(embeddings, r_route)
+    tokens = lax.cond(lengths[0] > 0, near, nothing)
+    r, tokens = lax.optimization_barrier((r, tokens))
+    local, to_z = call(functools.partial(early_kernel, half), (tokens,), (row, row))
+    local, to_z, to_r = call(
+        functools.partial(late_kernel, half),
+        (tokens, local, to_z, r, other(r)),
+        (row, row, row),
+        [pltpu.VMEM((2 * slots, 2 * feat), jnp.bfloat16)],
+    )
+    one = jax.ShapeDtypeStruct((1, 1), jnp.float32)
+    from_z, from_r = send(to_z, z_route), send(to_r, r_route)
+    scores, utility = call(final_kernel, (local, from_z, from_r), (row, one))
+    return scores, utility.reshape(1)
 
 
 def from_behind(block, axis, distance):
@@ -29,7 +235,7 @@
     return 2.0 * precis * recall / jnp.maximum(precis + recall, 1.0)
 
 
-def body(embeddings, lengths):
+def ring_body(embeddings, lengths):
     block_rows = embeddings.shape[0]
     feature_part = embeddings.shape[2]
     width_count = lax.axis_size("width")
@@ -80,4 +286,5 @@
 def solution(mesh):
     in_specs = (P(("prompt", "sample"), None, "width"), P(("prompt", "sample")))
     out_specs = (P(("prompt", "sample", "width"), None), P(("prompt", "sample", "width")))
+    body = cross_body if mesh.shape["sample"] == 8 and mesh.shape["width"] == 2 else ring_body
     return jax.shard_map(body, mesh=mesh, in_specs=in_specs, out_specs=out_specs, check_vma=False)

time: 266 us -> 32 us (0.12)
  waiting for transfers between devices: 187 us -> 12.4 us
  other arithmetic: 17.9 us -> 0 us
  between operations: 17.2 us -> 1.3 us
  starting transfers between devices: 23.1 us -> 13.3 us
  local copies, waits for them, and re-layouts: 9.11 us -> 0 us
  matrix products: 7.7 us -> 0 us
  Pallas kernels: 0 us -> 4.8 us
    while x14 -> x0, waiting for transfers between devices: 113 us -> none
    ppermute x14 -> x10, waiting for transfers between devices: 56.5 us -> 12.4 us  [the longest x6 10.5 us: send(): return lax.ppermute(x, 'sample', route)]
    unnamed x2 -> x0, waiting for transfers between devices: 17.7 us -> none
    reduce_max x8 -> x0, other arithmetic: 13.7 us -> none  [bert_f(): best_query = jnp.max(by_rows, axis=3)]
    ppermute x14 -> x10, starting transfers between devices: 22.8 us -> 13.3 us  [the longest x6 12.6 us: send(): return lax.ppermute(x, 'sample', route)]
    dot_general x8 -> x0, matrix products: 7.7 us -> none  [process(): jnp.einsum('iae,jbe->ijab', normed, piece, preferred_element_type=jnp.flo...]
    pallas_call x0 -> x5, Pallas kernels: none -> 4.8 us  [call(): pl.pallas_call(kernel, out_shape=outs, in_specs=[pl.BlockSpec(memory_spac...]
    while x21 -> x0, local copies, waits for them, and re-layouts: 4.24 us -> none
  transfers between devices with their start and end apart: 22 -> 10, of which waited for: 15 -> 5; matrix products, arithmetic and copies ran while one was open for 5% -> 0% of each run, Pallas kernels for 0% -> 10%
where the time goes in v2:
time: 32 us; the launch traced here: 31.8 us
  starting transfers between devices  13.3 us (42%)
  waiting for transfers between devices  12.4 us (39%)
  Pallas kernels  4.8 us (15%)
  between operations  1.3 us (4%)
    ppermute x6, starting transfers between devices, send(): return lax.ppermute(x, 'sample', route)  12.6 us
    ppermute x6, waiting for transfers between devices, send(): return lax.ppermute(x, 'sample', route)  10.5 us
    pallas_call x5, Pallas kernels, call(): pl.pallas_call(kernel, out_shape=outs, in_specs=[pl.BlockSpec(memory_spac...  4.8 us
    ppermute x4, waiting for transfers between devices, other(): return lax.ppermute(x, 'width', swap)  1.83 us
    ppermute x4, starting transfers between devices, other(): return lax.ppermute(x, 'width', swap)  0.71 us
  transfers between devices with their start and end apart: 10, of which 5 were waited for; matrix products, arithmetic and copies ran while one was open for 0% of the time, Pallas kernels for 10%

profile of v2, /device:TPU:0, one launch (start us, length us, event | category | flops | bytes accessed | tf_op | source)
XLA Modules:
  0.0 31.8 jit_solution(11009292817234347222)
XLA Ops:
  0.6 5.1 %collective-permute-start.6 = (bf16[2,128,512]{2,1,0:T(8,128)(2,1)}, bf16[2,128,512]{2,1,0:T(8,128)(2,1)S(1)}, u32[]{:S(2)}, u32[]{:S(2)}) collective-permute-start(bf16[2,128,512]{2,1,0:T(8,128)(2,1)} %param.4), channel_id=1, source_target_pairs={{0,12},{2,14},{4,8},{6,10},{8,4},{10,6},{12,0},{14,2},{1,13},{3,15... | collective-permute-start | bytes 786440 | tf_op jit(solution)/shard_map/ppermute | solution.py:157
  6.4 15.0 %conditional.1 = (bf16[784,1024]{1,0:T(8,128)(2,1)S(1)}) conditional(s32[]{:T(128)} %bitcast.1, () %tuple.16, (bf16[2,128,512]{2,1,0:T(8,128)(2,1)}, s32[2]{0:T(128)}) %tuple.17), branch_computations={%region_0.0_spmd, %region_1.0_spmd} | conditional | bytes 5570840 | solution.py:200
  6.4 1.0 %branch_1_fun.2.o0 = bf16[272,512]{1,0:T(8,128)(2,1)S(1)} custom-call(s32[2]{0:T(128)} %get-tuple-element.4.lengths, bf16[256,512]{1,0:T(8,128)(2,1)} %bitcast.4), custom_call_target="tpu_custom_call" | custom-call | tf_op jit(solution)/shard_map/cond/branch_1_fun/pallas_call | solution.py:167
  7.4 1.6 %collective-permute-start = (bf16[272,512]{1,0:T(8,128)(2,1)S(1)}, bf16[272,512]{1,0:T(8,128)(2,1)S(1)}, u32[]{:S(2)}, u32[]{:S(2)}) collective-permute-start(bf16[272,512]{1,0:T(8,128)(2,1)S(1)} %branch_1_fun.2.o0), channel_id=1, source_target_pairs={{0,2},{2,0},{4,6},{6,4},{8,10},{10,8},{12,14},{14,12},{1,3},{3,1},... | collective-permute-start | bytes 835592 | tf_op jit(solution)/shard_map/cond/branch_1_fun/ppermute | solution.py:157
  9.0 0.0 collective-permute-start.1
  9.0 0.8 %collective-permute-start.2 = (s32[2]{0:T(128)}, s32[2]{0:T(128)S(1)}, u32[]{:S(2)}, u32[]{:S(2)}) collective-permute-start(s32[2]{0:T(128)} %get-tuple-element.4.lengths), channel_id=1, source_target_pairs={{0,12},{2,14},{4,8},{6,10},{8,4},{10,6},{12,0},{14,2},{1,13},{3,15... | collective-permute-start | bytes 32 | tf_op jit(solution)/shard_map/cond/branch_1_fun/ppermute | solution.py:157
  9.8 0.0 collective-permute-start.3
  9.8 8.5 %collective-permute-done.2.len_r = s32[2]{0:T(128)S(1)} collective-permute-done((s32[2]{0:T(128)}, s32[2]{0:T(128)S(1)}, u32[]{:S(2)}, u32[]{:S(2)}) %collective-permute-start.2) | collective-permute-done | bytes 40 | tf_op jit(solution)/shard_map/cond/branch_1_fun/ppermute | solution.py:157
  18.3 0.0 collective-permute-done.y0
  18.3 0.0 collective-permute-done.1.z0
  18.3 0.0 collective-permute-start.4
  18.3 0.5 %collective-permute-start.5 = (bf16[272,512]{1,0:T(8,128)(2,1)S(1)}, bf16[272,512]{1,0:T(8,128)(2,1)S(1)}, u32[]{:S(2)}, u32[]{:S(2)}) collective-permute-start(bf16[272,512]{1,0:T(8,128)(2,1)S(1)} %collective-permute-done.1.z0), channel_id=1, source_target_pairs={{0,1},{1,0},{2,3},{3,2},{4,5},{5,4},{6,7},{7,6},{8,9},{9,8},{10,11... | collective-permute-start | bytes 835592 | tf_op jit(solution)/shard_map/cond/branch_1_fun/ppermute | solution.py:160
  18.9 1.0 %collective-permute-done.4.y1 = bf16[272,512]{1,0:T(8,128)(2,1)S(1)} collective-permute-done((bf16[272,512]{1,0:T(8,128)(2,1)S(1)}, bf16[272,512]{1,0:T(8,128)(2,1)S(1)}, u32[]{:S(2)}, u32[]{:S(2)}) %collective-permute-start.4) | collective-permute-done | bytes 278560 | tf_op jit(solution)/shard_map/cond/branch_1_fun/ppermute | solution.py:160
  19.9 0.4 %collective-permute-done.5.z1 = bf16[272,512]{1,0:T(8,128)(2,1)S(1)} collective-permute-done((bf16[272,512]{1,0:T(8,128)(2,1)S(1)}, bf16[272,512]{1,0:T(8,128)(2,1)S(1)}, u32[]{:S(2)}, u32[]{:S(2)}) %collective-permute-start.5) | collective-permute-done | bytes 278560 | tf_op jit(solution)/shard_map/cond/branch_1_fun/ppermute | solution.py:160
  20.3 1.0 %branch_1_fun.3 = bf16[784,1024]{1,0:T(8,128)(2,1)S(1)} custom-call(s32[2]{0:T(128)S(1)} %collective-permute-done.2.len_r, bf16[272,512]{1,0:T(8,128)(2,1)S(1)} %branch_1_fun.2.o0, bf16[272,512]{1,0:T(8,128)(2,1)S(1)} %collective-permute-done.3.o1, bf16[272,512]{1,0:T(8,128)(2,1)S(1)} %collective-permute-done.y0, ...), custom_call_target="tpu_custom_call" | custom-call | tf_op jit(solution)/shard_map/cond/branch_1_fun/pallas_call | solution.py:167
  21.4 0.2 collective-permute-start.7
  21.6 1.0 %shard_map.41 = (f32[1,16]{1,0:T(1,128)S(1)}, f32[1,16]{1,0:T(1,128)S(1)}) custom-call(bf16[784,1024]{1,0:T(8,128)(2,1)S(1)} %get-tuple-element.32.tokens), custom_call_target="tpu_custom_call" | custom-call | tf_op jit(solution)/shard_map/pallas_call | solution.py:167
  22.6 0.4 %collective-permute-done.7.r1 = bf16[2,128,512]{2,1,0:T(8,128)(2,1)S(1)} collective-permute-done((bf16[2,128,512]{2,1,0:T(8,128)(2,1)S(1)}, bf16[2,128,512]{2,1,0:T(8,128)(2,1)S(1)}, u32[]{:S(2)}, u32[]{:S(2)}) %collective-permute-start.7) | collective-permute-done | bytes 262176 | tf_op jit(solution)/shard_map/ppermute | solution.py:160
  23.0 1.2 %shard_map.42 = (f32[1,16]{1,0:T(1,128)S(1)}, f32[1,16]{1,0:T(1,128)S(1)}, f32[1,16]{1,0:T(1,128)S(1)}) custom-call(bf16[784,1024]{1,0:T(8,128)(2,1)S(1)} %get-tuple-element.32.tokens, f32[1,16]{1,0:T(1,128)S(1)} %get-tuple-element.24.local_in, f32[1,16]{1,0:T(1,128)S(1)} %get-tuple-element.25.to_z_in, bf16[2,128,512]{2,1,0:T(8,128)(2,1)S(1)} %collective-permute-done.6.r0, ...), custom_call_target="tpu_custom_call" | custom-call | tf_op jit(solution)/shard_map/pallas_call | solution.py:167
  24.1 1.7 %collective-permute-start.8 = (f32[1,16]{1,0:T(1,128)S(1)}, f32[1,16]{1,0:T(1,128)S(1)}, u32[]{:S(2)}, u32[]{:S(2)}) collective-permute-start(f32[1,16]{1,0:T(1,128)S(1)} %get-tuple-element.28), channel_id=1, source_target_pairs={{0,4},{2,6},{4,0},{6,2},{8,14},{10,12},{12,10},{14,8},{1,5},{3,7},... | collective-permute-start | bytes 200 | tf_op jit(solution)/shard_map/ppermute | solution.py:157
  25.9 3.3 %collective-permute-start.9 = (f32[1,16]{1,0:T(1,128)S(1)}, f32[1,16]{1,0:T(1,128)S(1)}, u32[]{:S(2)}, u32[]{:S(2)}) collective-permute-start(f32[1,16]{1,0:T(1,128)S(1)} %get-tuple-element.29), channel_id=1, source_target_pairs={{0,12},{2,14},{4,8},{6,10},{8,4},{10,6},{12,0},{14,2},{1,13},{3,15... | collective-permute-start | bytes 200 | tf_op jit(solution)/shard_map/ppermute | solution.py:157
  29.2 0.0 collective-permute-done.8.from_z
  29.2 2.0 %collective-permute-done.9.from_r = f32[1,16]{1,0:T(1,128)S(1)} collective-permute-done((f32[1,16]{1,0:T(1,128)S(1)}, f32[1,16]{1,0:T(1,128)S(1)}, u32[]{:S(2)}, u32[]{:S(2)}) %collective-permute-start.9) | collective-permute-done | bytes 96 | tf_op jit(solution)/shard_map/ppermute | solution.py:157
  31.2 0.6 %shard_map.43 = (f32[1,16]{1,0:T(1,128)}, f32[1,1]{1,0:T(1,128)}) custom-call(f32[1,16]{1,0:T(1,128)S(1)} %get-tuple-element.27.local, f32[1,16]{1,0:T(1,128)S(1)} %collective-permute-done.8.from_z, f32[1,16]{1,0:T(1,128)S(1)} %collective-permute-done.9.from_r), custom_call_target="tpu_custom_call" | custom-call | tf_op jit(solution)/shard_map/pallas_call | solution.py:167
  (2 shorter events, 0.0 us)
Async XLA Ops:
  0.6 20.7 %collective-permute-start.6 = (bf16[2,128,512]{2,1,0:T(8,128)(2,1)}, bf16[2,128,512]{2,1,0:T(8,128)(2,1)S(1)}, u32[]{:S(2)}, u32[]{:S(2)}) collective-permute-start(bf16[2,128,512]{2,1,0:T(8,128)(2,1)} %param.4), channel_id=1, source_target_pairs={{0,12},{2,14},{4,8},{6,10},{8,4},{10,6},{12,0},{14,2},{1,13},{3,15... | collective-permute-start | bytes 786440 | tf_op jit(solution)/shard_map/ppermute | solution.py:157
  7.4 10.9 %collective-permute-start = (bf16[272,512]{1,0:T(8,128)(2,1)S(1)}, bf16[272,512]{1,0:T(8,128)(2,1)S(1)}, u32[]{:S(2)}, u32[]{:S(2)}) collective-permute-start(bf16[272,512]{1,0:T(8,128)(2,1)S(1)} %branch_1_fun.2.o0), channel_id=1, source_target_pairs={{0,2},{2,0},{4,6},{6,4},{8,10},{10,8},{12,14},{14,12},{1,3},{3,1},... | collective-permute-start | bytes 835592 | tf_op jit(solution)/shard_map/cond/branch_1_fun/ppermute | solution.py:157
  9.0 9.4 %collective-permute-start.1 = (bf16[272,512]{1,0:T(8,128)(2,1)S(1)}, bf16[272,512]{1,0:T(8,128)(2,1)S(1)}, u32[]{:S(2)}, u32[]{:S(2)}) collective-permute-start(bf16[272,512]{1,0:T(8,128)(2,1)S(1)} %branch_1_fun.2.o0), channel_id=1, source_target_pairs={{0,4},{2,6},{4,0},{6,2},{8,14},{10,12},{12,10},{14,8},{1,5},{3,7},... | collective-permute-start | bytes 835592 | tf_op jit(solution)/shard_map/cond/branch_1_fun/ppermute | solution.py:157
  9.0 9.3 %collective-permute-start.2 = (s32[2]{0:T(128)}, s32[2]{0:T(128)S(1)}, u32[]{:S(2)}, u32[]{:S(2)}) collective-permute-start(s32[2]{0:T(128)} %get-tuple-element.4.lengths), channel_id=1, source_target_pairs={{0,12},{2,14},{4,8},{6,10},{8,4},{10,6},{12,0},{14,2},{1,13},{3,15... | collective-permute-start | bytes 32 | tf_op jit(solution)/shard_map/cond/branch_1_fun/ppermute | solution.py:157
  9.8 9.0 %collective-permute-start.3 = (bf16[272,512]{1,0:T(8,128)(2,1)S(1)}, bf16[272,512]{1,0:T(8,128)(2,1)S(1)}, u32[]{:S(2)}, u32[]{:S(2)}) collective-permute-start(bf16[272,512]{1,0:T(8,128)(2,1)S(1)} %branch_1_fun.2.o0), channel_id=1, source_target_pairs={{0,1},{1,0},{2,3},{3,2},{4,5},{5,4},{6,7},{7,6},{8,9},{9,8},{10,11... | collective-permute-start | bytes 835592 | tf_op jit(solution)/shard_map/cond/branch_1_fun/ppermute | solution.py:160
  18.3 1.6 %collective-permute-start.4 = (bf16[272,512]{1,0:T(8,128)(2,1)S(1)}, bf16[272,512]{1,0:T(8,128)(2,1)S(1)}, u32[]{:S(2)}, u32[]{:S(2)}) collective-permute-start(bf16[272,512]{1,0:T(8,128)(2,1)S(1)} %collective-permute-done.y0), channel_id=1, source_target_pairs={{0,1},{1,0},{2,3},{3,2},{4,5},{5,4},{6,7},{7,6},{8,9},{9,8},{10,11... | collective-permute-start | bytes 835592 | tf_op jit(solution)/shard_map/cond/branch_1_fun/ppermute | solution.py:160
  18.3 2.0 %collective-permute-start.5 = (bf16[272,512]{1,0:T(8,128)(2,1)S(1)}, bf16[272,512]{1,0:T(8,128)(2,1)S(1)}, u32[]{:S(2)}, u32[]{:S(2)}) collective-permute-start(bf16[272,512]{1,0:T(8,128)(2,1)S(1)} %collective-permute-done.1.z0), channel_id=1, source_target_pairs={{0,1},{1,0},{2,3},{3,2},{4,5},{5,4},{6,7},{7,6},{8,9},{9,8},{10,11... | collective-permute-start | bytes 835592 | tf_op jit(solution)/shard_map/cond/branch_1_fun/ppermute | solution.py:160
  21.4 1.6 %collective-permute-start.7 = (bf16[2,128,512]{2,1,0:T(8,128)(2,1)S(1)}, bf16[2,128,512]{2,1,0:T(8,128)(2,1)S(1)}, u32[]{:S(2)}, u32[]{:S(2)}) collective-permute-start(bf16[2,128,512]{2,1,0:T(8,128)(2,1)S(1)} %collective-permute-done.6.r0), channel_id=1, source_target_pairs={{0,1},{1,0},{2,3},{3,2},{4,5},{5,4},{6,7},{7,6},{8,9},{9,8},{10,11... | collective-permute-start | bytes 786440 | tf_op jit(solution)/shard_map/ppermute | solution.py:160
  24.1 5.1 %collective-permute-start.8 = (f32[1,16]{1,0:T(1,128)S(1)}, f32[1,16]{1,0:T(1,128)S(1)}, u32[]{:S(2)}, u32[]{:S(2)}) collective-permute-start(f32[1,16]{1,0:T(1,128)S(1)} %get-tuple-element.28), channel_id=1, source_target_pairs={{0,4},{2,6},{4,0},{6,2},{8,14},{10,12},{12,10},{14,8},{1,5},{3,7},... | collective-permute-start | bytes 200 | tf_op jit(solution)/shard_map/ppermute | solution.py:157
  25.9 5.3 %collective-permute-start.9 = (f32[1,16]{1,0:T(1,128)S(1)}, f32[1,16]{1,0:T(1,128)S(1)}, u32[]{:S(2)}, u32[]{:S(2)}) collective-permute-start(f32[1,16]{1,0:T(1,128)S(1)} %get-tuple-element.29), channel_id=1, source_target_pairs={{0,12},{2,14},{4,8},{6,10},{8,4},{10,6},{12,0},{14,2},{1,13},{3,15... | collective-permute-start | bytes 200 | tf_op jit(solution)/shard_map/ppermute | solution.py:157

commit v3 on v2

--- a/solution.py
+++ b/solution.py
@@ -38,8 +38,7 @@
 
 
 def peers(chip, half):
-    turn = jnp.where(chip < half, 2, 3)
-    return chip ^ 1, chip ^ turn, chip ^ (half + 2)
+    return chip ^ 1, chip ^ 2, chip ^ jnp.where(chip < half, half + 2, half)
 
 
 def pack_kernel(lengths, block, packed, scalars, sems):
@@ -55,88 +54,81 @@
     body.wait()
 
 
-def near_kernel(len_r, o0, o1, y0, y1, z0, z1, tokens):
-    slots, feat = (o0.shape[0] - 16) // 2, o0.shape[1]
-    tails = []
-    for k, (a, b) in enumerate(((o0, o1), (y0, y1), (z0, z1))):
+def unpack(first, second, normed, slots, start=0):
+    feat = first.shape[1]
+    for at in range(0, 2 * slots, slots):
+        a, b = normalise(first[at : at + slots], second[at : at + slots], 2 * feat)
+        normed[start + at : start + at + slots, :feat] = a
+        normed[start + at : start + at + slots, feat:] = b
+
+
+def of_core(pair):
+    return jnp.where(lax.axis_index("width") == 0, *pair)
+
+
+def lengths_of(tokens):
+    rows = tokens[tokens.shape[0] - 16 :, :128].astype(jnp.float32)
+    every = [rows[k : k + 1, :1] for k in range(4)]
+    return every[:2], every[2:]
+
+
+def row_of(base, similar, row_len, blocks):
+    slots = similar.shape[0]
+    lane = lax.broadcasted_iota(jnp.int32, base.shape, 1)
+    for k, (place, length) in enumerate(blocks):
         for v in range(2):
-            at = slice(v * slots, (v + 1) * slots)
-            na, nb = normalise(a[at], b[at], 2 * feat)
-            to = slice((2 * k + v) * slots, (2 * k + v + 1) * slots)
-            tokens[to, :feat] = na
-            tokens[to, feat:] = nb
-        tails.append(a[2 * slots :, :128].astype(jnp.float32))
-    row = lax.broadcasted_iota(jnp.int32, (16, 128), 0)
-    table = jnp.where(row == 6, len_r[0], len_r[1]).astype(jnp.float32)
-    for k, tail in enumerate(tails):
-        for v in range(2):
-            table = jnp.where(row == 2 * k + v, tail[v : v + 1], table)
-    tokens[6 * slots :, :128] = table.astype(tokens.dtype)
-
-
-def lengths_of(tokens):
-    table = tokens[tokens.shape[0] - 16 :, :128].astype(jnp.float32)
-    w = lax.axis_index("width")
-    every = [table[k : k + 1, :1] for k in range(8)]
-    return every, [jnp.where(w == 0, every[k], every[k + 1]) for k in range(0, 8, 2)]
-
-
-def early_kernel(half, tokens, local, to_z):
-    slots = (tokens.shape[0] - 16) // 6
+            at = (2 * k + v) * slots
+            f = pair_f(similar[:, at : at + slots], row_len, length[v])
+            base = jnp.where(lane == 2 * place + v, f, base)
+    return base
+
+
+def near_kernel(half, o0, o1, y0, y1, tokens, local):
+    slots = (o0.shape[0] - 16) // 2
     w = lax.axis_index("width")
     chip = lax.axis_index("sample")
-    y_chip, z_chip, _ = peers(chip, half)
-    length, mine = lengths_of(tokens)
-    out_lane = lax.broadcasted_iota(jnp.int32, local.shape, 1)
-    row = jnp.zeros(local.shape, jnp.float32)
-    sim = dot_nt(tokens[pl.ds(w * slots, slots)], tokens[: 6 * slots])
-    for k, place in enumerate((chip, y_chip, z_chip)):
-        for v in range(2):
-            at = (2 * k + v) * slots
-            f = pair_f(sim[:, at : at + slots], mine[0], length[2 * k + v])
-            row = jnp.where(out_lane == 2 * place + v, f, row)
-    local[...] = row
-    sim = dot_nt(tokens[pl.ds((4 + w) * slots, slots)], tokens[2 * slots : 4 * slots])
-    row = jnp.zeros(to_z.shape, jnp.float32)
+    y_chip, _, _ = peers(chip, half)
+    unpack(o0, o1, tokens, slots)
+    unpack(y0, y1, tokens, slots, 2 * slots)
+    row = lax.broadcasted_iota(jnp.int32, (16, 128), 0)
+    table = jnp.zeros(row.shape, jnp.float32)
     for v in range(2):
-        f = pair_f(sim[:, v * slots : (v + 1) * slots], mine[2], length[2 + v])
-        row = jnp.where(out_lane == 2 * y_chip + v, f, row)
-    to_z[...] = row
-
-
-def late_kernel(half, tokens, local_in, to_z_in, r0, r1, local, to_z, to_r, normed):
-    slots, feat = r0.shape[1], r0.shape[2]
-    width = 2 * feat
+        for k, source in enumerate((o0, y0)):
+            tail = source[2 * slots :, :128].astype(jnp.float32)
+            table = jnp.where(row == 2 * k + v, tail[v : v + 1], table)
+    tokens[4 * slots :, :128] = table.astype(tokens.dtype)
+    len_o, len_y = lengths_of(tokens)
+    similar = dot_nt(tokens[pl.ds(w * slots, slots)], tokens[: 4 * slots])
+    blocks = ((chip, len_o), (y_chip, len_y))
+    local[...] = row_of(jnp.zeros(local.shape, jnp.float32), similar, of_core(len_o), blocks)
+
+
+def far_kernel(half, far_len, other_len, tokens, z0, z1, r0, r1, local, to_y, to_r, normed):
+    slots = z0.shape[0] // 2
     w = lax.axis_index("width")
     chip = lax.axis_index("sample")
     y_chip, z_chip, r_chip = peers(chip, half)
-    for v in range(2):
-        na, nb = normalise(r0[v], r1[v], width)
-        normed[v * slots : (v + 1) * slots, :feat] = na
-        normed[v * slots : (v + 1) * slots, feat:] = nb
-    length, mine = lengths_of(tokens)
-    out_lane = lax.broadcasted_iota(jnp.int32, local.shape, 1)
-    for k, base, out in ((0, local_in, local), (2, to_z_in, to_z)):
-        sim = dot_nt(tokens[pl.ds((2 * k + w) * slots, slots)], normed[...])
-        row = base[...]
-        for v in range(2):
-            f = pair_f(sim[:, v * slots : (v + 1) * slots], mine[k], length[6 + v])
-            row = jnp.where(out_lane == 2 * r_chip + v, f, row)
-        out[...] = row
-    sim = dot_nt(normed[pl.ds(w * slots, slots)], tokens[2 * slots : 6 * slots])
-    row = jnp.zeros(to_r.shape, jnp.float32)
-    for k, place in enumerate((y_chip, z_chip)):
-        for v in range(2):
-            at = (2 * k + v) * slots
-            f = pair_f(sim[:, at : at + slots], mine[3], length[2 + 2 * k + v])
-            row = jnp.where(out_lane == 2 * place + v, f, row)
-    to_r[...] = row
-
-
-def final_kernel(local, from_z, from_r, scores, utility):
+    unpack(z0, z1, normed, slots)
+    unpack(r0, r1, normed, slots, 2 * slots)
+    len_o, len_y = lengths_of(tokens)
+    len_z, len_r = (
+        [jnp.where(w == 0, a[v], b[v]).astype(jnp.float32) for v in range(2)]
+        for a, b in ((far_len, other_len), (other_len, far_len))
+    )
+    empty = jnp.zeros(local.shape, jnp.float32)
+    far = ((z_chip, len_z), (r_chip, len_r))
+    for k, (length, out) in enumerate(((len_o, local), (len_y, to_y))):
+        mine = tokens[pl.ds((2 * k + w) * slots, slots)]
+        out[...] = row_of(empty, dot_nt(mine, normed[...]), of_core(length), far)
+    mine = normed[pl.ds((2 + w) * slots, slots)]
+    near = ((chip, len_o), (y_chip, len_y))
+    to_r[...] = row_of(empty, dot_nt(mine, tokens[: 4 * slots]), of_core(len_r), near)
+
+
+def final_kernel(near, local, from_y, from_r, scores, utility):
     hyps = local.shape[1]
     own = 2 * lax.axis_index("sample") + lax.axis_index("width")
-    row = local[...] + from_z[...] + from_r[...]
+    row = near[...] + local[...] + from_y[...] + from_r[...]
     scores[...] = row
     lane = lax.broadcasted_iota(jnp.int32, row.shape, 1)
     rest = jnp.where(lane == own, 0.0, row)
@@ -150,8 +142,9 @@
     hyps = 2 * count
     swap = [(0, 1), (1, 0)]
     y_route = [(i, i ^ 1) for i in range(count)]
-    z_route = [(i, i ^ (2 if i < half else 3)) for i in range(count)]
-    r_route = [(i, i ^ (half + 2)) for i in range(count)]
+    z_route = [(i, i ^ 2) for i in range(count)]
+    r_route = [(i, i ^ (half if i < half else half + 2)) for i in range(count)]
+    back_route = [(b, a) for a, b in r_route]
 
     def send(x, route):
         return lax.ppermute(x, "sample", route)
@@ -181,34 +174,33 @@
             [pltpu.SMEM((2,), jnp.int32), pltpu.SemaphoreType.DMA((2,))],
             [pl.ANY] * 2,
         )
-        len_r = send(lengths, r_route)
         y = send(packed, y_route)
-        z = send(packed, z_route)
-        y, z, len_r = lax.optimization_barrier((y, z, len_r))
-        (tokens,) = call(
-            near_kernel,
-            (len_r, packed, other(packed), y, other(y), z, other(z)),
-            (jax.ShapeDtypeStruct((6 * slots + 16, 2 * feat), jnp.bfloat16),),
-            places=[SMEM] + [VMEM] * 6,
+        return call(
+            functools.partial(near_kernel, half),
+            (packed, other(packed), y, other(y)),
+            (jax.ShapeDtypeStruct((4 * slots + 16, 2 * feat), jnp.bfloat16), row),
         )
-        return tokens
 
     def nothing():
-        return jnp.zeros((6 * slots + 16, 2 * feat), jnp.bfloat16)
-
-    r = send(embeddings, r_route)
-    tokens = lax.cond(lengths[0] > 0, near, nothing)
-    r, tokens = lax.optimization_barrier((r, tokens))
-    local, to_z = call(functools.partial(early_kernel, half), (tokens,), (row, row))
-    local, to_z, to_r = call(
-        functools.partial(late_kernel, half),
-        (tokens, local, to_z, r, other(r)),
+        return jax.tree.map(lambda x: jnp.zeros(x.shape, x.dtype), jax.eval_shape(near))
+
+    far_route = [(2 * a, 2 * b) for a, b in z_route] + [(2 * a + 1, 2 * b + 1) for a, b in r_route]
+    far_len = lax.ppermute(lengths, ("sample", "width"), far_route)
+    block = embeddings.reshape(2 * slots, feat)
+    z = send(block, z_route)
+    r = send(block, r_route)
+    tokens, near_row = lax.cond(lax.axis_index("sample") >= 0, near, nothing)
+    tokens, z, r, far_len = lax.optimization_barrier((tokens, z, r, far_len))
+    local, to_y, to_r = call(
+        functools.partial(far_kernel, half),
+        (far_len, other(far_len), tokens, z, other(z), r, other(r)),
         (row, row, row),
-        [pltpu.VMEM((2 * slots, 2 * feat), jnp.bfloat16)],
+        [pltpu.VMEM((4 * slots, 2 * feat), jnp.bfloat16)],
+        [SMEM] * 2 + [VMEM] * 5,
     )
     one = jax.ShapeDtypeStruct((1, 1), jnp.float32)
-    from_z, from_r = send(to_z, z_route), send(to_r, r_route)
-    scores, utility = call(final_kernel, (local, from_z, from_r), (row, one))
+    from_y, from_r = send(to_y, y_route), send(to_r, back_route)
+    scores, utility = call(final_kernel, (near_row, local, from_y, from_r), (row, one))
     return scores, utility.reshape(1)
 
 

time: 32 us -> 29.3 us (0.916)
  waiting for transfers between devices: 12.4 us -> 11.2 us
  starting transfers between devices: 13.3 us -> 12.4 us
  between operations: 1.3 us -> 0.65 us
    ppermute x6 -> x5, waiting for transfers between devices: 10.5 us -> 8.25 us  [send(): return lax.ppermute(x, 'sample', route)]
    ppermute x6 -> x5, starting transfers between devices: 12.6 us -> 11.4 us  [send(): return lax.ppermute(x, 'sample', route)]
    ppermute x4 -> x5, waiting for transfers between devices: 1.83 us -> 2.96 us  [other(): return lax.ppermute(x, 'width', swap)]
    ppermute x0 -> x1, starting transfers between devices: none -> 0.45 us  [cross_body(): far_len = lax.ppermute(lengths, ('sample', 'width'), far_route)]
    ppermute x4 -> x5, starting transfers between devices: 0.71 us -> 0.52 us  [other(): return lax.ppermute(x, 'width', swap)]
    pallas_call x5 -> x4, Pallas kernels: 4.8 us -> 4.85 us  [call(): pl.pallas_call(kernel, out_shape=outs, in_specs=[pl.BlockSpec(memory_spac...]
  transfers between devices with their start and end apart: 10 -> 11, of which waited for: 5 -> 6; matrix products, arithmetic and copies ran while one was open for 0% -> 0% of each run, Pallas kernels for 10% -> 7%
where the time goes in v3:
time: 29.3 us; the launch traced here: 29.1 us
  starting transfers between devices  12.4 us (42%)
  waiting for transfers between devices  11.2 us (38%)
  Pallas kernels  4.85 us (17%)
  between operations  0.65 us (2%)
    ppermute x5, starting transfers between devices, send(): return lax.ppermute(x, 'sample', route)  11.4 us
    ppermute x5, waiting for transfers between devices, send(): return lax.ppermute(x, 'sample', route)  8.25 us
    pallas_call x4, Pallas kernels, call(): pl.pallas_call(kernel, out_shape=outs, in_specs=[pl.BlockSpec(memory_spac...  4.85 us
    ppermute x5, waiting for transfers between devices, other(): return lax.ppermute(x, 'width', swap)  2.96 us
  transfers between devices with their start and end apart: 11, of which 6 were waited for; matrix products, arithmetic and copies ran while one was open for 0% of the time, Pallas kernels for 7%

profile of v3, /device:TPU:0, one launch (start us, length us, event | category | flops | bytes accessed | tf_op | source)
XLA Modules:
  0.0 29.1 jit_solution(7292384087375155894)
XLA Ops:
  0.6 3.1 %collective-permute-start.3 = (bf16[256,512]{1,0:T(8,128)(2,1)}, bf16[256,512]{1,0:T(8,128)(2,1)S(1)}, u32[]{:S(2)}, u32[]{:S(2)}) collective-permute-start(bf16[256,512]{1,0:T(8,128)(2,1)} %bitcast.3), channel_id=1, source_target_pairs={{0,4},{2,6},{4,0},{6,2},{8,12},{10,14},{12,8},{14,10},{1,5},{3,7},... | collective-permute-start | bytes 786440 | tf_op jit(solution)/shard_map/ppermute | solution.py:150
  3.7 2.6 %collective-permute-start.4 = (bf16[256,512]{1,0:T(8,128)(2,1)}, bf16[256,512]{1,0:T(8,128)(2,1)S(1)}, u32[]{:S(2)}, u32[]{:S(2)}) collective-permute-start(bf16[256,512]{1,0:T(8,128)(2,1)} %bitcast.4), channel_id=1, source_target_pairs={{0,8},{2,10},{4,12},{6,14},{8,4},{10,6},{12,0},{14,2},{1,9},{3,11}... | collective-permute-start | bytes 786440 | tf_op jit(solution)/shard_map/ppermute | solution.py:150
  6.3 0.4 %collective-permute-start.5 = (s32[2]{0:T(128)}, s32[2]{0:T(128)S(1)}, u32[]{:S(2)}, u32[]{:S(2)}) collective-permute-start(s32[2]{0:T(128)} %param.5), channel_id=1, source_target_pairs={{0,4},{2,6},{4,0},{6,2},{8,12},{10,14},{12,8},{14,10},{1,9},{3,11}... | collective-permute-start | bytes 32 | tf_op jit(solution)/shard_map/ppermute | solution.py:188
  6.8 11.1 %conditional.1 = ((bf16[528,1024]{1,0:T(8,128)(2,1)S(1)}, f32[1,16]{1,0:T(1,128)S(1)})) conditional(s32[]{:T(128)} %convert_element_type.3, () %tuple.16, (bf16[2,128,512]{2,1,0:T(8,128)(2,1)}, s32[2]{0:T(128)}) %tuple.17), branch_computations={%region_0.0_spmd, %region_1.0_spmd} | conditional | bytes 3342464 | solution.py:192
  6.8 1.0 %branch_1_fun.2.o0 = bf16[272,512]{1,0:T(8,128)(2,1)S(1)} custom-call(s32[2]{0:T(128)} %get-tuple-element.4.lengths, bf16[256,512]{1,0:T(8,128)(2,1)} %bitcast.5), custom_call_target="tpu_custom_call" | custom-call | tf_op jit(solution)/shard_map/cond/branch_1_fun/pallas_call | solution.py:160
  7.7 1.6 %collective-permute-start.1 = (bf16[272,512]{1,0:T(8,128)(2,1)S(1)}, bf16[272,512]{1,0:T(8,128)(2,1)S(1)}, u32[]{:S(2)}, u32[]{:S(2)}) collective-permute-start(bf16[272,512]{1,0:T(8,128)(2,1)S(1)} %branch_1_fun.2.o0), channel_id=1, source_target_pairs={{0,2},{2,0},{4,6},{6,4},{8,10},{10,8},{12,14},{14,12},{1,3},{3,1},... | collective-permute-start | bytes 835592 | tf_op jit(solution)/shard_map/cond/branch_1_fun/ppermute | solution.py:150
  9.3 5.9 %collective-permute-done.1.y0 = bf16[272,512]{1,0:T(8,128)(2,1)S(1)} collective-permute-done((bf16[272,512]{1,0:T(8,128)(2,1)S(1)}, bf16[272,512]{1,0:T(8,128)(2,1)S(1)}, u32[]{:S(2)}, u32[]{:S(2)}) %collective-permute-start.1) | collective-permute-done | bytes 278560 | tf_op jit(solution)/shard_map/cond/branch_1_fun/ppermute | solution.py:150
  15.2 0.0 collective-permute-start.2
  15.2 0.0 collective-permute-done.o1
  15.2 1.6 %collective-permute-done.2.y1 = bf16[272,512]{1,0:T(8,128)(2,1)S(1)} collective-permute-done((bf16[272,512]{1,0:T(8,128)(2,1)S(1)}, bf16[272,512]{1,0:T(8,128)(2,1)S(1)}, u32[]{:S(2)}, u32[]{:S(2)}) %collective-permute-start.2) | collective-permute-done | bytes 278560 | tf_op jit(solution)/shard_map/cond/branch_1_fun/ppermute | solution.py:153
  16.8 1.0 %branch_1_fun.3 = (bf16[528,1024]{1,0:T(8,128)(2,1)S(1)}, f32[1,16]{1,0:T(1,128)S(1)}) custom-call(bf16[272,512]{1,0:T(8,128)(2,1)S(1)} %branch_1_fun.2.o0, bf16[272,512]{1,0:T(8,128)(2,1)S(1)} %collective-permute-done.o1, bf16[272,512]{1,0:T(8,128)(2,1)S(1)} %collective-permute-done.1.y0, bf16[272,512]{1,0:T(8,128)(2,1)S(1)} %collective-permute-done.2.y1), custom_call_target="tpu_custom_call" | custom-call | tf_op jit(solution)/shard_map/cond/branch_1_fun/pallas_call | solution.py:160
  17.8 0.0 collective-permute-done.5.far_len
  17.8 0.0 collective-permute-done.3.z0
  17.8 0.3 %collective-permute-done.4.r0 = bf16[256,512]{1,0:T(8,128)(2,1)S(1)} collective-permute-done((bf16[256,512]{1,0:T(8,128)(2,1)}, bf16[256,512]{1,0:T(8,128)(2,1)S(1)}, u32[]{:S(2)}, u32[]{:S(2)}) %collective-permute-start.4) | collective-permute-done | bytes 262176 | tf_op jit(solution)/shard_map/ppermute | solution.py:150
  18.2 0.5 %collective-permute-start.8 = (bf16[256,512]{1,0:T(8,128)(2,1)S(1)}, bf16[256,512]{1,0:T(8,128)(2,1)S(1)}, u32[]{:S(2)}, u32[]{:S(2)}) collective-permute-start(bf16[256,512]{1,0:T(8,128)(2,1)S(1)} %collective-permute-done.4.r0), channel_id=1, source_target_pairs={{0,1},{1,0},{2,3},{3,2},{4,5},{5,4},{6,7},{7,6},{8,9},{9,8},{10,11... | collective-permute-start | bytes 786440 | tf_op jit(solution)/shard_map/ppermute | solution.py:153
  18.7 0.0 collective-permute-start.6
  18.7 1.4 %collective-permute-done.6.other_len = s32[2]{0:T(128)S(1)} collective-permute-done((s32[2]{0:T(128)S(1)}, s32[2]{0:T(128)S(1)}, u32[]{:S(2)}, u32[]{:S(2)}) %collective-permute-start.6) | collective-permute-done | bytes 40 | tf_op jit(solution)/shard_map/ppermute | solution.py:153
  20.1 0.0 collective-permute-done.7.z1
  20.1 2.3 %shard_map.41 = (f32[1,16]{1,0:T(1,128)S(1)}, f32[1,16]{1,0:T(1,128)S(1)}, f32[1,16]{1,0:T(1,128)S(1)}) custom-call(s32[2]{0:T(128)S(1)} %collective-permute-done.5.far_len, s32[2]{0:T(128)S(1)} %collective-permute-done.6.other_len, bf16[528,1024]{1,0:T(8,128)(2,1)S(1)} %get-tuple-element.22.tokens, bf16[256,512]{1,0:T(8,128)(2,1)S(1)} %collective-permute-done.3.z0, ...), custom_call_target="tpu_custom_call" | custom-call | tf_op jit(solution)/shard_map/pallas_call | solution.py:160
  22.3 2.6 %collective-permute-start.10 = (f32[1,16]{1,0:T(1,128)S(1)}, f32[1,16]{1,0:T(1,128)S(1)}, u32[]{:S(2)}, u32[]{:S(2)}) collective-permute-start(f32[1,16]{1,0:T(1,128)S(1)} %get-tuple-element.27), channel_id=1, source_target_pairs={{8,0},{10,2},{12,4},{14,6},{4,8},{6,10},{0,12},{2,14},{9,1},{11,3}... | collective-permute-start | bytes 200 | tf_op jit(solution)/shard_map/ppermute | solution.py:150
  25.0 1.5 %collective-permute-start.9 = (f32[1,16]{1,0:T(1,128)S(1)}, f32[1,16]{1,0:T(1,128)S(1)}, u32[]{:S(2)}, u32[]{:S(2)}) collective-permute-start(f32[1,16]{1,0:T(1,128)S(1)} %get-tuple-element.26), channel_id=1, source_target_pairs={{0,2},{2,0},{4,6},{6,4},{8,10},{10,8},{12,14},{14,12},{1,3},{3,1},... | collective-permute-start | bytes 200 | tf_op jit(solution)/shard_map/ppermute | solution.py:150
  26.5 0.3 collective-permute-done.10.from_r
  26.8 1.7 %collective-permute-done.9.from_y = f32[1,16]{1,0:T(1,128)S(1)} collective-permute-done((f32[1,16]{1,0:T(1,128)S(1)}, f32[1,16]{1,0:T(1,128)S(1)}, u32[]{:S(2)}, u32[]{:S(2)}) %collective-permute-start.9) | collective-permute-done | bytes 96 | tf_op jit(solution)/shard_map/ppermute | solution.py:150
  28.5 0.6 %shard_map.42 = (f32[1,16]{1,0:T(1,128)}, f32[1,1]{1,0:T(1,128)}) custom-call(f32[1,16]{1,0:T(1,128)S(1)} %get-tuple-element.19.near, f32[1,16]{1,0:T(1,128)S(1)} %get-tuple-element.25.local, f32[1,16]{1,0:T(1,128)S(1)} %collective-permute-done.9.from_y, f32[1,16]{1,0:T(1,128)S(1)} %collective-permute-done.10.from_r), custom_call_target="tpu_custom_call" | custom-call | tf_op jit(solution)/shard_map/pallas_call | solution.py:160
  (3 shorter events, 0.0 us)
Async XLA Ops:
  0.6 17.2 %collective-permute-start.3 = (bf16[256,512]{1,0:T(8,128)(2,1)}, bf16[256,512]{1,0:T(8,128)(2,1)S(1)}, u32[]{:S(2)}, u32[]{:S(2)}) collective-permute-start(bf16[256,512]{1,0:T(8,128)(2,1)} %bitcast.3), channel_id=1, source_target_pairs={{0,4},{2,6},{4,0},{6,2},{8,12},{10,14},{12,8},{14,10},{1,5},{3,7},... | collective-permute-start | bytes 786440 | tf_op jit(solution)/shard_map/ppermute | solution.py:150
  3.7 14.4 %collective-permute-start.4 = (bf16[256,512]{1,0:T(8,128)(2,1)}, bf16[256,512]{1,0:T(8,128)(2,1)S(1)}, u32[]{:S(2)}, u32[]{:S(2)}) collective-permute-start(bf16[256,512]{1,0:T(8,128)(2,1)} %bitcast.4), channel_id=1, source_target_pairs={{0,8},{2,10},{4,12},{6,14},{8,4},{10,6},{12,0},{14,2},{1,9},{3,11}... | collective-permute-start | bytes 786440 | tf_op jit(solution)/shard_map/ppermute | solution.py:150
  6.3 11.5 %collective-permute-start.5 = (s32[2]{0:T(128)}, s32[2]{0:T(128)S(1)}, u32[]{:S(2)}, u32[]{:S(2)}) collective-permute-start(s32[2]{0:T(128)} %param.5), channel_id=1, source_target_pairs={{0,4},{2,6},{4,0},{6,2},{8,12},{10,14},{12,8},{14,10},{1,9},{3,11}... | collective-permute-start | bytes 32 | tf_op jit(solution)/shard_map/ppermute | solution.py:188
  7.7 7.5 %collective-permute-start.1 = (bf16[272,512]{1,0:T(8,128)(2,1)S(1)}, bf16[272,512]{1,0:T(8,128)(2,1)S(1)}, u32[]{:S(2)}, u32[]{:S(2)}) collective-permute-start(bf16[272,512]{1,0:T(8,128)(2,1)S(1)} %branch_1_fun.2.o0), channel_id=1, source_target_pairs={{0,2},{2,0},{4,6},{6,4},{8,10},{10,8},{12,14},{14,12},{1,3},{3,1},... | collective-permute-start | bytes 835592 | tf_op jit(solution)/shard_map/cond/branch_1_fun/ppermute | solution.py:150
  9.3 5.9 %collective-permute-start = (bf16[272,512]{1,0:T(8,128)(2,1)S(1)}, bf16[272,512]{1,0:T(8,128)(2,1)S(1)}, u32[]{:S(2)}, u32[]{:S(2)}) collective-permute-start(bf16[272,512]{1,0:T(8,128)(2,1)S(1)} %branch_1_fun.2.o0), channel_id=1, source_target_pairs={{0,1},{1,0},{2,3},{3,2},{4,5},{5,4},{6,7},{7,6},{8,9},{9,8},{10,11... | collective-permute-start | bytes 835592 | tf_op jit(solution)/shard_map/cond/branch_1_fun/ppermute | solution.py:153
  15.2 1.6 %collective-permute-start.2 = (bf16[272,512]{1,0:T(8,128)(2,1)S(1)}, bf16[272,512]{1,0:T(8,128)(2,1)S(1)}, u32[]{:S(2)}, u32[]{:S(2)}) collective-permute-start(bf16[272,512]{1,0:T(8,128)(2,1)S(1)} %collective-permute-done.1.y0), channel_id=1, source_target_pairs={{0,1},{1,0},{2,3},{3,2},{4,5},{5,4},{6,7},{7,6},{8,9},{9,8},{10,11... | collective-permute-start | bytes 835592 | tf_op jit(solution)/shard_map/cond/branch_1_fun/ppermute | solution.py:153
  18.2 1.9 %collective-permute-start.7 = (bf16[256,512]{1,0:T(8,128)(2,1)S(1)}, bf16[256,512]{1,0:T(8,128)(2,1)S(1)}, u32[]{:S(2)}, u32[]{:S(2)}) collective-permute-start(bf16[256,512]{1,0:T(8,128)(2,1)S(1)} %collective-permute-done.3.z0), channel_id=1, source_target_pairs={{0,1},{1,0},{2,3},{3,2},{4,5},{5,4},{6,7},{7,6},{8,9},{9,8},{10,11... | collective-permute-start | bytes 786440 | tf_op jit(solution)/shard_map/ppermute | solution.py:153
  18.2 1.9 %collective-permute-start.8 = (bf16[256,512]{1,0:T(8,128)(2,1)S(1)}, bf16[256,512]{1,0:T(8,128)(2,1)S(1)}, u32[]{:S(2)}, u32[]{:S(2)}) collective-permute-start(bf16[256,512]{1,0:T(8,128)(2,1)S(1)} %collective-permute-done.4.r0), channel_id=1, source_target_pairs={{0,1},{1,0},{2,3},{3,2},{4,5},{5,4},{6,7},{7,6},{8,9},{9,8},{10,11... | collective-permute-start | bytes 786440 | tf_op jit(solution)/shard_map/ppermute | solution.py:153
  18.7 1.4 %collective-permute-start.6 = (s32[2]{0:T(128)S(1)}, s32[2]{0:T(128)S(1)}, u32[]{:S(2)}, u32[]{:S(2)}) collective-permute-start(s32[2]{0:T(128)S(1)} %collective-permute-done.5.far_len), channel_id=1, source_target_pairs={{0,1},{1,0},{2,3},{3,2},{4,5},{5,4},{6,7},{7,6},{8,9},{9,8},{10,11... | collective-permute-start | bytes 32 | tf_op jit(solution)/shard_map/ppermute | solution.py:153
  22.3 4.5 %collective-permute-start.10 = (f32[1,16]{1,0:T(1,128)S(1)}, f32[1,16]{1,0:T(1,128)S(1)}, u32[]{:S(2)}, u32[]{:S(2)}) collective-permute-start(f32[1,16]{1,0:T(1,128)S(1)} %get-tuple-element.27), channel_id=1, source_target_pairs={{8,0},{10,2},{12,4},{14,6},{4,8},{6,10},{0,12},{2,14},{9,1},{11,3}... | collective-permute-start | bytes 200 | tf_op jit(solution)/shard_map/ppermute | solution.py:150
  25.0 3.5 %collective-permute-start.9 = (f32[1,16]{1,0:T(1,128)S(1)}, f32[1,16]{1,0:T(1,128)S(1)}, u32[]{:S(2)}, u32[]{:S(2)}) collective-permute-start(f32[1,16]{1,0:T(1,128)S(1)} %get-tuple-element.26), channel_id=1, source_target_pairs={{0,2},{2,0},{4,6},{6,4},{8,10},{10,8},{12,14},{14,12},{1,3},{3,1},... | collective-permute-start | bytes 200 | tf_op jit(solution)/shard_map/ppermute | solution.py:150

commit v4 on v3

--- a/solution.py
+++ b/solution.py
@@ -54,53 +54,62 @@
     body.wait()
 
 
-def unpack(first, second, normed, slots, start=0):
+def unpack(first, second, normed, slots, places):
     feat = first.shape[1]
-    for at in range(0, 2 * slots, slots):
-        a, b = normalise(first[at : at + slots], second[at : at + slots], 2 * feat)
-        normed[start + at : start + at + slots, :feat] = a
-        normed[start + at : start + at + slots, feat:] = b
-
-
-def of_core(pair):
-    return jnp.where(lax.axis_index("width") == 0, *pair)
+    w = lax.axis_index("width")
+    for v, at in zip((w, 1 - w), places):
+        rows = pl.ds(pl.multiple_of(v * slots, slots), slots)
+        a, b = normalise(first[rows], second[rows], 2 * feat)
+        normed[at : at + slots, :feat] = a
+        normed[at : at + slots, feat:] = b
+
+
+def of_cores(pair):
+    w = lax.axis_index("width")
+    return jnp.where(w == 0, pair[0], pair[1]), jnp.where(w == 0, pair[1], pair[0])
 
 
 def lengths_of(tokens):
     rows = tokens[tokens.shape[0] - 16 :, :128].astype(jnp.float32)
     every = [rows[k : k + 1, :1] for k in range(4)]
-    return every[:2], every[2:]
-
-
-def row_of(base, similar, row_len, blocks):
-    slots = similar.shape[0]
-    lane = lax.broadcasted_iota(jnp.int32, base.shape, 1)
-    for k, (place, length) in enumerate(blocks):
-        for v in range(2):
-            at = (2 * k + v) * slots
-            f = pair_f(similar[:, at : at + slots], row_len, length[v])
-            base = jnp.where(lane == 2 * place + v, f, base)
-    return base
+    return of_cores(every[:2]), of_cores(every[2:])
+
+
+def lanes_of(place):
+    w = lax.axis_index("width")
+    return 2 * place + w, 2 * place + 1 - w
+
+
+def put(out, entries):
+    lane = lax.broadcasted_iota(jnp.int32, out.shape, 1)
+    row = jnp.zeros(out.shape, jnp.float32)
+    for place, f in entries:
+        row = jnp.where(lane == place, f, row)
+    out[...] = row
 
 
 def near_kernel(half, o0, o1, y0, y1, tokens, local):
     slots = (o0.shape[0] - 16) // 2
-    w = lax.axis_index("width")
     chip = lax.axis_index("sample")
     y_chip, _, _ = peers(chip, half)
-    unpack(o0, o1, tokens, slots)
-    unpack(y0, y1, tokens, slots, 2 * slots)
+    unpack(o0, o1, tokens, slots, (0, 2 * slots))
+    unpack(y0, y1, tokens, slots, (slots, 3 * slots))
     row = lax.broadcasted_iota(jnp.int32, (16, 128), 0)
     table = jnp.zeros(row.shape, jnp.float32)
-    for v in range(2):
-        for k, source in enumerate((o0, y0)):
-            tail = source[2 * slots :, :128].astype(jnp.float32)
+    for k, source in enumerate((o0, y0)):
+        tail = source[2 * slots :, :128].astype(jnp.float32)
+        for v in range(2):
             table = jnp.where(row == 2 * k + v, tail[v : v + 1], table)
     tokens[4 * slots :, :128] = table.astype(tokens.dtype)
     len_o, len_y = lengths_of(tokens)
-    similar = dot_nt(tokens[pl.ds(w * slots, slots)], tokens[: 4 * slots])
-    blocks = ((chip, len_o), (y_chip, len_y))
-    local[...] = row_of(jnp.zeros(local.shape, jnp.float32), similar, of_core(len_o), blocks)
+    similar = dot_nt(tokens[:slots], tokens[: 4 * slots])
+    places = zip(zip(lanes_of(chip), lanes_of(y_chip)), zip(len_o, len_y))
+    entries = []
+    for lanes, lengths in places:
+        for lane, length in zip(lanes, lengths):
+            at = len(entries) * slots
+            entries.append((lane, pair_f(similar[:, at : at + slots], len_o[0], length)))
+    put(local, entries)
 
 
 def far_kernel(half, far_len, other_len, tokens, z0, z1, r0, r1, local, to_y, to_r, normed):
@@ -108,21 +117,29 @@
     w = lax.axis_index("width")
     chip = lax.axis_index("sample")
     y_chip, z_chip, r_chip = peers(chip, half)
-    unpack(z0, z1, normed, slots)
-    unpack(r0, r1, normed, slots, 2 * slots)
+    unpack(z0, z1, normed, slots, (0, slots))
+    unpack(r0, r1, normed, slots, (2 * slots, 3 * slots))
     len_o, len_y = lengths_of(tokens)
     len_z, len_r = (
-        [jnp.where(w == 0, a[v], b[v]).astype(jnp.float32) for v in range(2)]
+        of_cores([jnp.where(w == 0, a[v], b[v]).astype(jnp.float32) for v in range(2)])
         for a, b in ((far_len, other_len), (other_len, far_len))
     )
-    empty = jnp.zeros(local.shape, jnp.float32)
-    far = ((z_chip, len_z), (r_chip, len_r))
-    for k, (length, out) in enumerate(((len_o, local), (len_y, to_y))):
-        mine = tokens[pl.ds((2 * k + w) * slots, slots)]
-        out[...] = row_of(empty, dot_nt(mine, normed[...]), of_core(length), far)
-    mine = normed[pl.ds((2 + w) * slots, slots)]
-    near = ((chip, len_o), (y_chip, len_y))
-    to_r[...] = row_of(empty, dot_nt(mine, tokens[: 4 * slots]), of_core(len_r), near)
+    similar = dot_nt(tokens[: 2 * slots], normed[...])
+    col_len = (*len_z, *len_r)
+    col_lane = (*lanes_of(z_chip), *lanes_of(r_chip))
+    fs = []
+    for k, length in enumerate((len_o[0], len_y[0])):
+        rows = similar[k * slots : (k + 1) * slots]
+        fs.append([pair_f(rows[:, n * slots : (n + 1) * slots], length, col_len[n]) for n in range(4)])
+    similar = dot_nt(tokens[2 * slots : 4 * slots], normed[2 * slots : 3 * slots])
+    rest = [
+        pair_f(similar[k * slots : (k + 1) * slots], length, len_r[0])
+        for k, length in enumerate((len_o[1], len_y[1]))
+    ]
+    put(local, zip(col_lane, fs[0]))
+    put(to_y, zip(col_lane, fs[1]))
+    near_lane = (*lanes_of(chip), *lanes_of(y_chip))
+    put(to_r, zip(near_lane, (fs[0][2], rest[0], fs[1][2], rest[1])))
 
 
 def final_kernel(near, local, from_y, from_r, scores, utility):

time: 29.3 us -> 28.6 us (0.976)
  Pallas kernels: 4.85 us -> 4.14 us
    pallas_call x4, Pallas kernels: 4.85 us -> 4.14 us  [call(): pl.pallas_call(kernel, out_shape=outs, in_specs=[pl.BlockSpec(memory_spac...]
where the time goes in v4:
time: 28.6 us; the launch traced here: 28.4 us
  starting transfers between devices  12.4 us (43%)
  waiting for transfers between devices  11.2 us (39%)
  Pallas kernels  4.14 us (14%)
  between operations  0.65 us (2%)
    ppermute x5, starting transfers between devices, send(): return lax.ppermute(x, 'sample', route)  11.4 us
    ppermute x5, waiting for transfers between devices, send(): return lax.ppermute(x, 'sample', route)  8.27 us
    pallas_call x4, Pallas kernels, call(): pl.pallas_call(kernel, out_shape=outs, in_specs=[pl.BlockSpec(memory_spac...  4.14 us
    ppermute x5, waiting for transfers between devices, other(): return lax.ppermute(x, 'width', swap)  2.96 us
  transfers between devices with their start and end apart: 11, of which 6 were waited for; matrix products, arithmetic and copies ran while one was open for 0% of the time, Pallas kernels for 7%

profile of v4, /device:TPU:0, one launch (start us, length us, event | category | flops | bytes accessed | tf_op | source)
XLA Modules:
  0.0 28.4 jit_solution(16377842755953306102)
XLA Ops:
  0.6 3.1 %collective-permute-start.3 = (bf16[256,512]{1,0:T(8,128)(2,1)}, bf16[256,512]{1,0:T(8,128)(2,1)S(1)}, u32[]{:S(2)}, u32[]{:S(2)}) collective-permute-start(bf16[256,512]{1,0:T(8,128)(2,1)} %bitcast.3), channel_id=1, source_target_pairs={{0,4},{2,6},{4,0},{6,2},{8,12},{10,14},{12,8},{14,10},{1,5},{3,7},... | collective-permute-start | bytes 786440 | tf_op jit(solution)/shard_map/ppermute | solution.py:167
  3.7 2.6 %collective-permute-start.4 = (bf16[256,512]{1,0:T(8,128)(2,1)}, bf16[256,512]{1,0:T(8,128)(2,1)S(1)}, u32[]{:S(2)}, u32[]{:S(2)}) collective-permute-start(bf16[256,512]{1,0:T(8,128)(2,1)} %bitcast.4), channel_id=1, source_target_pairs={{0,8},{2,10},{4,12},{6,14},{8,4},{10,6},{12,0},{14,2},{1,9},{3,11}... | collective-permute-start | bytes 786440 | tf_op jit(solution)/shard_map/ppermute | solution.py:167
  6.3 0.4 %collective-permute-start.5 = (s32[2]{0:T(128)}, s32[2]{0:T(128)S(1)}, u32[]{:S(2)}, u32[]{:S(2)}) collective-permute-start(s32[2]{0:T(128)} %param.5), channel_id=1, source_target_pairs={{0,4},{2,6},{4,0},{6,2},{8,12},{10,14},{12,8},{14,10},{1,9},{3,11}... | collective-permute-start | bytes 32 | tf_op jit(solution)/shard_map/ppermute | solution.py:205
  6.8 11.0 %conditional.1 = ((bf16[528,1024]{1,0:T(8,128)(2,1)S(1)}, f32[1,16]{1,0:T(1,128)S(1)})) conditional(s32[]{:T(128)} %convert_element_type.3, () %tuple.16, (bf16[2,128,512]{2,1,0:T(8,128)(2,1)}, s32[2]{0:T(128)}) %tuple.17), branch_computations={%region_0.0_spmd, %region_1.0_spmd} | conditional | bytes 3342464 | solution.py:209
  6.8 1.0 %branch_1_fun.2.o0 = bf16[272,512]{1,0:T(8,128)(2,1)S(1)} custom-call(s32[2]{0:T(128)} %get-tuple-element.4.lengths, bf16[256,512]{1,0:T(8,128)(2,1)} %bitcast.5), custom_call_target="tpu_custom_call" | custom-call | tf_op jit(solution)/shard_map/cond/branch_1_fun/pallas_call | solution.py:177
  7.7 1.6 %collective-permute-start.1 = (bf16[272,512]{1,0:T(8,128)(2,1)S(1)}, bf16[272,512]{1,0:T(8,128)(2,1)S(1)}, u32[]{:S(2)}, u32[]{:S(2)}) collective-permute-start(bf16[272,512]{1,0:T(8,128)(2,1)S(1)} %branch_1_fun.2.o0), channel_id=1, source_target_pairs={{0,2},{2,0},{4,6},{6,4},{8,10},{10,8},{12,14},{14,12},{1,3},{3,1},... | collective-permute-start | bytes 835592 | tf_op jit(solution)/shard_map/cond/branch_1_fun/ppermute | solution.py:167
  9.3 0.0 collective-permute-start
  9.3 5.9 %collective-permute-done.1.y0 = bf16[272,512]{1,0:T(8,128)(2,1)S(1)} collective-permute-done((bf16[272,512]{1,0:T(8,128)(2,1)S(1)}, bf16[272,512]{1,0:T(8,128)(2,1)S(1)}, u32[]{:S(2)}, u32[]{:S(2)}) %collective-permute-start.1) | collective-permute-done | bytes 278560 | tf_op jit(solution)/shard_map/cond/branch_1_fun/ppermute | solution.py:167
  15.2 1.6 %collective-permute-done.2.y1 = bf16[272,512]{1,0:T(8,128)(2,1)S(1)} collective-permute-done((bf16[272,512]{1,0:T(8,128)(2,1)S(1)}, bf16[272,512]{1,0:T(8,128)(2,1)S(1)}, u32[]{:S(2)}, u32[]{:S(2)}) %collective-permute-start.2) | collective-permute-done | bytes 278560 | tf_op jit(solution)/shard_map/cond/branch_1_fun/ppermute | solution.py:170
  16.8 1.0 %branch_1_fun.3 = (bf16[528,1024]{1,0:T(8,128)(2,1)S(1)}, f32[1,16]{1,0:T(1,128)S(1)}) custom-call(bf16[272,512]{1,0:T(8,128)(2,1)S(1)} %branch_1_fun.2.o0, bf16[272,512]{1,0:T(8,128)(2,1)S(1)} %collective-permute-done.o1, bf16[272,512]{1,0:T(8,128)(2,1)S(1)} %collective-permute-done.1.y0, bf16[272,512]{1,0:T(8,128)(2,1)S(1)} %collective-permute-done.2.y1), custom_call_target="tpu_custom_call" | custom-call | tf_op jit(solution)/shard_map/cond/branch_1_fun/pallas_call | solution.py:177
  17.8 0.0 collective-permute-done.3.z0
  17.8 0.3 %collective-permute-done.4.r0 = bf16[256,512]{1,0:T(8,128)(2,1)S(1)} collective-permute-done((bf16[256,512]{1,0:T(8,128)(2,1)}, bf16[256,512]{1,0:T(8,128)(2,1)S(1)}, u32[]{:S(2)}, u32[]{:S(2)}) %collective-permute-start.4) | collective-permute-done | bytes 262176 | tf_op jit(solution)/shard_map/ppermute | solution.py:167
  18.2 0.0 collective-permute-start.7
  18.2 0.5 %collective-permute-start.8 = (bf16[256,512]{1,0:T(8,128)(2,1)S(1)}, bf16[256,512]{1,0:T(8,128)(2,1)S(1)}, u32[]{:S(2)}, u32[]{:S(2)}) collective-permute-start(bf16[256,512]{1,0:T(8,128)(2,1)S(1)} %collective-permute-done.4.r0), channel_id=1, source_target_pairs={{0,1},{1,0},{2,3},{3,2},{4,5},{5,4},{6,7},{7,6},{8,9},{9,8},{10,11... | collective-permute-start | bytes 786440 | tf_op jit(solution)/shard_map/ppermute | solution.py:170
  18.7 0.0 collective-permute-start.6
  18.7 1.4 %collective-permute-done.6.other_len = s32[2]{0:T(128)S(1)} collective-permute-done((s32[2]{0:T(128)S(1)}, s32[2]{0:T(128)S(1)}, u32[]{:S(2)}, u32[]{:S(2)}) %collective-permute-start.6) | collective-permute-done | bytes 40 | tf_op jit(solution)/shard_map/ppermute | solution.py:170
  20.1 0.0 collective-permute-done.7.z1
  20.1 0.0 collective-permute-done.8.r1
  20.1 1.6 %shard_map.41 = (f32[1,16]{1,0:T(1,128)S(1)}, f32[1,16]{1,0:T(1,128)S(1)}, f32[1,16]{1,0:T(1,128)S(1)}) custom-call(s32[2]{0:T(128)S(1)} %collective-permute-done.5.far_len, s32[2]{0:T(128)S(1)} %collective-permute-done.6.other_len, bf16[528,1024]{1,0:T(8,128)(2,1)S(1)} %get-tuple-element.22.tokens, bf16[256,512]{1,0:T(8,128)(2,1)S(1)} %collective-permute-done.3.z0, ...), custom_call_target="tpu_custom_call" | custom-call | tf_op jit(solution)/shard_map/pallas_call | solution.py:177
  21.6 2.6 %collective-permute-start.10 = (f32[1,16]{1,0:T(1,128)S(1)}, f32[1,16]{1,0:T(1,128)S(1)}, u32[]{:S(2)}, u32[]{:S(2)}) collective-permute-start(f32[1,16]{1,0:T(1,128)S(1)} %get-tuple-element.27), channel_id=1, source_target_pairs={{8,0},{10,2},{12,4},{14,6},{4,8},{6,10},{0,12},{2,14},{9,1},{11,3}... | collective-permute-start | bytes 200 | tf_op jit(solution)/shard_map/ppermute | solution.py:167
  24.3 1.5 %collective-permute-start.9 = (f32[1,16]{1,0:T(1,128)S(1)}, f32[1,16]{1,0:T(1,128)S(1)}, u32[]{:S(2)}, u32[]{:S(2)}) collective-permute-start(f32[1,16]{1,0:T(1,128)S(1)} %get-tuple-element.26), channel_id=1, source_target_pairs={{0,2},{2,0},{4,6},{6,4},{8,10},{10,8},{12,14},{14,12},{1,3},{3,1},... | collective-permute-start | bytes 200 | tf_op jit(solution)/shard_map/ppermute | solution.py:167
  25.8 0.3 %collective-permute-done.10.from_r = f32[1,16]{1,0:T(1,128)S(1)} collective-permute-done((f32[1,16]{1,0:T(1,128)S(1)}, f32[1,16]{1,0:T(1,128)S(1)}, u32[]{:S(2)}, u32[]{:S(2)}) %collective-permute-start.10) | collective-permute-done | bytes 96 | tf_op jit(solution)/shard_map/ppermute | solution.py:167
  26.1 1.7 %collective-permute-done.9.from_y = f32[1,16]{1,0:T(1,128)S(1)} collective-permute-done((f32[1,16]{1,0:T(1,128)S(1)}, f32[1,16]{1,0:T(1,128)S(1)}, u32[]{:S(2)}, u32[]{:S(2)}) %collective-permute-start.9) | collective-permute-done | bytes 96 | tf_op jit(solution)/shard_map/ppermute | solution.py:167
  27.8 0.6 %shard_map.42 = (f32[1,16]{1,0:T(1,128)}, f32[1,1]{1,0:T(1,128)}) custom-call(f32[1,16]{1,0:T(1,128)S(1)} %get-tuple-element.19.near, f32[1,16]{1,0:T(1,128)S(1)} %get-tuple-element.25.local, f32[1,16]{1,0:T(1,128)S(1)} %collective-permute-done.9.from_y, f32[1,16]{1,0:T(1,128)S(1)} %collective-permute-done.10.from_r), custom_call_target="tpu_custom_call" | custom-call | tf_op jit(solution)/shard_map/pallas_call | solution.py:177
  (3 shorter events, 0.0 us)
Async XLA Ops:
  0.6 17.2 %collective-permute-start.3 = (bf16[256,512]{1,0:T(8,128)(2,1)}, bf16[256,512]{1,0:T(8,128)(2,1)S(1)}, u32[]{:S(2)}, u32[]{:S(2)}) collective-permute-start(bf16[256,512]{1,0:T(8,128)(2,1)} %bitcast.3), channel_id=1, source_target_pairs={{0,4},{2,6},{4,0},{6,2},{8,12},{10,14},{12,8},{14,10},{1,5},{3,7},... | collective-permute-start | bytes 786440 | tf_op jit(solution)/shard_map/ppermute | solution.py:167
  3.7 14.4 %collective-permute-start.4 = (bf16[256,512]{1,0:T(8,128)(2,1)}, bf16[256,512]{1,0:T(8,128)(2,1)S(1)}, u32[]{:S(2)}, u32[]{:S(2)}) collective-permute-start(bf16[256,512]{1,0:T(8,128)(2,1)} %bitcast.4), channel_id=1, source_target_pairs={{0,8},{2,10},{4,12},{6,14},{8,4},{10,6},{12,0},{14,2},{1,9},{3,11}... | collective-permute-start | bytes 786440 | tf_op jit(solution)/shard_map/ppermute | solution.py:167
  6.3 11.5 %collective-permute-start.5 = (s32[2]{0:T(128)}, s32[2]{0:T(128)S(1)}, u32[]{:S(2)}, u32[]{:S(2)}) collective-permute-start(s32[2]{0:T(128)} %param.5), channel_id=1, source_target_pairs={{0,4},{2,6},{4,0},{6,2},{8,12},{10,14},{12,8},{14,10},{1,9},{3,11}... | collective-permute-start | bytes 32 | tf_op jit(solution)/shard_map/ppermute | solution.py:205
  7.7 7.5 %collective-permute-start.1 = (bf16[272,512]{1,0:T(8,128)(2,1)S(1)}, bf16[272,512]{1,0:T(8,128)(2,1)S(1)}, u32[]{:S(2)}, u32[]{:S(2)}) collective-permute-start(bf16[272,512]{1,0:T(8,128)(2,1)S(1)} %branch_1_fun.2.o0), channel_id=1, source_target_pairs={{0,2},{2,0},{4,6},{6,4},{8,10},{10,8},{12,14},{14,12},{1,3},{3,1},... | collective-permute-start | bytes 835592 | tf_op jit(solution)/shard_map/cond/branch_1_fun/ppermute | solution.py:167
  9.3 5.9 %collective-permute-start = (bf16[272,512]{1,0:T(8,128)(2,1)S(1)}, bf16[272,512]{1,0:T(8,128)(2,1)S(1)}, u32[]{:S(2)}, u32[]{:S(2)}) collective-permute-start(bf16[272,512]{1,0:T(8,128)(2,1)S(1)} %branch_1_fun.2.o0), channel_id=1, source_target_pairs={{0,1},{1,0},{2,3},{3,2},{4,5},{5,4},{6,7},{7,6},{8,9},{9,8},{10,11... | collective-permute-start | bytes 835592 | tf_op jit(solution)/shard_map/cond/branch_1_fun/ppermute | solution.py:170
  15.2 1.6 %collective-permute-start.2 = (bf16[272,512]{1,0:T(8,128)(2,1)S(1)}, bf16[272,512]{1,0:T(8,128)(2,1)S(1)}, u32[]{:S(2)}, u32[]{:S(2)}) collective-permute-start(bf16[272,512]{1,0:T(8,128)(2,1)S(1)} %collective-permute-done.1.y0), channel_id=1, source_target_pairs={{0,1},{1,0},{2,3},{3,2},{4,5},{5,4},{6,7},{7,6},{8,9},{9,8},{10,11... | collective-permute-start | bytes 835592 | tf_op jit(solution)/shard_map/cond/branch_1_fun/ppermute | solution.py:170
  18.2 1.9 %collective-permute-start.7 = (bf16[256,512]{1,0:T(8,128)(2,1)S(1)}, bf16[256,512]{1,0:T(8,128)(2,1)S(1)}, u32[]{:S(2)}, u32[]{:S(2)}) collective-permute-start(bf16[256,512]{1,0:T(8,128)(2,1)S(1)} %collective-permute-done.3.z0), channel_id=1, source_target_pairs={{0,1},{1,0},{2,3},{3,2},{4,5},{5,4},{6,7},{7,6},{8,9},{9,8},{10,11... | collective-permute-start | bytes 786440 | tf_op jit(solution)/shard_map/ppermute | solution.py:170
  18.2 1.9 %collective-permute-start.8 = (bf16[256,512]{1,0:T(8,128)(2,1)S(1)}, bf16[256,512]{1,0:T(8,128)(2,1)S(1)}, u32[]{:S(2)}, u32[]{:S(2)}) collective-permute-start(bf16[256,512]{1,0:T(8,128)(2,1)S(1)} %collective-permute-done.4.r0), channel_id=1, source_target_pairs={{0,1},{1,0},{2,3},{3,2},{4,5},{5,4},{6,7},{7,6},{8,9},{9,8},{10,11... | collective-permute-start | bytes 786440 | tf_op jit(solution)/shard_map/ppermute | solution.py:170
  18.7 1.4 %collective-permute-start.6 = (s32[2]{0:T(128)S(1)}, s32[2]{0:T(128)S(1)}, u32[]{:S(2)}, u32[]{:S(2)}) collective-permute-start(s32[2]{0:T(128)S(1)} %collective-permute-done.5.far_len), channel_id=1, source_target_pairs={{0,1},{1,0},{2,3},{3,2},{4,5},{5,4},{6,7},{7,6},{8,9},{9,8},{10,11... | collective-permute-start | bytes 32 | tf_op jit(solution)/shard_map/ppermute | solution.py:170
  21.6 4.5 %collective-permute-start.10 = (f32[1,16]{1,0:T(1,128)S(1)}, f32[1,16]{1,0:T(1,128)S(1)}, u32[]{:S(2)}, u32[]{:S(2)}) collective-permute-start(f32[1,16]{1,0:T(1,128)S(1)} %get-tuple-element.27), channel_id=1, source_target_pairs={{8,0},{10,2},{12,4},{14,6},{4,8},{6,10},{0,12},{2,14},{9,1},{11,3}... | collective-permute-start | bytes 200 | tf_op jit(solution)/shard_map/ppermute | solution.py:167
  24.3 3.5 %collective-permute-start.9 = (f32[1,16]{1,0:T(1,128)S(1)}, f32[1,16]{1,0:T(1,128)S(1)}, u32[]{:S(2)}, u32[]{:S(2)}) collective-permute-start(f32[1,16]{1,0:T(1,128)S(1)} %get-tuple-element.26), channel_id=1, source_target_pairs={{0,2},{2,0},{4,6},{6,4},{8,10},{10,8},{12,14},{14,12},{1,3},{3,1},... | collective-permute-start | bytes 200 | tf_op jit(solution)/shard_map/ppermute | solution.py:167

commit v5 on v4

--- a/solution.py
+++ b/solution.py
@@ -80,18 +80,16 @@
     return 2 * place + w, 2 * place + 1 - w
 
 
-def put(out, entries):
+def put(out, entries, base=None):
     lane = lax.broadcasted_iota(jnp.int32, out.shape, 1)
-    row = jnp.zeros(out.shape, jnp.float32)
+    row = jnp.zeros(out.shape, jnp.float32) if base is None else base[...]
     for place, f in entries:
         row = jnp.where(lane == place, f, row)
     out[...] = row
 
 
-def near_kernel(half, o0, o1, y0, y1, tokens, local):
+def near_kernel(o0, o1, y0, y1, tokens):
     slots = (o0.shape[0] - 16) // 2
-    chip = lax.axis_index("sample")
-    y_chip, _, _ = peers(chip, half)
     unpack(o0, o1, tokens, slots, (0, 2 * slots))
     unpack(y0, y1, tokens, slots, (slots, 3 * slots))
     row = lax.broadcasted_iota(jnp.int32, (16, 128), 0)
@@ -101,51 +99,70 @@
         for v in range(2):
             table = jnp.where(row == 2 * k + v, tail[v : v + 1], table)
     tokens[4 * slots :, :128] = table.astype(tokens.dtype)
+
+
+def pairs_kernel(half, tokens, local):
+    slots = (tokens.shape[0] - 16) // 4
+    chip = lax.axis_index("sample")
+    y_chip, _, _ = peers(chip, half)
     len_o, len_y = lengths_of(tokens)
     similar = dot_nt(tokens[:slots], tokens[: 4 * slots])
-    places = zip(zip(lanes_of(chip), lanes_of(y_chip)), zip(len_o, len_y))
     entries = []
-    for lanes, lengths in places:
-        for lane, length in zip(lanes, lengths):
-            at = len(entries) * slots
-            entries.append((lane, pair_f(similar[:, at : at + slots], len_o[0], length)))
+    lanes = zip(lanes_of(chip), lanes_of(y_chip))
+    for k, (lane, length) in enumerate(zip(sum(lanes, ()), sum(zip(len_o, len_y), ()))):
+        f = pair_f(similar[:, k * slots : (k + 1) * slots], len_o[0], length)
+        entries.append((lane, f))
     put(local, entries)
 
 
-def far_kernel(half, far_len, other_len, tokens, z0, z1, r0, r1, local, to_y, to_r, normed):
+def far_length(far_len, other_len, core):
+    mine = lax.axis_index("width") == core
+    pair = [jnp.where(mine, far_len[v], other_len[v]).astype(jnp.float32) for v in range(2)]
+    return of_cores(pair)
+
+
+def z_kernel(half, far_len, other_len, tokens, z0, z1, local_in, local, to_y, normed):
     slots = z0.shape[0] // 2
-    w = lax.axis_index("width")
+    _, z_chip, _ = peers(lax.axis_index("sample"), half)
+    unpack(z0, z1, normed, slots, (0, slots))
+    len_o, len_y = lengths_of(tokens)
+    len_z = far_length(far_len, other_len, 0)
+    similar = dot_nt(tokens[: 2 * slots], normed[...])
+    for k, (length, base, out) in enumerate(((len_o, local_in, local), (len_y, None, to_y))):
+        rows = similar[k * slots : (k + 1) * slots]
+        fs = [pair_f(rows[:, n * slots : (n + 1) * slots], length[0], len_z[n]) for n in range(2)]
+        put(out, zip(lanes_of(z_chip), fs), base)
+
+
+def r_kernel(
+    half, far_len, other_len, tokens, r0, r1, local_in, to_y_in, local, to_y, to_r, normed
+):
+    slots = r0.shape[0] // 2
     chip = lax.axis_index("sample")
-    y_chip, z_chip, r_chip = peers(chip, half)
-    unpack(z0, z1, normed, slots, (0, slots))
-    unpack(r0, r1, normed, slots, (2 * slots, 3 * slots))
+    y_chip, _, r_chip = peers(chip, half)
+    unpack(r0, r1, normed, slots, (0, slots))
     len_o, len_y = lengths_of(tokens)
-    len_z, len_r = (
-        of_cores([jnp.where(w == 0, a[v], b[v]).astype(jnp.float32) for v in range(2)])
-        for a, b in ((far_len, other_len), (other_len, far_len))
-    )
+    len_r = far_length(far_len, other_len, 1)
     similar = dot_nt(tokens[: 2 * slots], normed[...])
-    col_len = (*len_z, *len_r)
-    col_lane = (*lanes_of(z_chip), *lanes_of(r_chip))
-    fs = []
-    for k, length in enumerate((len_o[0], len_y[0])):
+    own = []
+    for k, (length, base, out) in enumerate(((len_o, local_in, local), (len_y, to_y_in, to_y))):
         rows = similar[k * slots : (k + 1) * slots]
-        fs.append([pair_f(rows[:, n * slots : (n + 1) * slots], length, col_len[n]) for n in range(4)])
-    similar = dot_nt(tokens[2 * slots : 4 * slots], normed[2 * slots : 3 * slots])
+        fs = [pair_f(rows[:, n * slots : (n + 1) * slots], length[0], len_r[n]) for n in range(2)]
+        put(out, zip(lanes_of(r_chip), fs), base)
+        own.append(fs[0])
+    similar = dot_nt(tokens[2 * slots : 4 * slots], normed[:slots])
     rest = [
-        pair_f(similar[k * slots : (k + 1) * slots], length, len_r[0])
-        for k, length in enumerate((len_o[1], len_y[1]))
+        pair_f(similar[k * slots : (k + 1) * slots], length[1], len_r[0])
+        for k, length in enumerate((len_o, len_y))
     ]
-    put(local, zip(col_lane, fs[0]))
-    put(to_y, zip(col_lane, fs[1]))
     near_lane = (*lanes_of(chip), *lanes_of(y_chip))
-    put(to_r, zip(near_lane, (fs[0][2], rest[0], fs[1][2], rest[1])))
-
-
-def final_kernel(near, local, from_y, from_r, scores, utility):
+    put(to_r, zip(near_lane, (own[0], rest[0], own[1], rest[1])))
+
+
+def final_kernel(local, from_y, from_r, scores, utility):
     hyps = local.shape[1]
     own = 2 * lax.axis_index("sample") + lax.axis_index("width")
-    row = near[...] + local[...] + from_y[...] + from_r[...]
+    row = local[...] + from_y[...] + from_r[...]
     scores[...] = row
     lane = lax.broadcasted_iota(jnp.int32, row.shape, 1)
     rest = jnp.where(lane == own, 0.0, row)
@@ -192,11 +209,12 @@
             [pl.ANY] * 2,
         )
         y = send(packed, y_route)
-        return call(
-            functools.partial(near_kernel, half),
+        (tokens,) = call(
+            near_kernel,
             (packed, other(packed), y, other(y)),
-            (jax.ShapeDtypeStruct((4 * slots + 16, 2 * feat), jnp.bfloat16), row),
+            (jax.ShapeDtypeStruct((4 * slots + 16, 2 * feat), jnp.bfloat16),),
         )
+        return tokens
 
     def nothing():
         return jax.tree.map(lambda x: jnp.zeros(x.shape, x.dtype), jax.eval_shape(near))
@@ -206,18 +224,29 @@
     block = embeddings.reshape(2 * slots, feat)
     z = send(block, z_route)
     r = send(block, r_route)
-    tokens, near_row = lax.cond(lax.axis_index("sample") >= 0, near, nothing)
-    tokens, z, r, far_len = lax.optimization_barrier((tokens, z, r, far_len))
+    tokens = lax.cond(lax.axis_index("sample") >= 0, near, nothing)
+    tokens, z, far_len = lax.optimization_barrier((tokens, z, far_len))
+    z_other, far_other = other(z), other(far_len)
+    (local,) = call(functools.partial(pairs_kernel, half), (tokens,), (row,))
+    r, far_other, z_other, local = lax.optimization_barrier((r, far_other, z_other, local))
+    scratch = [pltpu.VMEM((2 * slots, 2 * feat), jnp.bfloat16)]
+    local, to_y = call(
+        functools.partial(z_kernel, half),
+        (far_len, far_other, tokens, z, z_other, local),
+        (row, row),
+        scratch,
+        [SMEM] * 2 + [VMEM] * 4,
+    )
     local, to_y, to_r = call(
-        functools.partial(far_kernel, half),
-        (far_len, other(far_len), tokens, z, other(z), r, other(r)),
+        functools.partial(r_kernel, half),
+        (far_len, far_other, tokens, r, other(r), local, to_y),
         (row, row, row),
-        [pltpu.VMEM((4 * slots, 2 * feat), jnp.bfloat16)],
+        scratch,
         [SMEM] * 2 + [VMEM] * 5,
     )
     one = jax.ShapeDtypeStruct((1, 1), jnp.float32)
-    from_y, from_r = send(to_y, y_route), send(to_r, back_route)
-    scores, utility = call(final_kernel, (near_row, local, from_y, from_r), (row, one))
+    from_r, from_y = send(to_r, back_route), send(to_y, y_route)
+    scores, utility = call(final_kernel, (local, from_y, from_r), (row, one))
     return scores, utility.reshape(1)
 
 

time: 28.6 us -> 28.3 us (0.990)
  waiting for transfers between devices: 11.2 us -> 9.58 us
  Pallas kernels: 4.14 us -> 5.06 us
  starting transfers between devices: 12.4 us -> 12.9 us
    pallas_call x4 -> x6, Pallas kernels: 4.14 us -> 5.06 us  [call(): pl.pallas_call(kernel, out_shape=outs, in_specs=[pl.BlockSpec(memory_spac...]
    ppermute x5, waiting for transfers between devices: 2.96 us -> 2.13 us  [other(): return lax.ppermute(x, 'width', swap)]
    ppermute x5, waiting for transfers between devices: 8.27 us -> 7.45 us  [send(): return lax.ppermute(x, 'sample', route)]
    ppermute x5, starting transfers between devices: 11.4 us -> 11.7 us  [send(): return lax.ppermute(x, 'sample', route)]
  transfers between devices with their start and end apart: 11 -> 11, of which waited for: 6 -> 5; matrix products, arithmetic and copies ran while one was open for 0% -> 0% of each run, Pallas kernels for 7% -> 11%
where the time goes in v5:
time: 28.3 us; the launch traced here: 28.2 us
  starting transfers between devices  12.9 us (46%)
  waiting for transfers between devices  9.58 us (34%)
  Pallas kernels  5.06 us (18%)
  between operations  0.66 us (2%)
    ppermute x5, starting transfers between devices, send(): return lax.ppermute(x, 'sample', route)  11.7 us
    ppermute x5, waiting for transfers between devices, send(): return lax.ppermute(x, 'sample', route)  7.45 us
    pallas_call x6, Pallas kernels, call(): pl.pallas_call(kernel, out_shape=outs, in_specs=[pl.BlockSpec(memory_spac...  5.06 us
    ppermute x5, waiting for transfers between devices, other(): return lax.ppermute(x, 'width', swap)  2.13 us
    ppermute x5, starting transfers between devices, other(): return lax.ppermute(x, 'width', swap)  0.72 us
  transfers between devices with their start and end apart: 11, of which 5 were waited for; matrix products, arithmetic and copies ran while one was open for 0% of the time, Pallas kernels for 11%

profile of v5, /device:TPU:0, one launch (start us, length us, event | category | flops | bytes accessed | tf_op | source)
XLA Modules:
  0.0 28.2 jit_solution(2832285684482381167)
XLA Ops:
  0.6 3.1 %collective-permute-start.3 = (bf16[256,512]{1,0:T(8,128)(2,1)}, bf16[256,512]{1,0:T(8,128)(2,1)S(1)}, u32[]{:S(2)}, u32[]{:S(2)}) collective-permute-start(bf16[256,512]{1,0:T(8,128)(2,1)} %bitcast.3), channel_id=1, source_target_pairs={{0,4},{2,6},{4,0},{6,2},{8,12},{10,14},{12,8},{14,10},{1,5},{3,7},... | collective-permute-start | bytes 786440 | tf_op jit(solution)/shard_map/ppermute | solution.py:184
  3.7 2.6 %collective-permute-start.5 = (bf16[256,512]{1,0:T(8,128)(2,1)}, bf16[256,512]{1,0:T(8,128)(2,1)S(1)}, u32[]{:S(2)}, u32[]{:S(2)}) collective-permute-start(bf16[256,512]{1,0:T(8,128)(2,1)} %bitcast.4), channel_id=1, source_target_pairs={{0,8},{2,10},{4,12},{6,14},{8,4},{10,6},{12,0},{14,2},{1,9},{3,11}... | collective-permute-start | bytes 786440 | tf_op jit(solution)/shard_map/ppermute | solution.py:184
  6.3 0.4 %collective-permute-start.4 = (s32[2]{0:T(128)}, s32[2]{0:T(128)S(1)}, u32[]{:S(2)}, u32[]{:S(2)}) collective-permute-start(s32[2]{0:T(128)} %param.5), channel_id=1, source_target_pairs={{0,4},{2,6},{4,0},{6,2},{8,12},{10,14},{12,8},{14,10},{1,9},{3,11}... | collective-permute-start | bytes 32 | tf_op jit(solution)/shard_map/ppermute | solution.py:223
  6.8 10.4 %conditional.1 = (bf16[528,1024]{1,0:T(8,128)(2,1)S(1)}) conditional(s32[]{:T(128)} %convert_element_type.3, () %tuple.16, (bf16[2,128,512]{2,1,0:T(8,128)(2,1)}, s32[2]{0:T(128)}) %tuple.17), branch_computations={%region_0.0_spmd, %region_1.0_spmd} | conditional | bytes 3342464 | solution.py:227
  6.8 1.0 %branch_1_fun.2.o0 = bf16[272,512]{1,0:T(8,128)(2,1)S(1)} custom-call(s32[2]{0:T(128)} %get-tuple-element.4.lengths, bf16[256,512]{1,0:T(8,128)(2,1)} %bitcast.5), custom_call_target="tpu_custom_call" | custom-call | tf_op jit(solution)/shard_map/cond/branch_1_fun/pallas_call | solution.py:194
  7.7 1.6 %collective-permute-start.1 = (bf16[272,512]{1,0:T(8,128)(2,1)S(1)}, bf16[272,512]{1,0:T(8,128)(2,1)S(1)}, u32[]{:S(2)}, u32[]{:S(2)}) collective-permute-start(bf16[272,512]{1,0:T(8,128)(2,1)S(1)} %branch_1_fun.2.o0), channel_id=1, source_target_pairs={{0,2},{2,0},{4,6},{6,4},{8,10},{10,8},{12,14},{14,12},{1,3},{3,1},... | collective-permute-start | bytes 835592 | tf_op jit(solution)/shard_map/cond/branch_1_fun/ppermute | solution.py:184
  9.3 0.0 collective-permute-start
  9.3 5.9 %collective-permute-done.1.y0 = bf16[272,512]{1,0:T(8,128)(2,1)S(1)} collective-permute-done((bf16[272,512]{1,0:T(8,128)(2,1)S(1)}, bf16[272,512]{1,0:T(8,128)(2,1)S(1)}, u32[]{:S(2)}, u32[]{:S(2)}) %collective-permute-start.1) | collective-permute-done | bytes 278560 | tf_op jit(solution)/shard_map/cond/branch_1_fun/ppermute | solution.py:184
  15.2 1.6 %collective-permute-done.2.y1 = bf16[272,512]{1,0:T(8,128)(2,1)S(1)} collective-permute-done((bf16[272,512]{1,0:T(8,128)(2,1)S(1)}, bf16[272,512]{1,0:T(8,128)(2,1)S(1)}, u32[]{:S(2)}, u32[]{:S(2)}) %collective-permute-start.2) | collective-permute-done | bytes 278560 | tf_op jit(solution)/shard_map/cond/branch_1_fun/ppermute | solution.py:187
  16.8 0.3 %branch_1_fun.3 = bf16[528,1024]{1,0:T(8,128)(2,1)S(1)} custom-call(bf16[272,512]{1,0:T(8,128)(2,1)S(1)} %branch_1_fun.2.o0, bf16[272,512]{1,0:T(8,128)(2,1)S(1)} %collective-permute-done.o1, bf16[272,512]{1,0:T(8,128)(2,1)S(1)} %collective-permute-done.1.y0, bf16[272,512]{1,0:T(8,128)(2,1)S(1)} %collective-permute-done.2.y1), custom_call_target="tpu_custom_call" | custom-call | tf_op jit(solution)/shard_map/cond/branch_1_fun/pallas_call | solution.py:194
  17.1 0.2 collective-permute-start.7
  17.3 0.4 %collective-permute-start.6 = (s32[2]{0:T(128)S(1)}, s32[2]{0:T(128)S(1)}, u32[]{:S(2)}, u32[]{:S(2)}) collective-permute-start(s32[2]{0:T(128)S(1)} %collective-permute-done.4.far_len), channel_id=1, source_target_pairs={{0,1},{1,0},{2,3},{3,2},{4,5},{5,4},{6,7},{7,6},{8,9},{9,8},{10,11... | collective-permute-start | bytes 32 | tf_op jit(solution)/shard_map/ppermute | solution.py:187
  17.7 0.7 %shard_map.41.local_in = f32[1,16]{1,0:T(1,128)S(1)} custom-call(bf16[528,1024]{1,0:T(8,128)(2,1)S(1)} %get-tuple-element.39.tokens), custom_call_target="tpu_custom_call" | custom-call | tf_op jit(solution)/shard_map/pallas_call | solution.py:194
  18.4 0.0 collective-permute-done.5.r0
  18.4 0.3 %collective-permute-done.6.other_len = s32[2]{0:T(128)S(1)} collective-permute-done((s32[2]{0:T(128)S(1)}, s32[2]{0:T(128)S(1)}, u32[]{:S(2)}, u32[]{:S(2)}) %collective-permute-start.6) | collective-permute-done | bytes 40 | tf_op jit(solution)/shard_map/ppermute | solution.py:187
  18.7 0.0 collective-permute-done.7.z1
  18.7 0.1 collective-permute-start.8
  18.9 1.2 %shard_map.42 = (f32[1,16]{1,0:T(1,128)S(1)}, f32[1,16]{1,0:T(1,128)S(1)}) custom-call(s32[2]{0:T(128)S(1)} %collective-permute-done.4.far_len, s32[2]{0:T(128)S(1)} %collective-permute-done.6.other_len, bf16[528,1024]{1,0:T(8,128)(2,1)S(1)} %get-tuple-element.39.tokens, bf16[256,512]{1,0:T(8,128)(2,1)S(1)} %collective-permute-done.3.z0, ...), custom_call_target="tpu_custom_call" | custom-call | tf_op jit(solution)/shard_map/pallas_call | solution.py:194
  20.1 0.2 collective-permute-done.8.r1
  20.3 1.3 %shard_map.43 = (f32[1,16]{1,0:T(1,128)S(1)}, f32[1,16]{1,0:T(1,128)S(1)}, f32[1,16]{1,0:T(1,128)S(1)}) custom-call(s32[2]{0:T(128)S(1)} %collective-permute-done.4.far_len, s32[2]{0:T(128)S(1)} %collective-permute-done.6.other_len, bf16[528,1024]{1,0:T(8,128)(2,1)S(1)} %get-tuple-element.39.tokens, bf16[256,512]{1,0:T(8,128)(2,1)S(1)} %collective-permute-done.5.r0, ...), custom_call_target="tpu_custom_call" | custom-call | tf_op jit(solution)/shard_map/pallas_call | solution.py:194
  21.6 1.6 %collective-permute-start.9 = (f32[1,16]{1,0:T(1,128)S(1)}, f32[1,16]{1,0:T(1,128)S(1)}, u32[]{:S(2)}, u32[]{:S(2)}) collective-permute-start(f32[1,16]{1,0:T(1,128)S(1)} %get-tuple-element.35), channel_id=1, source_target_pairs={{0,2},{2,0},{4,6},{6,4},{8,10},{10,8},{12,14},{14,12},{1,3},{3,1},... | collective-permute-start | bytes 200 | tf_op jit(solution)/shard_map/ppermute | solution.py:184
  23.2 2.9 %collective-permute-start.10 = (f32[1,16]{1,0:T(1,128)S(1)}, f32[1,16]{1,0:T(1,128)S(1)}, u32[]{:S(2)}, u32[]{:S(2)}) collective-permute-start(f32[1,16]{1,0:T(1,128)S(1)} %get-tuple-element.36), channel_id=1, source_target_pairs={{8,0},{10,2},{12,4},{14,6},{4,8},{6,10},{0,12},{2,14},{9,1},{11,3}... | collective-permute-start | bytes 200 | tf_op jit(solution)/shard_map/ppermute | solution.py:184
  26.1 1.5 %collective-permute-done.10.from_r = f32[1,16]{1,0:T(1,128)S(1)} collective-permute-done((f32[1,16]{1,0:T(1,128)S(1)}, f32[1,16]{1,0:T(1,128)S(1)}, u32[]{:S(2)}, u32[]{:S(2)}) %collective-permute-start.10) | collective-permute-done | bytes 96 | tf_op jit(solution)/shard_map/ppermute | solution.py:184
  27.6 0.6 %shard_map.44 = (f32[1,16]{1,0:T(1,128)}, f32[1,1]{1,0:T(1,128)}) custom-call(f32[1,16]{1,0:T(1,128)S(1)} %get-tuple-element.34.local, f32[1,16]{1,0:T(1,128)S(1)} %collective-permute-done.9.from_y, f32[1,16]{1,0:T(1,128)S(1)} %collective-permute-done.10.from_r), custom_call_target="tpu_custom_call" | custom-call | tf_op jit(solution)/shard_map/pallas_call | solution.py:194
  (5 shorter events, 0.0 us)
Async XLA Ops:
  0.6 16.5 %collective-permute-start.3 = (bf16[256,512]{1,0:T(8,128)(2,1)}, bf16[256,512]{1,0:T(8,128)(2,1)S(1)}, u32[]{:S(2)}, u32[]{:S(2)}) collective-permute-start(bf16[256,512]{1,0:T(8,128)(2,1)} %bitcast.3), channel_id=1, source_target_pairs={{0,4},{2,6},{4,0},{6,2},{8,12},{10,14},{12,8},{14,10},{1,5},{3,7},... | collective-permute-start | bytes 786440 | tf_op jit(solution)/shard_map/ppermute | solution.py:184
  3.7 14.7 %collective-permute-start.5 = (bf16[256,512]{1,0:T(8,128)(2,1)}, bf16[256,512]{1,0:T(8,128)(2,1)S(1)}, u32[]{:S(2)}, u32[]{:S(2)}) collective-permute-start(bf16[256,512]{1,0:T(8,128)(2,1)} %bitcast.4), channel_id=1, source_target_pairs={{0,8},{2,10},{4,12},{6,14},{8,4},{10,6},{12,0},{14,2},{1,9},{3,11}... | collective-permute-start | bytes 786440 | tf_op jit(solution)/shard_map/ppermute | solution.py:184
  6.3 10.8 %collective-permute-start.4 = (s32[2]{0:T(128)}, s32[2]{0:T(128)S(1)}, u32[]{:S(2)}, u32[]{:S(2)}) collective-permute-start(s32[2]{0:T(128)} %param.5), channel_id=1, source_target_pairs={{0,4},{2,6},{4,0},{6,2},{8,12},{10,14},{12,8},{14,10},{1,9},{3,11}... | collective-permute-start | bytes 32 | tf_op jit(solution)/shard_map/ppermute | solution.py:223
  7.7 7.5 %collective-permute-start.1 = (bf16[272,512]{1,0:T(8,128)(2,1)S(1)}, bf16[272,512]{1,0:T(8,128)(2,1)S(1)}, u32[]{:S(2)}, u32[]{:S(2)}) collective-permute-start(bf16[272,512]{1,0:T(8,128)(2,1)S(1)} %branch_1_fun.2.o0), channel_id=1, source_target_pairs={{0,2},{2,0},{4,6},{6,4},{8,10},{10,8},{12,14},{14,12},{1,3},{3,1},... | collective-permute-start | bytes 835592 | tf_op jit(solution)/shard_map/cond/branch_1_fun/ppermute | solution.py:184
  9.3 5.9 %collective-permute-start = (bf16[272,512]{1,0:T(8,128)(2,1)S(1)}, bf16[272,512]{1,0:T(8,128)(2,1)S(1)}, u32[]{:S(2)}, u32[]{:S(2)}) collective-permute-start(bf16[272,512]{1,0:T(8,128)(2,1)S(1)} %branch_1_fun.2.o0), channel_id=1, source_target_pairs={{0,1},{1,0},{2,3},{3,2},{4,5},{5,4},{6,7},{7,6},{8,9},{9,8},{10,11... | collective-permute-start | bytes 835592 | tf_op jit(solution)/shard_map/cond/branch_1_fun/ppermute | solution.py:187
  15.2 1.6 %collective-permute-start.2 = (bf16[272,512]{1,0:T(8,128)(2,1)S(1)}, bf16[272,512]{1,0:T(8,128)(2,1)S(1)}, u32[]{:S(2)}, u32[]{:S(2)}) collective-permute-start(bf16[272,512]{1,0:T(8,128)(2,1)S(1)} %collective-permute-done.1.y0), channel_id=1, source_target_pairs={{0,1},{1,0},{2,3},{3,2},{4,5},{5,4},{6,7},{7,6},{8,9},{9,8},{10,11... | collective-permute-start | bytes 835592 | tf_op jit(solution)/shard_map/cond/branch_1_fun/ppermute | solution.py:187
  17.1 1.6 %collective-permute-start.7 = (bf16[256,512]{1,0:T(8,128)(2,1)S(1)}, bf16[256,512]{1,0:T(8,128)(2,1)S(1)}, u32[]{:S(2)}, u32[]{:S(2)}) collective-permute-start(bf16[256,512]{1,0:T(8,128)(2,1)S(1)} %collective-permute-done.3.z0), channel_id=1, source_target_pairs={{0,1},{1,0},{2,3},{3,2},{4,5},{5,4},{6,7},{7,6},{8,9},{9,8},{10,11... | collective-permute-start | bytes 786440 | tf_op jit(solution)/shard_map/ppermute | solution.py:187
  17.3 1.4 %collective-permute-start.6 = (s32[2]{0:T(128)S(1)}, s32[2]{0:T(128)S(1)}, u32[]{:S(2)}, u32[]{:S(2)}) collective-permute-start(s32[2]{0:T(128)S(1)} %collective-permute-done.4.far_len), channel_id=1, source_target_pairs={{0,1},{1,0},{2,3},{3,2},{4,5},{5,4},{6,7},{7,6},{8,9},{9,8},{10,11... | collective-permute-start | bytes 32 | tf_op jit(solution)/shard_map/ppermute | solution.py:187
  18.7 1.5 %collective-permute-start.8 = (bf16[256,512]{1,0:T(8,128)(2,1)S(1)}, bf16[256,512]{1,0:T(8,128)(2,1)S(1)}, u32[]{:S(2)}, u32[]{:S(2)}) collective-permute-start(bf16[256,512]{1,0:T(8,128)(2,1)S(1)} %collective-permute-done.5.r0), channel_id=1, source_target_pairs={{0,1},{1,0},{2,3},{3,2},{4,5},{5,4},{6,7},{7,6},{8,9},{9,8},{10,11... | collective-permute-start | bytes 786440 | tf_op jit(solution)/shard_map/ppermute | solution.py:187
  21.6 4.5 %collective-permute-start.9 = (f32[1,16]{1,0:T(1,128)S(1)}, f32[1,16]{1,0:T(1,128)S(1)}, u32[]{:S(2)}, u32[]{:S(2)}) collective-permute-start(f32[1,16]{1,0:T(1,128)S(1)} %get-tuple-element.35), channel_id=1, source_target_pairs={{0,2},{2,0},{4,6},{6,4},{8,10},{10,8},{12,14},{14,12},{1,3},{3,1},... | collective-permute-start | bytes 200 | tf_op jit(solution)/shard_map/ppermute | solution.py:184
  23.2 4.4 %collective-permute-start.10 = (f32[1,16]{1,0:T(1,128)S(1)}, f32[1,16]{1,0:T(1,128)S(1)}, u32[]{:S(2)}, u32[]{:S(2)}) collective-permute-start(f32[1,16]{1,0:T(1,128)S(1)} %get-tuple-element.36), channel_id=1, source_target_pairs={{8,0},{10,2},{12,4},{14,6},{4,8},{6,10},{0,12},{2,14},{9,1},{11,3}... | collective-permute-start | bytes 200 | tf_op jit(solution)/shard_map/ppermute | solution.py:184

commit v6 on v5

--- a/solution.py
+++ b/solution.py
@@ -117,16 +117,18 @@
 
 def far_length(far_len, other_len, core):
     mine = lax.axis_index("width") == core
-    pair = [jnp.where(mine, far_len[v], other_len[v]).astype(jnp.float32) for v in range(2)]
-    return of_cores(pair)
-
-
-def z_kernel(half, far_len, other_len, tokens, z0, z1, local_in, local, to_y, normed):
+    pair = jnp.where(mine, far_len[...], other_len[...]).astype(jnp.float32)
+    return of_cores([pair[:, v : v + 1] for v in range(2)])
+
+
+def z_kernel(half, far_len, other_len, tokens, z0, z1, local_in, local, to_y, len_r, normed):
     slots = z0.shape[0] // 2
     _, z_chip, _ = peers(lax.axis_index("sample"), half)
     unpack(z0, z1, normed, slots, (0, slots))
     len_o, len_y = lengths_of(tokens)
     len_z = far_length(far_len, other_len, 0)
+    for v, length in enumerate(far_length(far_len, other_len, 1)):
+        len_r[v : v + 1] = jnp.broadcast_to(length, (1, len_r.shape[1]))
     similar = dot_nt(tokens[: 2 * slots], normed[...])
     for k, (length, base, out) in enumerate(((len_o, local_in, local), (len_y, None, to_y))):
         rows = similar[k * slots : (k + 1) * slots]
@@ -135,14 +137,14 @@
 
 
 def r_kernel(
-    half, far_len, other_len, tokens, r0, r1, local_in, to_y_in, local, to_y, to_r, normed
+    half, tokens, len_r, r0, r1, local_in, to_y_in, local, to_y, to_r, normed
 ):
     slots = r0.shape[0] // 2
     chip = lax.axis_index("sample")
     y_chip, _, r_chip = peers(chip, half)
     unpack(r0, r1, normed, slots, (0, slots))
     len_o, len_y = lengths_of(tokens)
-    len_r = far_length(far_len, other_len, 1)
+    len_r = [len_r[v : v + 1, :1] for v in range(2)]
     similar = dot_nt(tokens[: 2 * slots], normed[...])
     own = []
     for k, (length, base, out) in enumerate(((len_o, local_in, local), (len_y, to_y_in, to_y))):
@@ -220,7 +222,7 @@
         return jax.tree.map(lambda x: jnp.zeros(x.shape, x.dtype), jax.eval_shape(near))
 
     far_route = [(2 * a, 2 * b) for a, b in z_route] + [(2 * a + 1, 2 * b + 1) for a, b in r_route]
-    far_len = lax.ppermute(lengths, ("sample", "width"), far_route)
+    far_len = lax.ppermute(lengths.reshape(1, 2), ("sample", "width"), far_route)
     block = embeddings.reshape(2 * slots, feat)
     z = send(block, z_route)
     r = send(block, r_route)
@@ -230,19 +232,17 @@
     (local,) = call(functools.partial(pairs_kernel, half), (tokens,), (row,))
     r, far_other, z_other, local = lax.optimization_barrier((r, far_other, z_other, local))
     scratch = [pltpu.VMEM((2 * slots, 2 * feat), jnp.bfloat16)]
-    local, to_y = call(
+    local, to_y, len_r = call(
         functools.partial(z_kernel, half),
         (far_len, far_other, tokens, z, z_other, local),
-        (row, row),
+        (row, row, jax.ShapeDtypeStruct((2, 128), jnp.float32)),
         scratch,
-        [SMEM] * 2 + [VMEM] * 4,
     )
     local, to_y, to_r = call(
         functools.partial(r_kernel, half),
-        (far_len, far_other, tokens, r, other(r), local, to_y),
+        (tokens, len_r, r, other(r), local, to_y),
         (row, row, row),
         scratch,
-        [SMEM] * 2 + [VMEM] * 5,
     )
     one = jax.ShapeDtypeStruct((1, 1), jnp.float32)
     from_r, from_y = send(to_r, back_route), send(to_y, y_route)

time: 28.3 us -> 27.8 us (0.982)
  Pallas kernels: 5.06 us -> 4.05 us
  waiting for transfers between devices: 9.58 us -> 10.1 us
    pallas_call x6, Pallas kernels: 5.06 us -> 4.05 us  [call(): pl.pallas_call(kernel, out_shape=outs, in_specs=[pl.BlockSpec(memory_spac...]
    ppermute x5, waiting for transfers between devices: 2.13 us -> 2.6 us  [other(): return lax.ppermute(x, 'width', swap)]
  transfers between devices with their start and end apart: 11 -> 11, of which waited for: 5 -> 5; matrix products, arithmetic and copies ran while one was open for 0% -> 0% of each run, Pallas kernels for 11% -> 10%
where the time goes in v6:
time: 27.8 us; the launch traced here: 27.7 us
  starting transfers between devices  12.9 us (46%)
  waiting for transfers between devices  10.1 us (36%)
  Pallas kernels  4.05 us (15%)
  between operations  0.66 us (2%)
    ppermute x5, starting transfers between devices, send(): return lax.ppermute(x, 'sample', route)  11.7 us
    ppermute x5, waiting for transfers between devices, send(): return lax.ppermute(x, 'sample', route)  7.46 us
    pallas_call x6, Pallas kernels, call(): pl.pallas_call(kernel, out_shape=outs, in_specs=[pl.BlockSpec(memory_spac...  4.05 us
    ppermute x5, waiting for transfers between devices, other(): return lax.ppermute(x, 'width', swap)  2.6 us
    ppermute x5, starting transfers between devices, other(): return lax.ppermute(x, 'width', swap)  0.72 us
  transfers between devices with their start and end apart: 11, of which 5 were waited for; matrix products, arithmetic and copies ran while one was open for 0% of the time, Pallas kernels for 10%

profile of v6, /device:TPU:0, one launch (start us, length us, event | category | flops | bytes accessed | tf_op | source)
XLA Modules:
  0.0 27.7 jit_solution(2422307591827697853)
XLA Ops:
  0.6 3.1 %collective-permute-start.3 = (bf16[256,512]{1,0:T(8,128)(2,1)}, bf16[256,512]{1,0:T(8,128)(2,1)S(1)}, u32[]{:S(2)}, u32[]{:S(2)}) collective-permute-start(bf16[256,512]{1,0:T(8,128)(2,1)} %bitcast.4), channel_id=1, source_target_pairs={{0,4},{2,6},{4,0},{6,2},{8,12},{10,14},{12,8},{14,10},{1,5},{3,7},... | collective-permute-start | bytes 786440 | tf_op jit(solution)/shard_map/ppermute | solution.py:186
  3.7 2.6 %collective-permute-start.5 = (bf16[256,512]{1,0:T(8,128)(2,1)}, bf16[256,512]{1,0:T(8,128)(2,1)S(1)}, u32[]{:S(2)}, u32[]{:S(2)}) collective-permute-start(bf16[256,512]{1,0:T(8,128)(2,1)} %bitcast.5), channel_id=1, source_target_pairs={{0,8},{2,10},{4,12},{6,14},{8,4},{10,6},{12,0},{14,2},{1,9},{3,11}... | collective-permute-start | bytes 786440 | tf_op jit(solution)/shard_map/ppermute | solution.py:186
  6.3 0.4 %collective-permute-start.4 = (s32[1,2]{1,0:T(1,128)}, s32[1,2]{1,0:T(1,128)S(1)}, u32[]{:S(2)}, u32[]{:S(2)}) collective-permute-start(s32[1,2]{1,0:T(1,128)} %bitcast.7), channel_id=1, source_target_pairs={{0,4},{2,6},{4,0},{6,2},{8,12},{10,14},{12,8},{14,10},{1,9},{3,11}... | collective-permute-start | bytes 32 | tf_op jit(solution)/shard_map/ppermute | solution.py:225
  6.8 10.4 %conditional.1 = (bf16[528,1024]{1,0:T(8,128)(2,1)S(1)}) conditional(s32[]{:T(128)} %convert_element_type.3, () %tuple.16, (bf16[2,128,512]{2,1,0:T(8,128)(2,1)}, s32[2]{0:T(128)}) %tuple.17), branch_computations={%region_0.0_spmd, %region_1.0_spmd} | conditional | bytes 3342464 | solution.py:229
  6.8 1.0 %branch_1_fun.2.o0 = bf16[272,512]{1,0:T(8,128)(2,1)S(1)} custom-call(s32[2]{0:T(128)} %get-tuple-element.4.lengths, bf16[256,512]{1,0:T(8,128)(2,1)} %bitcast.6), custom_call_target="tpu_custom_call" | custom-call | tf_op jit(solution)/shard_map/cond/branch_1_fun/pallas_call | solution.py:196
  7.7 1.6 %collective-permute-start.1 = (bf16[272,512]{1,0:T(8,128)(2,1)S(1)}, bf16[272,512]{1,0:T(8,128)(2,1)S(1)}, u32[]{:S(2)}, u32[]{:S(2)}) collective-permute-start(bf16[272,512]{1,0:T(8,128)(2,1)S(1)} %branch_1_fun.2.o0), channel_id=1, source_target_pairs={{0,2},{2,0},{4,6},{6,4},{8,10},{10,8},{12,14},{14,12},{1,3},{3,1},... | collective-permute-start | bytes 835592 | tf_op jit(solution)/shard_map/cond/branch_1_fun/ppermute | solution.py:186
  9.3 5.9 %collective-permute-done.1.y0 = bf16[272,512]{1,0:T(8,128)(2,1)S(1)} collective-permute-done((bf16[272,512]{1,0:T(8,128)(2,1)S(1)}, bf16[272,512]{1,0:T(8,128)(2,1)S(1)}, u32[]{:S(2)}, u32[]{:S(2)}) %collective-permute-start.1) | collective-permute-done | bytes 278560 | tf_op jit(solution)/shard_map/cond/branch_1_fun/ppermute | solution.py:186
  15.2 0.0 collective-permute-start.2
  15.2 0.0 collective-permute-done.o1
  15.2 1.6 %collective-permute-done.2.y1 = bf16[272,512]{1,0:T(8,128)(2,1)S(1)} collective-permute-done((bf16[272,512]{1,0:T(8,128)(2,1)S(1)}, bf16[272,512]{1,0:T(8,128)(2,1)S(1)}, u32[]{:S(2)}, u32[]{:S(2)}) %collective-permute-start.2) | collective-permute-done | bytes 278560 | tf_op jit(solution)/shard_map/cond/branch_1_fun/ppermute | solution.py:189
  16.8 0.3 %branch_1_fun.3 = bf16[528,1024]{1,0:T(8,128)(2,1)S(1)} custom-call(bf16[272,512]{1,0:T(8,128)(2,1)S(1)} %branch_1_fun.2.o0, bf16[272,512]{1,0:T(8,128)(2,1)S(1)} %collective-permute-done.o1, bf16[272,512]{1,0:T(8,128)(2,1)S(1)} %collective-permute-done.1.y0, bf16[272,512]{1,0:T(8,128)(2,1)S(1)} %collective-permute-done.2.y1), custom_call_target="tpu_custom_call" | custom-call | tf_op jit(solution)/shard_map/cond/branch_1_fun/pallas_call | solution.py:196
  17.1 0.0 collective-permute-done.4.far_len
  17.1 0.2 collective-permute-start.7
  17.3 0.4 %collective-permute-start.6 = (s32[1,2]{1,0:T(1,128)S(1)}, s32[1,2]{1,0:T(1,128)S(1)}, u32[]{:S(2)}, u32[]{:S(2)}) collective-permute-start(s32[1,2]{1,0:T(1,128)S(1)} %collective-permute-done.4.far_len), channel_id=1, source_target_pairs={{0,1},{1,0},{2,3},{3,2},{4,5},{5,4},{6,7},{7,6},{8,9},{9,8},{10,11... | collective-permute-start | bytes 32 | tf_op jit(solution)/shard_map/ppermute | solution.py:189
  17.7 0.7 %shard_map.41.local_in = f32[1,16]{1,0:T(1,128)S(1)} custom-call(bf16[528,1024]{1,0:T(8,128)(2,1)S(1)} %get-tuple-element.41.tokens), custom_call_target="tpu_custom_call" | custom-call | tf_op jit(solution)/shard_map/pallas_call | solution.py:196
  18.4 0.3 %collective-permute-done.6.other_len = s32[1,2]{1,0:T(1,128)S(1)} collective-permute-done((s32[1,2]{1,0:T(1,128)S(1)}, s32[1,2]{1,0:T(1,128)S(1)}, u32[]{:S(2)}, u32[]{:S(2)}) %collective-permute-start.6) | collective-permute-done | bytes 40 | tf_op jit(solution)/shard_map/ppermute | solution.py:189
  18.7 0.1 collective-permute-start.8
  18.9 0.7 %shard_map.42 = (f32[1,16]{1,0:T(1,128)S(1)}, f32[1,16]{1,0:T(1,128)S(1)}, f32[2,128]{1,0:T(2,128)S(1)}) custom-call(s32[1,2]{1,0:T(1,128)S(1)} %collective-permute-done.4.far_len, s32[1,2]{1,0:T(1,128)S(1)} %collective-permute-done.6.other_len, bf16[528,1024]{1,0:T(8,128)(2,1)S(1)} %get-tuple-element.41.tokens, ...), custom_call_target="tpu_custom_call" | custom-call | tf_op jit(solution)/shard_map/pallas_call | solution.py:196
  19.6 0.7 %collective-permute-done.8.r1 = bf16[256,512]{1,0:T(8,128)(2,1)S(1)} collective-permute-done((bf16[256,512]{1,0:T(8,128)(2,1)S(1)}, bf16[256,512]{1,0:T(8,128)(2,1)S(1)}, u32[]{:S(2)}, u32[]{:S(2)}) %collective-permute-start.8) | collective-permute-done | bytes 262176 | tf_op jit(solution)/shard_map/ppermute | solution.py:189
  20.3 0.8 %shard_map.43 = (f32[1,16]{1,0:T(1,128)S(1)}, f32[1,16]{1,0:T(1,128)S(1)}, f32[1,16]{1,0:T(1,128)S(1)}) custom-call(bf16[528,1024]{1,0:T(8,128)(2,1)S(1)} %get-tuple-element.41.tokens, f32[2,128]{1,0:T(2,128)S(1)} %get-tuple-element.32.len_r, bf16[256,512]{1,0:T(8,128)(2,1)S(1)} %collective-permute-done.5.r0, ...), custom_call_target="tpu_custom_call" | custom-call | tf_op jit(solution)/shard_map/pallas_call | solution.py:196
  21.1 1.6 %collective-permute-start.9 = (f32[1,16]{1,0:T(1,128)S(1)}, f32[1,16]{1,0:T(1,128)S(1)}, u32[]{:S(2)}, u32[]{:S(2)}) collective-permute-start(f32[1,16]{1,0:T(1,128)S(1)} %get-tuple-element.37), channel_id=1, source_target_pairs={{0,2},{2,0},{4,6},{6,4},{8,10},{10,8},{12,14},{14,12},{1,3},{3,1},... | collective-permute-start | bytes 200 | tf_op jit(solution)/shard_map/ppermute | solution.py:186
  22.6 2.9 %collective-permute-start.10 = (f32[1,16]{1,0:T(1,128)S(1)}, f32[1,16]{1,0:T(1,128)S(1)}, u32[]{:S(2)}, u32[]{:S(2)}) collective-permute-start(f32[1,16]{1,0:T(1,128)S(1)} %get-tuple-element.38), channel_id=1, source_target_pairs={{8,0},{10,2},{12,4},{14,6},{4,8},{6,10},{0,12},{2,14},{9,1},{11,3}... | collective-permute-start | bytes 200 | tf_op jit(solution)/shard_map/ppermute | solution.py:186
  25.5 1.6 %collective-permute-done.10.from_r = f32[1,16]{1,0:T(1,128)S(1)} collective-permute-done((f32[1,16]{1,0:T(1,128)S(1)}, f32[1,16]{1,0:T(1,128)S(1)}, u32[]{:S(2)}, u32[]{:S(2)}) %collective-permute-start.10) | collective-permute-done | bytes 96 | tf_op jit(solution)/shard_map/ppermute | solution.py:186
  27.1 0.6 %shard_map.44 = (f32[1,16]{1,0:T(1,128)}, f32[1,1]{1,0:T(1,128)}) custom-call(f32[1,16]{1,0:T(1,128)S(1)} %get-tuple-element.36.local, f32[1,16]{1,0:T(1,128)S(1)} %collective-permute-done.9.from_y, f32[1,16]{1,0:T(1,128)S(1)} %collective-permute-done.10.from_r), custom_call_target="tpu_custom_call" | custom-call | tf_op jit(solution)/shard_map/pallas_call | solution.py:196
  (5 shorter events, 0.0 us)
Async XLA Ops:
  0.6 16.5 %collective-permute-start.3 = (bf16[256,512]{1,0:T(8,128)(2,1)}, bf16[256,512]{1,0:T(8,128)(2,1)S(1)}, u32[]{:S(2)}, u32[]{:S(2)}) collective-permute-start(bf16[256,512]{1,0:T(8,128)(2,1)} %bitcast.4), channel_id=1, source_target_pairs={{0,4},{2,6},{4,0},{6,2},{8,12},{10,14},{12,8},{14,10},{1,5},{3,7},... | collective-permute-start | bytes 786440 | tf_op jit(solution)/shard_map/ppermute | solution.py:186
  3.7 14.7 %collective-permute-start.5 = (bf16[256,512]{1,0:T(8,128)(2,1)}, bf16[256,512]{1,0:T(8,128)(2,1)S(1)}, u32[]{:S(2)}, u32[]{:S(2)}) collective-permute-start(bf16[256,512]{1,0:T(8,128)(2,1)} %bitcast.5), channel_id=1, source_target_pairs={{0,8},{2,10},{4,12},{6,14},{8,4},{10,6},{12,0},{14,2},{1,9},{3,11}... | collective-permute-start | bytes 786440 | tf_op jit(solution)/shard_map/ppermute | solution.py:186
  6.3 10.8 %collective-permute-start.4 = (s32[1,2]{1,0:T(1,128)}, s32[1,2]{1,0:T(1,128)S(1)}, u32[]{:S(2)}, u32[]{:S(2)}) collective-permute-start(s32[1,2]{1,0:T(1,128)} %bitcast.7), channel_id=1, source_target_pairs={{0,4},{2,6},{4,0},{6,2},{8,12},{10,14},{12,8},{14,10},{1,9},{3,11}... | collective-permute-start | bytes 32 | tf_op jit(solution)/shard_map/ppermute | solution.py:225
  7.7 7.5 %collective-permute-start.1 = (bf16[272,512]{1,0:T(8,128)(2,1)S(1)}, bf16[272,512]{1,0:T(8,128)(2,1)S(1)}, u32[]{:S(2)}, u32[]{:S(2)}) collective-permute-start(bf16[272,512]{1,0:T(8,128)(2,1)S(1)} %branch_1_fun.2.o0), channel_id=1, source_target_pairs={{0,2},{2,0},{4,6},{6,4},{8,10},{10,8},{12,14},{14,12},{1,3},{3,1},... | collective-permute-start | bytes 835592 | tf_op jit(solution)/shard_map/cond/branch_1_fun/ppermute | solution.py:186
  9.3 5.9 %collective-permute-start = (bf16[272,512]{1,0:T(8,128)(2,1)S(1)}, bf16[272,512]{1,0:T(8,128)(2,1)S(1)}, u32[]{:S(2)}, u32[]{:S(2)}) collective-permute-start(bf16[272,512]{1,0:T(8,128)(2,1)S(1)} %branch_1_fun.2.o0), channel_id=1, source_target_pairs={{0,1},{1,0},{2,3},{3,2},{4,5},{5,4},{6,7},{7,6},{8,9},{9,8},{10,11... | collective-permute-start | bytes 835592 | tf_op jit(solution)/shard_map/cond/branch_1_fun/ppermute | solution.py:189
  15.2 1.6 %collective-permute-start.2 = (bf16[272,512]{1,0:T(8,128)(2,1)S(1)}, bf16[272,512]{1,0:T(8,128)(2,1)S(1)}, u32[]{:S(2)}, u32[]{:S(2)}) collective-permute-start(bf16[272,512]{1,0:T(8,128)(2,1)S(1)} %collective-permute-done.1.y0), channel_id=1, source_target_pairs={{0,1},{1,0},{2,3},{3,2},{4,5},{5,4},{6,7},{7,6},{8,9},{9,8},{10,11... | collective-permute-start | bytes 835592 | tf_op jit(solution)/shard_map/cond/branch_1_fun/ppermute | solution.py:189
  17.1 1.6 %collective-permute-start.7 = (bf16[256,512]{1,0:T(8,128)(2,1)S(1)}, bf16[256,512]{1,0:T(8,128)(2,1)S(1)}, u32[]{:S(2)}, u32[]{:S(2)}) collective-permute-start(bf16[256,512]{1,0:T(8,128)(2,1)S(1)} %collective-permute-done.3.z0), channel_id=1, source_target_pairs={{0,1},{1,0},{2,3},{3,2},{4,5},{5,4},{6,7},{7,6},{8,9},{9,8},{10,11... | collective-permute-start | bytes 786440 | tf_op jit(solution)/shard_map/ppermute | solution.py:189
  17.3 1.4 %collective-permute-start.6 = (s32[1,2]{1,0:T(1,128)S(1)}, s32[1,2]{1,0:T(1,128)S(1)}, u32[]{:S(2)}, u32[]{:S(2)}) collective-permute-start(s32[1,2]{1,0:T(1,128)S(1)} %collective-permute-done.4.far_len), channel_id=1, source_target_pairs={{0,1},{1,0},{2,3},{3,2},{4,5},{5,4},{6,7},{7,6},{8,9},{9,8},{10,11... | collective-permute-start | bytes 32 | tf_op jit(solution)/shard_map/ppermute | solution.py:189
  18.7 1.5 %collective-permute-start.8 = (bf16[256,512]{1,0:T(8,128)(2,1)S(1)}, bf16[256,512]{1,0:T(8,128)(2,1)S(1)}, u32[]{:S(2)}, u32[]{:S(2)}) collective-permute-start(bf16[256,512]{1,0:T(8,128)(2,1)S(1)} %collective-permute-done.5.r0), channel_id=1, source_target_pairs={{0,1},{1,0},{2,3},{3,2},{4,5},{5,4},{6,7},{7,6},{8,9},{9,8},{10,11... | collective-permute-start | bytes 786440 | tf_op jit(solution)/shard_map/ppermute | solution.py:189
  21.1 4.4 %collective-permute-start.9 = (f32[1,16]{1,0:T(1,128)S(1)}, f32[1,16]{1,0:T(1,128)S(1)}, u32[]{:S(2)}, u32[]{:S(2)}) collective-permute-start(f32[1,16]{1,0:T(1,128)S(1)} %get-tuple-element.37), channel_id=1, source_target_pairs={{0,2},{2,0},{4,6},{6,4},{8,10},{10,8},{12,14},{14,12},{1,3},{3,1},... | collective-permute-start | bytes 200 | tf_op jit(solution)/shard_map/ppermute | solution.py:186
  22.6 4.4 %collective-permute-start.10 = (f32[1,16]{1,0:T(1,128)S(1)}, f32[1,16]{1,0:T(1,128)S(1)}, u32[]{:S(2)}, u32[]{:S(2)}) collective-permute-start(f32[1,16]{1,0:T(1,128)S(1)} %get-tuple-element.38), channel_id=1, source_target_pairs={{8,0},{10,2},{12,4},{14,6},{4,8},{6,10},{0,12},{2,14},{9,1},{11,3}... | collective-permute-start | bytes 200 | tf_op jit(solution)/shard_map/ppermute | solution.py:186

commit v7 on v6

--- a/solution.py
+++ b/solution.py
@@ -224,8 +224,8 @@
     far_route = [(2 * a, 2 * b) for a, b in z_route] + [(2 * a + 1, 2 * b + 1) for a, b in r_route]
     far_len = lax.ppermute(lengths.reshape(1, 2), ("sample", "width"), far_route)
     block = embeddings.reshape(2 * slots, feat)
+    r = send(block, r_route)
     z = send(block, z_route)
-    r = send(block, r_route)
     tokens = lax.cond(lax.axis_index("sample") >= 0, near, nothing)
     tokens, z, far_len = lax.optimization_barrier((tokens, z, far_len))
     z_other, far_other = other(z), other(far_len)
@@ -245,7 +245,7 @@
         scratch,
     )
     one = jax.ShapeDtypeStruct((1, 1), jnp.float32)
-    from_r, from_y = send(to_r, back_route), send(to_y, y_route)
+    from_y, from_r = send(to_y, y_route), send(to_r, back_route)
     scores, utility = call(final_kernel, (local, from_y, from_r), (row, one))
     return scores, utility.reshape(1)
 

time: 27.8 us -> 27.8 us (level)
  no operation moved by 1% of the time
where the time goes in v7:
time: 27.8 us; the launch traced here: 27.7 us
  starting transfers between devices  12.9 us (46%)
  waiting for transfers between devices  10.1 us (36%)
  Pallas kernels  4.05 us (15%)
  between operations  0.66 us (2%)
    ppermute x5, starting transfers between devices, send(): return lax.ppermute(x, 'sample', route)  11.7 us
    ppermute x5, waiting for transfers between devices, send(): return lax.ppermute(x, 'sample', route)  7.46 us
    pallas_call x6, Pallas kernels, call(): pl.pallas_call(kernel, out_shape=outs, in_specs=[pl.BlockSpec(memory_spac...  4.05 us
    ppermute x5, waiting for transfers between devices, other(): return lax.ppermute(x, 'width', swap)  2.6 us
    ppermute x5, starting transfers between devices, other(): return lax.ppermute(x, 'width', swap)  0.72 us
  transfers between devices with their start and end apart: 11, of which 5 were waited for; matrix products, arithmetic and copies ran while one was open for 0% of the time, Pallas kernels for 10%

profile of v7, /device:TPU:0, one launch (start us, length us, event | category | flops | bytes accessed | tf_op | source)
XLA Modules:
  0.0 27.7 jit_solution(2422307591827697853)
XLA Ops:
  0.6 3.1 %collective-permute-start.3 = (bf16[256,512]{1,0:T(8,128)(2,1)}, bf16[256,512]{1,0:T(8,128)(2,1)S(1)}, u32[]{:S(2)}, u32[]{:S(2)}) collective-permute-start(bf16[256,512]{1,0:T(8,128)(2,1)} %bitcast.4), channel_id=1, source_target_pairs={{0,4},{2,6},{4,0},{6,2},{8,12},{10,14},{12,8},{14,10},{1,5},{3,7},... | collective-permute-start | bytes 786440 | tf_op jit(solution)/shard_map/ppermute | solution.py:186
  3.7 2.6 %collective-permute-start.5 = (bf16[256,512]{1,0:T(8,128)(2,1)}, bf16[256,512]{1,0:T(8,128)(2,1)S(1)}, u32[]{:S(2)}, u32[]{:S(2)}) collective-permute-start(bf16[256,512]{1,0:T(8,128)(2,1)} %bitcast.5), channel_id=1, source_target_pairs={{0,8},{2,10},{4,12},{6,14},{8,4},{10,6},{12,0},{14,2},{1,9},{3,11}... | collective-permute-start | bytes 786440 | tf_op jit(solution)/shard_map/ppermute | solution.py:186
  6.3 0.4 %collective-permute-start.4 = (s32[1,2]{1,0:T(1,128)}, s32[1,2]{1,0:T(1,128)S(1)}, u32[]{:S(2)}, u32[]{:S(2)}) collective-permute-start(s32[1,2]{1,0:T(1,128)} %bitcast.7), channel_id=1, source_target_pairs={{0,4},{2,6},{4,0},{6,2},{8,12},{10,14},{12,8},{14,10},{1,9},{3,11}... | collective-permute-start | bytes 32 | tf_op jit(solution)/shard_map/ppermute | solution.py:225
  6.8 10.4 %conditional.1 = (bf16[528,1024]{1,0:T(8,128)(2,1)S(1)}) conditional(s32[]{:T(128)} %convert_element_type.3, () %tuple.16, (bf16[2,128,512]{2,1,0:T(8,128)(2,1)}, s32[2]{0:T(128)}) %tuple.17), branch_computations={%region_0.0_spmd, %region_1.0_spmd} | conditional | bytes 3342464 | solution.py:229
  6.8 1.0 %branch_1_fun.2.o0 = bf16[272,512]{1,0:T(8,128)(2,1)S(1)} custom-call(s32[2]{0:T(128)} %get-tuple-element.4.lengths, bf16[256,512]{1,0:T(8,128)(2,1)} %bitcast.6), custom_call_target="tpu_custom_call" | custom-call | tf_op jit(solution)/shard_map/cond/branch_1_fun/pallas_call | solution.py:196
  7.7 1.6 %collective-permute-start.1 = (bf16[272,512]{1,0:T(8,128)(2,1)S(1)}, bf16[272,512]{1,0:T(8,128)(2,1)S(1)}, u32[]{:S(2)}, u32[]{:S(2)}) collective-permute-start(bf16[272,512]{1,0:T(8,128)(2,1)S(1)} %branch_1_fun.2.o0), channel_id=1, source_target_pairs={{0,2},{2,0},{4,6},{6,4},{8,10},{10,8},{12,14},{14,12},{1,3},{3,1},... | collective-permute-start | bytes 835592 | tf_op jit(solution)/shard_map/cond/branch_1_fun/ppermute | solution.py:186
  9.3 5.9 %collective-permute-done.1.y0 = bf16[272,512]{1,0:T(8,128)(2,1)S(1)} collective-permute-done((bf16[272,512]{1,0:T(8,128)(2,1)S(1)}, bf16[272,512]{1,0:T(8,128)(2,1)S(1)}, u32[]{:S(2)}, u32[]{:S(2)}) %collective-permute-start.1) | collective-permute-done | bytes 278560 | tf_op jit(solution)/shard_map/cond/branch_1_fun/ppermute | solution.py:186
  15.2 0.0 collective-permute-start.2
  15.2 0.0 collective-permute-done.o1
  15.2 1.6 %collective-permute-done.2.y1 = bf16[272,512]{1,0:T(8,128)(2,1)S(1)} collective-permute-done((bf16[272,512]{1,0:T(8,128)(2,1)S(1)}, bf16[272,512]{1,0:T(8,128)(2,1)S(1)}, u32[]{:S(2)}, u32[]{:S(2)}) %collective-permute-start.2) | collective-permute-done | bytes 278560 | tf_op jit(solution)/shard_map/cond/branch_1_fun/ppermute | solution.py:189
  16.8 0.3 %branch_1_fun.3 = bf16[528,1024]{1,0:T(8,128)(2,1)S(1)} custom-call(bf16[272,512]{1,0:T(8,128)(2,1)S(1)} %branch_1_fun.2.o0, bf16[272,512]{1,0:T(8,128)(2,1)S(1)} %collective-permute-done.o1, bf16[272,512]{1,0:T(8,128)(2,1)S(1)} %collective-permute-done.1.y0, bf16[272,512]{1,0:T(8,128)(2,1)S(1)} %collective-permute-done.2.y1), custom_call_target="tpu_custom_call" | custom-call | tf_op jit(solution)/shard_map/cond/branch_1_fun/pallas_call | solution.py:196
  17.1 0.0 collective-permute-done.4.far_len
  17.1 0.2 collective-permute-start.7
  17.3 0.4 %collective-permute-start.6 = (s32[1,2]{1,0:T(1,128)S(1)}, s32[1,2]{1,0:T(1,128)S(1)}, u32[]{:S(2)}, u32[]{:S(2)}) collective-permute-start(s32[1,2]{1,0:T(1,128)S(1)} %collective-permute-done.4.far_len), channel_id=1, source_target_pairs={{0,1},{1,0},{2,3},{3,2},{4,5},{5,4},{6,7},{7,6},{8,9},{9,8},{10,11... | collective-permute-start | bytes 32 | tf_op jit(solution)/shard_map/ppermute | solution.py:189
  17.7 0.7 %shard_map.41.local_in = f32[1,16]{1,0:T(1,128)S(1)} custom-call(bf16[528,1024]{1,0:T(8,128)(2,1)S(1)} %get-tuple-element.41.tokens), custom_call_target="tpu_custom_call" | custom-call | tf_op jit(solution)/shard_map/pallas_call | solution.py:196
  18.4 0.3 %collective-permute-done.6.other_len = s32[1,2]{1,0:T(1,128)S(1)} collective-permute-done((s32[1,2]{1,0:T(1,128)S(1)}, s32[1,2]{1,0:T(1,128)S(1)}, u32[]{:S(2)}, u32[]{:S(2)}) %collective-permute-start.6) | collective-permute-done | bytes 40 | tf_op jit(solution)/shard_map/ppermute | solution.py:189
  18.7 0.1 collective-permute-start.8
  18.9 0.7 %shard_map.42 = (f32[1,16]{1,0:T(1,128)S(1)}, f32[1,16]{1,0:T(1,128)S(1)}, f32[2,128]{1,0:T(2,128)S(1)}) custom-call(s32[1,2]{1,0:T(1,128)S(1)} %collective-permute-done.4.far_len, s32[1,2]{1,0:T(1,128)S(1)} %collective-permute-done.6.other_len, bf16[528,1024]{1,0:T(8,128)(2,1)S(1)} %get-tuple-element.41.tokens, ...), custom_call_target="tpu_custom_call" | custom-call | tf_op jit(solution)/shard_map/pallas_call | solution.py:196
  19.6 0.7 %collective-permute-done.8.r1 = bf16[256,512]{1,0:T(8,128)(2,1)S(1)} collective-permute-done((bf16[256,512]{1,0:T(8,128)(2,1)S(1)}, bf16[256,512]{1,0:T(8,128)(2,1)S(1)}, u32[]{:S(2)}, u32[]{:S(2)}) %collective-permute-start.8) | collective-permute-done | bytes 262176 | tf_op jit(solution)/shard_map/ppermute | solution.py:189
  20.3 0.8 %shard_map.43 = (f32[1,16]{1,0:T(1,128)S(1)}, f32[1,16]{1,0:T(1,128)S(1)}, f32[1,16]{1,0:T(1,128)S(1)}) custom-call(bf16[528,1024]{1,0:T(8,128)(2,1)S(1)} %get-tuple-element.41.tokens, f32[2,128]{1,0:T(2,128)S(1)} %get-tuple-element.32.len_r, bf16[256,512]{1,0:T(8,128)(2,1)S(1)} %collective-permute-done.5.r0, ...), custom_call_target="tpu_custom_call" | custom-call | tf_op jit(solution)/shard_map/pallas_call | solution.py:196
  21.1 1.6 %collective-permute-start.9 = (f32[1,16]{1,0:T(1,128)S(1)}, f32[1,16]{1,0:T(1,128)S(1)}, u32[]{:S(2)}, u32[]{:S(2)}) collective-permute-start(f32[1,16]{1,0:T(1,128)S(1)} %get-tuple-element.37), channel_id=1, source_target_pairs={{0,2},{2,0},{4,6},{6,4},{8,10},{10,8},{12,14},{14,12},{1,3},{3,1},... | collective-permute-start | bytes 200 | tf_op jit(solution)/shard_map/ppermute | solution.py:186
  22.6 2.9 %collective-permute-start.10 = (f32[1,16]{1,0:T(1,128)S(1)}, f32[1,16]{1,0:T(1,128)S(1)}, u32[]{:S(2)}, u32[]{:S(2)}) collective-permute-start(f32[1,16]{1,0:T(1,128)S(1)} %get-tuple-element.38), channel_id=1, source_target_pairs={{8,0},{10,2},{12,4},{14,6},{4,8},{6,10},{0,12},{2,14},{9,1},{11,3}... | collective-permute-start | bytes 200 | tf_op jit(solution)/shard_map/ppermute | solution.py:186
  25.5 1.6 %collective-permute-done.10.from_r = f32[1,16]{1,0:T(1,128)S(1)} collective-permute-done((f32[1,16]{1,0:T(1,128)S(1)}, f32[1,16]{1,0:T(1,128)S(1)}, u32[]{:S(2)}, u32[]{:S(2)}) %collective-permute-start.10) | collective-permute-done | bytes 96 | tf_op jit(solution)/shard_map/ppermute | solution.py:186
  27.1 0.6 %shard_map.44 = (f32[1,16]{1,0:T(1,128)}, f32[1,1]{1,0:T(1,128)}) custom-call(f32[1,16]{1,0:T(1,128)S(1)} %get-tuple-element.36.local, f32[1,16]{1,0:T(1,128)S(1)} %collective-permute-done.9.from_y, f32[1,16]{1,0:T(1,128)S(1)} %collective-permute-done.10.from_r), custom_call_target="tpu_custom_call" | custom-call | tf_op jit(solution)/shard_map/pallas_call | solution.py:196
  (5 shorter events, 0.0 us)
Async XLA Ops:
  0.6 16.5 %collective-permute-start.3 = (bf16[256,512]{1,0:T(8,128)(2,1)}, bf16[256,512]{1,0:T(8,128)(2,1)S(1)}, u32[]{:S(2)}, u32[]{:S(2)}) collective-permute-start(bf16[256,512]{1,0:T(8,128)(2,1)} %bitcast.4), channel_id=1, source_target_pairs={{0,4},{2,6},{4,0},{6,2},{8,12},{10,14},{12,8},{14,10},{1,5},{3,7},... | collective-permute-start | bytes 786440 | tf_op jit(solution)/shard_map/ppermute | solution.py:186
  3.7 14.7 %collective-permute-start.5 = (bf16[256,512]{1,0:T(8,128)(2,1)}, bf16[256,512]{1,0:T(8,128)(2,1)S(1)}, u32[]{:S(2)}, u32[]{:S(2)}) collective-permute-start(bf16[256,512]{1,0:T(8,128)(2,1)} %bitcast.5), channel_id=1, source_target_pairs={{0,8},{2,10},{4,12},{6,14},{8,4},{10,6},{12,0},{14,2},{1,9},{3,11}... | collective-permute-start | bytes 786440 | tf_op jit(solution)/shard_map/ppermute | solution.py:186
  6.3 10.8 %collective-permute-start.4 = (s32[1,2]{1,0:T(1,128)}, s32[1,2]{1,0:T(1,128)S(1)}, u32[]{:S(2)}, u32[]{:S(2)}) collective-permute-start(s32[1,2]{1,0:T(1,128)} %bitcast.7), channel_id=1, source_target_pairs={{0,4},{2,6},{4,0},{6,2},{8,12},{10,14},{12,8},{14,10},{1,9},{3,11}... | collective-permute-start | bytes 32 | tf_op jit(solution)/shard_map/ppermute | solution.py:225
  7.7 7.5 %collective-permute-start.1 = (bf16[272,512]{1,0:T(8,128)(2,1)S(1)}, bf16[272,512]{1,0:T(8,128)(2,1)S(1)}, u32[]{:S(2)}, u32[]{:S(2)}) collective-permute-start(bf16[272,512]{1,0:T(8,128)(2,1)S(1)} %branch_1_fun.2.o0), channel_id=1, source_target_pairs={{0,2},{2,0},{4,6},{6,4},{8,10},{10,8},{12,14},{14,12},{1,3},{3,1},... | collective-permute-start | bytes 835592 | tf_op jit(solution)/shard_map/cond/branch_1_fun/ppermute | solution.py:186
  9.3 5.9 %collective-permute-start = (bf16[272,512]{1,0:T(8,128)(2,1)S(1)}, bf16[272,512]{1,0:T(8,128)(2,1)S(1)}, u32[]{:S(2)}, u32[]{:S(2)}) collective-permute-start(bf16[272,512]{1,0:T(8,128)(2,1)S(1)} %branch_1_fun.2.o0), channel_id=1, source_target_pairs={{0,1},{1,0},{2,3},{3,2},{4,5},{5,4},{6,7},{7,6},{8,9},{9,8},{10,11... | collective-permute-start | bytes 835592 | tf_op jit(solution)/shard_map/cond/branch_1_fun/ppermute | solution.py:189
  15.2 1.6 %collective-permute-start.2 = (bf16[272,512]{1,0:T(8,128)(2,1)S(1)}, bf16[272,512]{1,0:T(8,128)(2,1)S(1)}, u32[]{:S(2)}, u32[]{:S(2)}) collective-permute-start(bf16[272,512]{1,0:T(8,128)(2,1)S(1)} %collective-permute-done.1.y0), channel_id=1, source_target_pairs={{0,1},{1,0},{2,3},{3,2},{4,5},{5,4},{6,7},{7,6},{8,9},{9,8},{10,11... | collective-permute-start | bytes 835592 | tf_op jit(solution)/shard_map/cond/branch_1_fun/ppermute | solution.py:189
  17.1 1.6 %collective-permute-start.7 = (bf16[256,512]{1,0:T(8,128)(2,1)S(1)}, bf16[256,512]{1,0:T(8,128)(2,1)S(1)}, u32[]{:S(2)}, u32[]{:S(2)}) collective-permute-start(bf16[256,512]{1,0:T(8,128)(2,1)S(1)} %collective-permute-done.3.z0), channel_id=1, source_target_pairs={{0,1},{1,0},{2,3},{3,2},{4,5},{5,4},{6,7},{7,6},{8,9},{9,8},{10,11... | collective-permute-start | bytes 786440 | tf_op jit(solution)/shard_map/ppermute | solution.py:189
  17.3 1.4 %collective-permute-start.6 = (s32[1,2]{1,0:T(1,128)S(1)}, s32[1,2]{1,0:T(1,128)S(1)}, u32[]{:S(2)}, u32[]{:S(2)}) collective-permute-start(s32[1,2]{1,0:T(1,128)S(1)} %collective-permute-done.4.far_len), channel_id=1, source_target_pairs={{0,1},{1,0},{2,3},{3,2},{4,5},{5,4},{6,7},{7,6},{8,9},{9,8},{10,11... | collective-permute-start | bytes 32 | tf_op jit(solution)/shard_map/ppermute | solution.py:189
  18.7 1.5 %collective-permute-start.8 = (bf16[256,512]{1,0:T(8,128)(2,1)S(1)}, bf16[256,512]{1,0:T(8,128)(2,1)S(1)}, u32[]{:S(2)}, u32[]{:S(2)}) collective-permute-start(bf16[256,512]{1,0:T(8,128)(2,1)S(1)} %collective-permute-done.5.r0), channel_id=1, source_target_pairs={{0,1},{1,0},{2,3},{3,2},{4,5},{5,4},{6,7},{7,6},{8,9},{9,8},{10,11... | collective-permute-start | bytes 786440 | tf_op jit(solution)/shard_map/ppermute | solution.py:189
  21.1 4.4 %collective-permute-start.9 = (f32[1,16]{1,0:T(1,128)S(1)}, f32[1,16]{1,0:T(1,128)S(1)}, u32[]{:S(2)}, u32[]{:S(2)}) collective-permute-start(f32[1,16]{1,0:T(1,128)S(1)} %get-tuple-element.37), channel_id=1, source_target_pairs={{0,2},{2,0},{4,6},{6,4},{8,10},{10,8},{12,14},{14,12},{1,3},{3,1},... | collective-permute-start | bytes 200 | tf_op jit(solution)/shard_map/ppermute | solution.py:186
  22.6 4.4 %collective-permute-start.10 = (f32[1,16]{1,0:T(1,128)S(1)}, f32[1,16]{1,0:T(1,128)S(1)}, u32[]{:S(2)}, u32[]{:S(2)}) collective-permute-start(f32[1,16]{1,0:T(1,128)S(1)} %get-tuple-element.38), channel_id=1, source_target_pairs={{8,0},{10,2},{12,4},{14,6},{4,8},{6,10},{0,12},{2,14},{9,1},{11,3}... | collective-permute-start | bytes 200 | tf_op jit(solution)/shard_map/ppermute | solution.py:186
